TPU v7x, 32 devices: a whole 2x2x4 slice. The times are simulated.
32 devices in a mesh: dp: 16 (over z, x, core), seq: 2 (over y).
Axes of the slice: x: 2, y: 2, z: 4, core: 2. Of those that a mesh axis runs over, the one named last changes fastest.
Arguments:
- inputs: bfloat16 [64, 512, 768], P('dp', 'seq'), may hold values from -6 to 6
- cotangent: bfloat16 [64, 512, 768], P('dp', 'seq'), may hold values from -6 to 6
- w_query: bfloat16 [768, 768], replicated, may hold values from -0.21875 to 0.21875
- b_query: bfloat16 [768], replicated, may hold values from -3 to 3
- w_key: bfloat16 [768, 768], replicated, may hold values from -0.21875 to 0.21875
- w_value: bfloat16 [768, 768], replicated, may hold values from -0.21875 to 0.21875
- b_value: bfloat16 [768], replicated, may hold values from -3 to 3
- w_out: bfloat16 [768, 768], replicated, may hold values from -0.875 to 0.875
- b_out: bfloat16 [768], replicated, may hold values from -3 to 3
- gain_one: bfloat16 [768], replicated, may hold values from 0.5 to 1.5
- shift_one: bfloat16 [768], replicated, may hold values from -3 to 3
- w_up: bfloat16 [768, 3072], replicated, may hold values from -0.21875 to 0.21875
- b_up: bfloat16 [3072], replicated, may hold values from -3 to 3
- w_down: bfloat16 [3072, 768], replicated, may hold values from -0.109375 to 0.109375
- b_down: bfloat16 [768], replicated, may hold values from -3 to 3
- gain_two: bfloat16 [768], replicated, may hold values from 0.5 to 1.5
- shift_two: bfloat16 [768], replicated, may hold values from -3 to 3
- live_counts: int32 [16], P('dp'), may hold values from 1 to 4, as said below
- valid_mask: int32 [64, 512], P('dp', 'seq'), may hold values from 0 to 1, as said below
- segments: int32 [64, 512], P('dp', 'seq'), may hold values from 0 to 8, as said below
Outputs:
- result_out: bfloat16 [64, 512, 768], P('dp', 'seq')
- grad_inputs: float32 [64, 512, 768], P('dp', 'seq')
- grad_w_query: float32 [768, 768], replicated
- grad_b_query: float32 [768], replicated
- grad_w_key: float32 [768, 768], replicated
- grad_w_value: float32 [768, 768], replicated
- grad_b_value: float32 [768], replicated
- grad_w_out: float32 [768, 768], replicated
- grad_b_out: float32 [768], replicated
- grad_gain_one: float32 [768], replicated
- grad_shift_one: float32 [768], replicated
- grad_w_up: float32 [768, 3072], replicated
- grad_b_up: float32 [3072], replicated
- grad_w_down: float32 [3072, 768], replicated
- grad_b_down: float32 [768], replicated
- grad_gain_two: float32 [768], replicated
- grad_shift_two: float32 [768], replicated
- rms_values: float32 [4], replicated
Inputs may be any that keep to these rules, and one draw needn't show every extreme that they name: `live_counts`: the live micro-batches of a data group are the first of its 4 sequences; in every draw some data group has all 4 live. `valid_mask`: padding lies only at the end of a sequence; in each data group one live sequence, drawn from the seed, has no padding and a single segment. `segments`: segment numbers never fall along a sequence and start at 0; every sequence other than the single-segment ones reaches the largest number.
All inputs are finite; a program needn't handle non-finite values.
Results may differ from a plain program's by a relative error of at most 0.019.
Values may be sent and summed in bfloat16 or wider, within the bound.
No kernel may reach another device: no remote copies, remote signals or barrier semaphores. Data moves between devices by JAX's collectives and lax.ppermute only.
A program may use at most 256 MiB of HBM per device.

v0:
```python
import jax
import jax.numpy as jnp
from jax import lax
from jax.sharding import PartitionSpec as P

HEADS = 12
HEAD_DIM = 64


EPSILON = 1e-05
NEGATIVE = -1e30
SCORE_SCALE = 0.125


def from_behind(value, axis, steps):
    count = lax.axis_size(axis)
    pairs = [(source, (source + steps) % count) for source in range(count)]
    return lax.ppermute(value, axis, pairs)


def layer_norm(values, scale_gain, shift_bias):
    center = values - jnp.mean(values, axis=-1, keepdims=True)
    spread = jnp.mean(center * center, axis=-1, keepdims=True)
    return center * lax.rsqrt(spread + EPSILON) * scale_gain + shift_bias


def gelu_exact(values):
    return jax.nn.gelu(values, approximate=False)


def matmul(left, right):
    return jnp.dot(left, right, preferred_element_type=jnp.float32)


def outer_sum(left, right):
    return lax.dot_general(
        left, right, (((0,), (0,)), ((), ())), preferred_element_type=jnp.float32
    )


def back_mul(grads_in, weight):
    return lax.dot_general(
        grads_in, weight, (((1,), (1,)), ((), ())), preferred_element_type=jnp.float32
    )


def pack_flat(pieces, count):
    flat = jnp.concatenate([piece.reshape(-1) for piece in pieces])
    extra = -flat.shape[0] % count
    flat = jnp.concatenate([flat, jnp.zeros((extra,), jnp.float32)])
    return flat.reshape(count, -1)


def unpack_flat(tiled, pieces):
    flat = tiled.reshape(-1)
    outcome = []
    offset = 0
    for piece in pieces:
        number = piece.size
        outcome.append(flat[offset : offset + number].reshape(piece.shape))
        offset = offset + number
    return outcome


def visible_mask(query_marks, query_place, mark_rows, key_place):
    same_doc = query_marks[:, :, None] == mark_rows[:, None, :]
    itself = query_place[:, None] == key_place[None, :]
    return (same_doc | itself[None])[:, None]


def fold_block(running, queries, key_part, value_part, allowed):
    row_top, row_total, summed = running
    scores = jnp.einsum("sqhd,skhd->shqk", queries, key_part, preferred_element_type=jnp.float32)
    scores = jnp.where(allowed, scores, NEGATIVE)
    new_top = jnp.maximum(row_top, jnp.max(scores, axis=-1))
    factor = jnp.exp(row_top - new_top)
    weights_exp = jnp.where(allowed, jnp.exp(scores - new_top[..., None]), 0.0)
    row_total = row_total * factor + jnp.sum(weights_exp, axis=-1)
    summed = summed * factor[..., None] + jnp.einsum(
        "shqk,skhd->shqd",
        weights_exp.astype(jnp.bfloat16),
        value_part,
        preferred_element_type=jnp.float32,
    )
    return (new_top, row_total, summed)


def grad_block(queries, grad_context, log_total, delta_row, key_part, value_part, allowed):
    scores = jnp.einsum("sqhd,skhd->shqk", queries, key_part, preferred_element_type=jnp.float32)
    chances = jnp.where(allowed, jnp.exp(scores - log_total[..., None]), 0.0)
    grad_values = jnp.einsum(
        "shqk,sqhd->skhd",
        chances.astype(jnp.bfloat16),
        grad_context,
        preferred_element_type=jnp.float32,
    )
    grad_chances = jnp.einsum(
        "sqhd,skhd->shqk", grad_context, value_part, preferred_element_type=jnp.float32
    )
    grad_scores = (chances * (grad_chances - delta_row[..., None])).astype(jnp.bfloat16)
    grad_queries = jnp.einsum(
        "shqk,skhd->sqhd", grad_scores, key_part, preferred_element_type=jnp.float32
    )
    grad_keys = jnp.einsum(
        "shqk,sqhd->skhd", grad_scores, queries, preferred_element_type=jnp.float32
    )
    return (grad_queries, grad_keys, grad_values)


def on_device(
    inputs,
    cotangent,
    w_query,
    b_query,
    w_key,
    w_value,
    b_value,
    w_out,
    b_out,
    gain_one,
    shift_one,
    w_up,
    b_up,
    w_down,
    b_down,
    gain_two,
    shift_two,
    live_counts,
    valid_mask,
    segments,
):
    place_index = lax.axis_index("seq")
    seq_devices = lax.axis_size("seq")
    all_devices = lax.axis_size(("dp", "seq"))
    piece_len = inputs.shape[1]
    live_rows = (jnp.arange(inputs.shape[0]) < live_counts[0]).astype(jnp.float32)
    token_weight = valid_mask.astype(jnp.float32) * live_rows[:, None]
    own_marks = jnp.where(token_weight > 0, segments, -1)
    all_marks = lax.all_gather(own_marks, "seq", axis=1, tiled=True)
    query_place = place_index * piece_len + jnp.arange(piece_len)
    seq_count, span_len, model_width = inputs.shape
    row_count = seq_count * span_len
    token_rows = inputs.reshape(row_count, model_width)

    def block_mask(start, length):
        mark_rows = lax.dynamic_slice_in_dim(all_marks, start, length, 1)
        return visible_mask(segments, query_place, mark_rows, start + jnp.arange(length))

    def headwise(flat):
        return flat.reshape(seq_count, span_len, HEADS, HEAD_DIM)

    queries = headwise(
        ((matmul(token_rows, w_query) + b_query.astype(jnp.float32)) * SCORE_SCALE).astype(
            jnp.bfloat16
        )
    )
    keys_own = headwise(matmul(token_rows, w_key).astype(jnp.bfloat16))
    values_own = headwise(
        (matmul(token_rows, w_value) + b_value.astype(jnp.float32)).astype(jnp.bfloat16)
    )
    own_pair = jnp.stack((keys_own, values_own))
    stat_shape = (seq_count, HEADS, span_len)
    running = (
        jnp.full(stat_shape, NEGATIVE, jnp.float32),
        jnp.zeros(stat_shape, jnp.float32),
        jnp.zeros(stat_shape + (HEAD_DIM,), jnp.float32),
    )

    def forward_turn(step_idx, carried):
        running, moving = carried
        source = (place_index - step_idx) % seq_devices
        running = fold_block(
            running, queries, moving[0], moving[1], block_mask(source * span_len, span_len)
        )
        moving = from_behind(moving, "seq", 1)
        return (running, moving)

    running, moving = lax.fori_loop(0, seq_devices - 1, forward_turn, (running, own_pair))
    source = (place_index - (seq_devices - 1)) % seq_devices
    row_top, row_total, summed = fold_block(
        running, queries, moving[0], moving[1], block_mask(source * span_len, span_len)
    )
    context_heads = summed / row_total[..., None]
    log_total = row_top + jnp.log(row_total)
    context_rows = jnp.transpose(context_heads, (0, 2, 1, 3)).reshape(row_count, model_width)
    context = context_rows.astype(jnp.bfloat16)
    attention = matmul(context, w_out) + b_out.astype(jnp.float32)
    rows_float = token_rows.astype(jnp.float32)
    middle, norm_pull_one = jax.vjp(
        layer_norm,
        rows_float + attention,
        gain_one.astype(jnp.float32),
        shift_one.astype(jnp.float32),
    )
    middle_low = middle.astype(jnp.bfloat16)
    hidden = matmul(middle_low, w_up) + b_up.astype(jnp.float32)
    activated_f, gelu_pull = jax.vjp(gelu_exact, hidden)
    activated = activated_f.astype(jnp.bfloat16)
    feed_out = matmul(activated, w_down) + b_down.astype(jnp.float32)
    result, norm_pull_two = jax.vjp(
        layer_norm, middle + feed_out, gain_two.astype(jnp.float32), shift_two.astype(jnp.float32)
    )
    weight_rows = token_weight.reshape(-1)
    sums = [
        jnp.sum(weight_rows * jnp.sum(entry * entry, axis=-1))
        for entry in (rows_float, attention, feed_out, result)
    ]
    local_totals = jnp.stack(
        sums + [jnp.sum(weight_rows), jnp.float32(0.0), jnp.float32(0.0), jnp.float32(0.0)]
    )
    grad_result = (
        cotangent.astype(jnp.float32).reshape(row_count, model_width) * weight_rows[:, None]
    )
    grad_h_two, grad_gain_two, grad_shift_two = norm_pull_two(grad_result)
    grad_feed = grad_h_two.astype(jnp.bfloat16)
    grad_w_down = outer_sum(activated, grad_feed)
    grad_b_down = jnp.sum(grad_feed.astype(jnp.float32), axis=0)
    grad_hidden = gelu_pull(back_mul(grad_feed, w_down))[0].astype(jnp.bfloat16)
    grad_w_up = outer_sum(middle_low, grad_hidden)
    grad_b_up = jnp.sum(grad_hidden.astype(jnp.float32), axis=0)
    grad_middle = grad_h_two + back_mul(grad_hidden, w_up)
    grad_h_one, grad_gain_one, grad_shift_one = norm_pull_one(grad_middle)
    grad_attention = grad_h_one.astype(jnp.bfloat16)
    grad_w_out = outer_sum(context, grad_attention)
    grad_b_out = jnp.sum(grad_attention.astype(jnp.float32), axis=0)
    grad_context = headwise(back_mul(grad_attention, w_out).astype(jnp.bfloat16))
    delta_row = jnp.sum(
        grad_context.astype(jnp.float32) * jnp.transpose(context_heads, (0, 2, 1, 3)), axis=-1
    )
    delta_row = jnp.transpose(delta_row, (0, 2, 1))

    def pass_back(owed_grads):
        return from_behind(owed_grads.astype(jnp.bfloat16), "seq", 1).astype(owed_grads.dtype)

    def backward_turn(step_idx, carried):
        grad_queries, moving, owed_grads = carried
        source = (place_index - step_idx) % seq_devices
        part_query, part_key, part_value = grad_block(
            queries,
            grad_context,
            log_total,
            delta_row,
            moving[0],
            moving[1],
            block_mask(source * span_len, span_len),
        )
        owed_grads = pass_back(owed_grads + jnp.stack((part_key, part_value)))
        moving = from_behind(moving, "seq", 1)
        return (grad_queries + part_query, moving, owed_grads)

    start_grads = jnp.zeros((2, seq_count, span_len, HEADS, HEAD_DIM), jnp.float32)
    start_query = jnp.zeros((seq_count, span_len, HEADS, HEAD_DIM), jnp.float32)
    grad_queries, moving, owed_grads = lax.fori_loop(
        0, seq_devices - 1, backward_turn, (start_query, own_pair, start_grads)
    )
    source = (place_index - (seq_devices - 1)) % seq_devices
    part_query, part_key, part_value = grad_block(
        queries,
        grad_context,
        log_total,
        delta_row,
        moving[0],
        moving[1],
        block_mask(source * span_len, span_len),
    )
    grad_queries = grad_queries + part_query
    owed_grads = pass_back(owed_grads + jnp.stack((part_key, part_value)))
    query_low = grad_queries.astype(jnp.bfloat16).reshape(row_count, model_width)
    key_low = owed_grads[0].astype(jnp.bfloat16).reshape(row_count, model_width)
    value_low = owed_grads[1].astype(jnp.bfloat16).reshape(row_count, model_width)
    grad_w_query = outer_sum(token_rows, query_low) * SCORE_SCALE
    grad_b_query = jnp.sum(query_low.astype(jnp.float32), axis=0) * SCORE_SCALE
    grad_w_key = outer_sum(token_rows, key_low)
    grad_w_value = outer_sum(token_rows, value_low)
    grad_b_value = jnp.sum(value_low.astype(jnp.float32), axis=0)
    grad_rows = (
        grad_h_one
        + back_mul(query_low, w_query) * SCORE_SCALE
        + back_mul(key_low, w_key)
        + back_mul(value_low, w_value)
    )
    all_pieces = (
        grad_w_query,
        grad_b_query,
        grad_w_key,
        grad_w_value,
        grad_b_value,
        grad_w_out,
        grad_b_out,
        grad_gain_one,
        grad_shift_one,
        grad_w_up,
        grad_b_up,
        grad_w_down,
        grad_b_down,
        grad_gain_two,
        grad_shift_two,
        local_totals,
    )
    summed_part = lax.psum_scatter(
        pack_flat(all_pieces, all_devices), ("dp", "seq"), scatter_dimension=0, tiled=True
    )
    summed_whole = lax.all_gather(
        summed_part.astype(jnp.bfloat16), ("dp", "seq"), axis=0, tiled=True
    ).astype(summed_part.dtype)
    (
        grad_w_query,
        grad_b_query,
        grad_w_key,
        grad_w_value,
        grad_b_value,
        grad_w_out,
        grad_b_out,
        grad_gain_one,
        grad_shift_one,
        grad_w_up,
        grad_b_up,
        grad_w_down,
        grad_b_down,
        grad_gain_two,
        grad_shift_two,
        all_totals,
    ) = unpack_flat(summed_whole, all_pieces)
    rms_values = jnp.sqrt(all_totals[:4] / (model_width * all_totals[4]))
    result_out = result.astype(jnp.bfloat16).reshape(seq_count, span_len, model_width)
    grad_inputs = grad_rows.reshape(seq_count, span_len, model_width)
    return (
        result_out,
        grad_inputs,
        grad_w_query,
        grad_b_query,
        grad_w_key,
        grad_w_value,
        grad_b_value,
        grad_w_out,
        grad_b_out,
        grad_gain_one,
        grad_shift_one,
        grad_w_up,
        grad_b_up,
        grad_w_down,
        grad_b_down,
        grad_gain_two,
        grad_shift_two,
        rms_values,
    )


def solution(mesh):
    return jax.shard_map(
        on_device,
        mesh=mesh,
        in_specs=(
            P("dp", "seq", None),
            P("dp", "seq", None),
            P(),
            P(),
            P(),
            P(),
            P(),
            P(),
            P(),
            P(),
            P(),
            P(),
            P(),
            P(),
            P(),
            P(),
            P(),
            P("dp"),
            P("dp", "seq"),
            P("dp", "seq"),
        ),
        out_specs=(
            P("dp", "seq", None),
            P("dp", "seq", None),
            P(),
            P(),
            P(),
            P(),
            P(),
            P(),
            P(),
            P(),
            P(),
            P(),
            P(),
            P(),
            P(),
            P(),
            P(),
            P(),
        ),
        check_vma=False,
    )
```

profile of v0, /device:TPU:0, one launch (start us, length us, event | category | flops | bytes accessed | tf_op | source)
XLA Modules:
  0.0 1746.6 jit_solution(4626977209176422132)
XLA Ops:
  8.0 4.3 add_convert_fusion.2
  24.5 3.9 stack_reshape.6
  37.6 4.0 squeeze.27
  44.8 3.8 multiply_convert_fusion.3
  54.1 49.5 %all_gather.6 = s32[4,512]{1,0:T(4,128)S(1)} all-gather(s32[4,256]{1,0:T(4,128)S(1)} %get-tuple-element.117), channel_id=1, replica_groups=mesh['dp'=16,'seq'=2] {'seq'}, dimensions={1}, use_global_device_ids=true | all-gather | bytes 12288 | tf_op jit(solution)/shard_map/all_gather | solution.py:139
  109.6 5.7 select_reduce_fusion.1
  115.3 3.4 select_reduce_fusion
  119.4 3.2 fusion.10
  122.6 7.8 fusion.8
  131.1 6.0 fusion.14
  137.1 6.4 fusion.95
  149.1 35.2 %multiply_convert_fusion.2 = (bf16[1024,3072]{1,0:T(8,128)(2,1)S(1)}, f32[1024,3072]{1,0:T(8,128)}, f32[1024,3072]{1,0:T(8,128)}) fusion(f32[3072]{0:T(1024)S(1)} %copy-done.52, bf16[768,3072]{1,0:T(8,128)(2,1)S(1)} %bitcast.204, f32[1024,768]{1,0:T(8,128)S(1)} %get-tuple-element.116, f32[768]{0:T(1024)S(1)} %convert_element_type.176, ...), kind=kOutput, calls=%fused_computation.9 | convolution fusion | flops 5043388416 | bytes 39348224 | tf_op jit(solution)/shard_map/dot_general | solution.py:32
  184.4 5.6 fusion.89
  191.4 3.5 multiply_reduce_fusion.5
  198.6 17.8 %convert_reduce_fusion.1 = (f32[3072]{0:T(1024)}, bf16[1024,3072]{1,0:T(8,128)(2,1)}) fusion(f32[1024,3072]{1,0:T(8,128)} %get-tuple-element.114, bf16[1024,768]{1,0:T(8,128)(2,1)S(1)} %get-tuple-element.102, bf16[3072,768]{1,0:T(8,128)(2,1)} %param.33, f32[1024,3072]{1,0:T(8,128)} %get-tuple-element.153, f32[3072]{0:T(1024)S(1)} %copy-done.52), kind=kOutput, calls=%fused_computation.3 | convolution fusion | flops 4885312512 | bytes 37773312 | tf_op jit(solution)/shard_map/dot_general | solution.py:42
  216.5 11.0 multiply_reduce_fusion.6
  227.5 8.5 convolution_bitcast_fusion
  246.6 3.0 multiply_reduce_fusion.7
  249.7 7.9 fusion.50
  257.6 7.8 multiply_convert_fusion.1
  274.5 9.6 copy.149
  284.1 3.4 reshape.329
  287.6 9.1 multiply_convert_fusion
  296.7 3.7 convolution_bitcast_fusion.1
  300.4 5.7 fusion.56
  306.2 3.4 fusion.40
  309.6 30.0 %collective-permute-done.1 = bf16[2,4,256,12,64]{2,4,3,1,0:T(8,128)(2,1)} collective-permute-done((bf16[2,4,256,12,64]{2,4,3,1,0:T(8,128)(2,1)}, bf16[2,4,256,12,64]{2,4,3,1,0:T(8,128)(2,1)}, u32[]{:S(2)}, u32[]{:S(2)}) %collective-permute-start.1) | collective-permute-done | bytes 3145760 | tf_op jit(solution)/shard_map/while/body/eval_jaxpr/ppermute | solution.py:18
  339.5 6.6 fusion.20
  359.9 9.9 fusion.99
  369.8 10.8 reshape.331
  381.2 33.7 %collective-permute-done.2 = bf16[2,4,256,12,64]{2,4,3,1,0:T(8,128)(2,1)} collective-permute-done((bf16[2,4,256,12,64]{2,4,3,1,0:T(8,128)(2,1)}, bf16[2,4,256,12,64]{2,4,3,1,0:T(8,128)(2,1)}, u32[]{:S(2)}, u32[]{:S(2)}) %collective-permute-start.2) | collective-permute-done | bytes 3145760 | tf_op jit(solution)/shard_map/ppermute | solution.py:18
  430.0 3.3 convolution_bitcast_fusion.3
  435.2 3.4 reshape.327
  438.7 233.9 %concatenate.3 = f32[7087136]{0:T(1024)} concatenate(f32[589824]{0:T(1024)} %reshape.326, f32[768]{0:T(1024)S(1)} %mul.346, f32[589824]{0:T(1024)} %reshape.327, f32[589824]{0:T(1024)} %reshape.328, f32[768]{0:T(1024)S(1)} %reduce_sum.321, f32[589824]{0:T(1024)S(1)} %copy-done.15, f32[768]{0:T(1024)S(1)} %get-tuple-element.103, f32[768]{0:T(1024)S(1)} %get-tuple-element.77, ...), dimensions={0} | concatenate | bytes 56697088 | tf_op jit(solution)/shard_map/concatenate | solution.py:50
  672.6 37.0 %reshape.332 = f32[32,221473]{1,0:T(8,128)} reshape(f32[7087136]{0:T(1024)} %concatenate.3) | data formatting | bytes 56697088 | tf_op jit(solution)/shard_map/reshape | solution.py:51
  709.6 455.3 %all-reduce.2 = bf16[32,221473]{1,0:T(8,128)(2,1)} all-reduce(f32[32,221473]{1,0:T(8,128)} %reshape.332), channel_id=2, replica_groups=mesh['dp'=16,'seq'=2] {'dp','seq'}, use_global_device_ids=true, to_apply=%region_31.32.clone | all-reduce | flops 7087136 | bytes 42522816
  1164.9 3.4 fusion.64
  1172.8 3.6 add_add_fusion.2
  1176.5 160.9 %all-gather.3.cloned.1.call-done = bf16[32,1,221473]{2,1,0:T(2,128)(2,1)} async-done(((bf16[1,1,221473]{2,1,0:T(2,128)(2,1)}), bf16[32,1,221473]{2,1,0:T(2,128)(2,1)}) %all-gather.3.cloned.1.call-update) | async-done | bytes 14174288 | tf_op jit(solution)/shard_map/all_gather | solution.py:303
  1337.4 303.5 %convert_reduce_fusion = f32[32,221473]{1,0:T(8,128)} fusion(bf16[32,1,221473]{2,1,0:T(2,128)(2,1)} %all-gather.3.cloned.1.call-done), kind=kLoop, calls=%fused_computation | loop fusion | flops 7087136 | bytes 42522816 | tf_op jit(solution)/shard_map/reshape | solution.py:55
  1640.8 38.0 %reshape.342 = f32[7087136]{0:T(1024)} reshape(f32[32,221473]{1,0:T(8,128)} %convert_reduce_fusion) | data formatting | bytes 56697088 | tf_op jit(solution)/shard_map/reshape | solution.py:55
  1682.8 6.9 fusion.94
  1689.7 14.1 fusion.93
  1705.6 11.3 reshape.340
  1716.9 3.4 reshape.338
  1720.2 3.4 reshape.337
  1723.6 3.4 reshape.336
  1728.6 11.0 reshape.339
  (250 shorter events, 110.3 us)
Async XLA Ops:
  7.2 138.0 %copy-start = (bf16[768,768]{1,0:T(8,128)(2,1)S(1)}, bf16[768,768]{1,0:T(8,128)(2,1)}, u32[]{:S(2)}) copy-start(bf16[768,768]{1,0:T(8,128)(2,1)} %param.27) | copy-start | bytes 3538948
  7.2 1330.2 %all-gather.3.cloned.1.call-start = ((), (), s32[]{:S(2)}) async-start(), calls=%async_computation | async-start | bytes 29246976 | tf_op jit(solution)/shard_map/all_gather | solution.py:303
  32.2 83.1 %collective-permute-start = (bf16[2,4,256,12,64]{2,4,3,1,0:T(8,128)(2,1)}, bf16[2,4,256,12,64]{2,4,3,1,0:T(8,128)(2,1)}, u32[]{:S(2)}, u32[]{:S(2)}) collective-permute-start(bf16[2,4,256,12,64]{2,4,3,1,0:T(8,128)(2,1)} %pad_maximum_fusion), channel_id=1, source_target_pairs={{0,1},{1,0},{2,3},{3,2},{4,5},{5,4},{6,7},{7,6},{8,9},{9,8},{10,11... | collective-permute-start | bytes 9437192 | tf_op jit(solution)/shard_map/while/body/eval_jaxpr/ppermute | solution.py:18
  35.1 7.1 copy-start.59
  35.1 7.1 copy-start.60
  35.1 7.1 copy-start.61
  35.1 7.1 copy-start.62
  35.2 7.2 copy-start.63
  35.2 7.7 copy-start.64
  35.2 8.3 copy-start.65
  35.2 8.9 copy-start.49
  35.2 8.9 copy-start.58
  35.2 9.0 copy-start.53
  37.6 7.2 copy-start.26
  44.2 61.8 %copy-start.42 = (f32[4,256]{1,0:T(4,128)}, f32[4,256]{1,0:T(4,128)S(1)}, u32[]{:S(2)}) copy-start(f32[4,256]{1,0:T(4,128)S(1)} %get-tuple-element.118) | copy-start | bytes 12292
  54.1 61.2 %copy-start.3 = (bf16[4,256,12,64]{1,0,3,2:T(4,128)(2,1)}, bf16[4,256,12,64]{1,0,3,2:T(4,128)(2,1)S(1)}, u32[]{:S(2)}) copy-start(bf16[4,256,12,64]{1,0,3,2:T(4,128)(2,1)S(1)} %reshape.320) | copy-start | bytes 4718596
  54.1 55.5 %copy-start.11 = (bf16[4,256,12,64]{1,0,3,2:T(4,128)(2,1)S(1)}, bf16[4,256,12,64]{1,0,3,2:T(4,128)(2,1)}, u32[]{:S(2)}) copy-start(bf16[4,256,12,64]{1,0,3,2:T(4,128)(2,1)} %squeeze.27) | copy-start | bytes 4718596
  109.6 21.5 %copy-start.23 = (pred[4,256,256]{1,2,0:T(8,128)(4,1)}, pred[4,256,256]{1,2,0:T(8,128)(4,1)S(1)}, u32[]{:S(2)}) copy-start(pred[4,256,256]{1,2,0:T(8,128)(4,1)S(1)} %get-tuple-element.144) | copy-start | bytes 786436
  109.6 27.5 %copy-start.21 = (pred[4,256,256]{1,2,0:T(8,128)(4,1)}, pred[4,256,256]{1,2,0:T(8,128)(4,1)S(1)}, u32[]{:S(2)}) copy-start(pred[4,256,256]{1,2,0:T(8,128)(4,1)S(1)} %get-tuple-element.143) | copy-start | bytes 786436
  118.7 18.4 %copy-start.2 = (f32[4,12,256,256]{2,3,1,0:T(8,128)}, f32[4,12,256,256]{2,3,1,0:T(8,128)S(1)}, u32[]{:S(2)}) copy-start(f32[4,12,256,256]{2,3,1,0:T(8,128)S(1)} %get-tuple-element.148) | copy-start | bytes 37748740
  122.6 8.5 copy-start.30
  145.2 39.1 %slice-start.3 = ((s8[4718592]{0:T(1024)(128)(4,1)}), s8[4194304]{0:T(1024)(128)(4,1)S(1)}, s32[]{:S(2)}) async-start(s8[4718592]{0:T(1024)(128)(4,1)} %bitcast.201), calls=%async_computation.4 | async-start | bytes 8388608
  148.4 35.9 %copy-start.44 = (f32[1024]{0:T(1024)}, f32[1024]{0:T(1024)S(1)}, u32[]{:S(2)}) copy-start(f32[1024]{0:T(1024)S(1)} %multiply_reduce_fusion.11) | copy-start | bytes 12292
  149.1 35.3 %copy-start.55 = (f32[768]{0:T(1024)S(1)}, f32[768]{0:T(1024)}, u32[]{:S(2)}) copy-start(f32[768]{0:T(1024)} %convert_element_type.180) | copy-start | bytes 9220
  149.1 35.3 %slice-start.4 = ((s8[4718592]{0:T(1024)(128)(4,1)}), s8[524288]{0:T(1024)(128)(4,1)S(1)}, s32[]{:S(2)}) async-start(s8[4718592]{0:T(1024)(128)(4,1)} %bitcast.201), calls=%async_computation.5 | async-start | bytes 1048576
  184.3 5.7 copy-start.69
  198.6 17.9 %copy-start.37 = (bf16[1024,768]{1,0:T(8,128)(2,1)}, bf16[1024,768]{1,0:T(8,128)(2,1)S(1)}, u32[]{:S(2)}) copy-start(bf16[1024,768]{1,0:T(8,128)(2,1)S(1)} %get-tuple-element.102) | copy-start | bytes 4718596
  216.5 11.0 copy-start.16
  227.5 8.5 copy-start.45
  246.6 11.0 copy-start.8
  249.7 8.0 copy-start.31
  257.6 7.8 copy-start.4
  268.1 3.6 copy-start.33
  268.1 3.6 copy-start.39
  270.0 4.5 copy-start.57
  270.0 69.6 %collective-permute-start.1 = (bf16[2,4,256,12,64]{2,4,3,1,0:T(8,128)(2,1)}, bf16[2,4,256,12,64]{2,4,3,1,0:T(8,128)(2,1)}, u32[]{:S(2)}, u32[]{:S(2)}) collective-permute-start(bf16[2,4,256,12,64]{2,4,3,1,0:T(8,128)(2,1)} %pad_maximum_fusion.1), channel_id=1, source_target_pairs={{0,1},{1,0},{2,3},{3,2},{4,5},{5,4},{6,7},{7,6},{8,9},{9,8},{10,11... | collective-permute-start | bytes 9437192 | tf_op jit(solution)/shard_map/while/body/eval_jaxpr/ppermute | solution.py:18
  296.7 3.7 copy-start.12
  296.7 9.4 slice-start
  296.7 9.4 slice-start.1
  300.4 5.7 slice-start.2
  300.4 5.7 copy-start.9
  309.6 38.0 %copy-start.14 = (f32[4,12,64,256]{3,2,1,0:T(8,128)S(1)}, f32[4,12,64,256]{3,2,1,0:T(8,128)}, u32[]{:S(2)}) copy-start(f32[4,12,64,256]{3,2,1,0:T(8,128)} %fusion.56) | copy-start | bytes 9437188
  346.2 68.7 %collective-permute-start.2 = (bf16[2,4,256,12,64]{2,4,3,1,0:T(8,128)(2,1)}, bf16[2,4,256,12,64]{2,4,3,1,0:T(8,128)(2,1)}, u32[]{:S(2)}, u32[]{:S(2)}) collective-permute-start(bf16[2,4,256,12,64]{2,4,3,1,0:T(8,128)(2,1)} %fusion.20), channel_id=1, source_target_pairs={{0,1},{1,0},{2,3},{3,2},{4,5},{5,4},{6,7},{7,6},{8,9},{9,8},{10,11... | collective-permute-start | bytes 9437192 | tf_op jit(solution)/shard_map/ppermute | solution.py:18
  369.8 10.8 copy-start.43
  369.8 10.8 copy-start.50
  709.6 458.8 %copy-start.36 = (bf16[96,8,4,256]{3,1,2,0:T(8,128)(2,1)S(1)}, bf16[96,8,4,256]{3,1,2,0:T(8,128)(2,1)}, u32[]{:S(2)}) copy-start(bf16[96,8,4,256]{3,1,2,0:T(8,128)(2,1)} %copy-done.35) | copy-start | bytes 4718596
  709.6 458.8 %copy-start.66 = (bf16[768,768]{1,0:T(8,128)(2,1)S(1)}, bf16[768,768]{1,0:T(8,128)(2,1)}, u32[]{:S(2)}) copy-start(bf16[768,768]{1,0:T(8,128)(2,1)} %param.25) | copy-start | bytes 3538948
  1728.6 11.0 copy-start.1
  (33 other events, 78.7 us)
Sparse Core Ops, SparseCore 0:
  1168.5 168.8 all-gather.2
where the time goes:
time: 1770 us; the launch traced here: 1750 us
  blocking collectives  505 us (29%)
  local copies, waits for them, and re-layouts  459 us (26%)
  other arithmetic  350 us (20%)
  waiting for transfers between devices  225 us (13%)
  matrix products  185 us (10%)
    unnamed x1, blocking collectives  455 us
    reshape x1, other arithmetic, unpack_flat(): flat = tiled.reshape(-1)  303 us
    concatenate x1, local copies, waits for them, and re-layouts, pack_flat(): flat = jnp.concatenate([flat, jnp.zeros((extra,), jnp.float32)])  234 us
    all_gather x1, waiting for transfers between devices, on_device(): lax.all_gather(summed_part.astype(jnp.bfloat16), ('dp', 'seq'), axis=0, t...  161 us
    ppermute x3, waiting for transfers between devices, from_behind(): return lax.ppermute(value, axis, pairs)  63.6 us
    dot_general x6, matrix products, matmul(): return jnp.dot(left, right, preferred_element_type=jnp.float32)  54.1 us
    all_gather x1, blocking collectives, on_device(): all_marks = lax.all_gather(own_marks, 'seq', axis=1, tiled=True)  49.5 us
    reshape x1, local copies, waits for them, and re-layouts, unpack_flat(): flat = tiled.reshape(-1)  38 us
  transfers between devices with their start and end apart: 4, of which 3 were waited for; matrix products, arithmetic and copies ran while one was open for 6% of the time, Pallas kernels for 0%

commit v1 on v0

v1 whole, which is shorter than its diff:
```python
import functools

import jax
import jax.numpy as jnp
from jax import lax
from jax.experimental import pallas as pl
from jax.experimental.pallas import tpu as pltpu
from jax.sharding import PartitionSpec as P

HEAD_DIM = 64
EPSILON = 1e-05
NEGATIVE = -1e30
SCORE_SCALE = 0.125
LOW = jnp.bfloat16
WIDE = jnp.float32
VMEM_LIMIT = 56 * 1024 * 1024
HIDDEN_STEP = 512

ERF_P = 0.3275911
ERF_C = (0.254829592, -0.284496736, 1.421413741, -1.453152027, 1.061405429)
ROOT_HALF = 0.7071067811865476
DENSITY = 0.3989422804014327


def nn(left, right):
    return jnp.dot(left, right, preferred_element_type=WIDE)


def nt(left, right):
    return lax.dot_general(
        left, right, (((1,), (1,)), ((), ())), preferred_element_type=WIDE
    )


def tn(left, right):
    return lax.dot_general(
        left, right, (((0,), (0,)), ((), ())), preferred_element_type=WIDE
    )


def gelu_pair(hidden):
    tail_exp = jnp.exp(hidden * hidden * -0.5)
    t = 1.0 / (1.0 + (ERF_P * ROOT_HALF) * jnp.abs(hidden))
    c1, c2, c3, c4, c5 = (0.5 * c for c in ERF_C)
    tail = ((((c5 * t + c4) * t + c3) * t + c2) * t + c1) * t * tail_exp
    below = jnp.where(hidden >= 0.0, 1.0 - tail, tail)
    return hidden * below, below + hidden * (DENSITY * tail_exp)


def lane_half(half):
    lane = lax.broadcasted_iota(jnp.int32, (1, 2 * HEAD_DIM), 1)
    inside = (lane < HEAD_DIM) if half == 0 else (lane >= HEAD_DIM)
    return inside.astype(WIDE).astype(LOW)


def fill_bias(bias_ref, seg_row, mark_col):
    length = bias_ref.shape[0]
    key_place = lax.broadcasted_iota(jnp.int32, (length, length), 0)
    query_place = lax.broadcasted_iota(jnp.int32, (length, length), 1)
    visible = (mark_col == seg_row) | (key_place == query_place)
    bias_ref[...] = jnp.where(visible, 0.0, NEGATIVE)


def total(rows_weight, values):
    per_row = jnp.sum(values * values, axis=1, keepdims=True) * rows_weight
    return jnp.sum(per_row, axis=0, keepdims=True)


def attend_kernel(
    x_ref, seg_ref, mark_ref, wq_ref, bq_ref, wk_ref, wv_ref, bv_ref, wo_ref, bo_ref, gain_ref,
    shift_ref, q_ref, k_ref, v_ref, ctx_ref, lse_ref, mid_ref, norm_ref, rstd_ref, stat_ref,
    bias_ref,
):
    x = x_ref[...]
    q_ref[...] = ((nn(x, wq_ref[...]) + bq_ref[...]) * SCORE_SCALE).astype(LOW)
    k_ref[...] = nn(x, wk_ref[...]).astype(LOW)
    v_ref[...] = (nn(x, wv_ref[...]) + bv_ref[...]).astype(LOW)
    fill_bias(bias_ref, seg_ref[...], mark_ref[...])
    width = 2 * HEAD_DIM
    pairs = x.shape[1] // width

    def pair_step(pair, carried):
        lanes = pl.ds(pl.multiple_of(pair * width, width), width)
        q, k, v = q_ref[:, lanes], k_ref[:, lanes], v_ref[:, lanes]
        v_turned = v.T
        outs = []
        for half in range(2):
            scores = nt(k * lane_half(half), q) + bias_ref[...]
            top = jnp.max(scores, axis=0, keepdims=True)
            weights = jnp.exp(scores - top)
            amount = jnp.sum(weights, axis=0, keepdims=True)
            summed = nn(v_turned[half * HEAD_DIM : (half + 1) * HEAD_DIM], weights.astype(LOW))
            outs.append(summed * (1.0 / amount))
            lse_ref[pl.ds(pair * 2 + half, 1), :] = top + jnp.log(amount)
        ctx_ref[:, lanes] = jnp.concatenate(outs, axis=0).T.astype(LOW)
        return carried

    lax.fori_loop(0, pairs, pair_step, 0)
    attention = nn(ctx_ref[...], wo_ref[...]) + bo_ref[...]
    rows = x.astype(WIDE)
    total_in = rows + attention
    center = total_in - jnp.mean(total_in, axis=1, keepdims=True)
    rstd = lax.rsqrt(jnp.mean(center * center, axis=1, keepdims=True) + EPSILON)
    normal = center * rstd
    mid_ref[...] = normal * gain_ref[...] + shift_ref[...]
    norm_ref[...] = normal.astype(LOW)
    rstd_ref[...] = rstd
    row_weight = (mark_ref[...] >= 0).astype(WIDE)
    stat_ref[...] = jnp.concatenate(
        [
            jnp.broadcast_to(total(row_weight, rows), (1, 128)),
            jnp.broadcast_to(total(row_weight, attention), (1, 128)),
            jnp.zeros((6, 128), WIDE),
        ],
        axis=0,
    )


def whole(shape):
    return pl.BlockSpec(shape, lambda *_: (0,) * len(shape), pipeline_mode=pl.Buffered(1))


def attend(x, seg_row, mark_col, wq, bq, wk, wv, bv, wo, bo, gain, shift):
    length, width = x.shape
    heads = width // HEAD_DIM
    lse_rows = heads + (-heads) % 8
    shapes = (
        jax.ShapeDtypeStruct((length, width), LOW),
        jax.ShapeDtypeStruct((length, width), LOW),
        jax.ShapeDtypeStruct((length, width), LOW),
        jax.ShapeDtypeStruct((length, width), LOW),
        jax.ShapeDtypeStruct((lse_rows, length), WIDE),
        jax.ShapeDtypeStruct((length, width), WIDE),
        jax.ShapeDtypeStruct((length, width), LOW),
        jax.ShapeDtypeStruct((length, 1), WIDE),
        jax.ShapeDtypeStruct((8, 128), WIDE),
    )
    args = (x, seg_row, mark_col, wq, bq, wk, wv, bv, wo, bo, gain, shift)
    return pl.pallas_call(
        attend_kernel,
        out_shape=shapes,
        in_specs=[pl.BlockSpec(memory_space=pltpu.VMEM)] * len(args),
        out_specs=tuple([pl.BlockSpec(memory_space=pltpu.VMEM)] * len(shapes)),
        scratch_shapes=[pltpu.VMEM((length, length), WIDE)],
        compiler_params=pltpu.CompilerParams(vmem_limit_bytes=VMEM_LIMIT),
        cost_estimate=pl.CostEstimate(
            flops=2 * length * width * (4 * width + 2 * length),
            transcendentals=heads * length * length,
            bytes_accessed=12 * length * width + 8 * width * width,
        ),
        name="attend",
    )(*args)


def feed_kernel(
    place_ref, mid0_ref, mid1_ref, cot_ref, weight_ref, wu_ref, bu_ref, wd_ref, bd_ref, gain_ref,
    shift_ref, act_s_ref, act_k_ref, slope_s_ref, slope_k_ref, low_ref, result_ref, grad_ref,
    grad_low_ref, sums_ref, stat_ref, *, half_tiles,
):
    step = pl.program_id(0)
    half = act_s_ref.shape[1]
    core = place_ref[0]
    middle = jnp.where(step < half_tiles, mid0_ref[...], mid1_ref[...])
    middle_low = middle.astype(LOW)
    low_ref[...] = middle_low
    feed = jnp.zeros_like(middle) + bd_ref[...]
    for part, (act_ref, slope_ref) in enumerate(((act_s_ref, slope_s_ref), (act_k_ref, slope_k_ref))):
        base = (1 - core if part == 0 else core) * half
        for start in range(0, half, HIDDEN_STEP):
            place = pl.ds(pl.multiple_of(base + start, HIDDEN_STEP), HIDDEN_STEP)
            here = pl.ds(start, HIDDEN_STEP)
            hidden = nn(middle_low, wu_ref[:, place]) + bu_ref[:, place]
            active, slope = gelu_pair(hidden)
            active = active.astype(LOW)
            act_ref[:, here] = active
            slope_ref[:, here] = slope.astype(LOW)
            feed = feed + nn(active, wd_ref[place, :])
    total_in = middle + feed
    center = total_in - jnp.mean(total_in, axis=1, keepdims=True)
    rstd = lax.rsqrt(jnp.mean(center * center, axis=1, keepdims=True) + EPSILON)
    normal = center * rstd
    gain = gain_ref[...]
    result = normal * gain + shift_ref[...]
    result_ref[...] = result.astype(LOW)
    weight = weight_ref[...]
    grad_result = cot_ref[...].astype(WIDE) * weight
    pulled = grad_result * gain
    grad = rstd * (
        pulled
        - jnp.mean(pulled, axis=1, keepdims=True)
        - normal * jnp.mean(pulled * normal, axis=1, keepdims=True)
    )
    grad_ref[...] = grad
    grad_low = grad.astype(LOW)
    grad_low_ref[...] = grad_low

    @pl.when(step == 0)
    def _():
        sums_ref[...] = jnp.zeros_like(sums_ref)
        stat_ref[...] = jnp.zeros_like(stat_ref)

    sums_ref[0:1, :] += jnp.sum(grad_result * normal, axis=0, keepdims=True)
    sums_ref[1:2, :] += jnp.sum(grad_result, axis=0, keepdims=True)
    sums_ref[2:3, :] += jnp.sum(grad_low.astype(WIDE), axis=0, keepdims=True)
    stat_ref[0:1, :] += jnp.broadcast_to(total(weight, feed), (1, 128))
    stat_ref[1:2, :] += jnp.broadcast_to(total(weight, result), (1, 128))


def feed_forward(place, mids, cot, weight_col, wu, bu, wd, bd, gain, shift):
    length, width = mids[0].shape
    rows = length * len(mids)
    tile = 256
    steps = rows // tile
    half_tiles = steps // 2
    hidden = wu.shape[1]
    half = hidden // 2

    def tiled(columns):
        return pl.BlockSpec((tile, columns), lambda i, *_: (i, 0))

    args = (mids[0], mids[1], cot, weight_col, wu, bu, wd, bd, gain, shift)
    in_specs = [
        pl.BlockSpec((tile, width), lambda i, *_: (jnp.minimum(i, half_tiles - 1), 0)),
        pl.BlockSpec((tile, width), lambda i, *_: (jnp.maximum(i - half_tiles, 0), 0)),
        tiled(width),
        tiled(1),
    ] + [whole(arg.shape) for arg in args[4:]]
    shapes = (
        jax.ShapeDtypeStruct((rows, half), LOW),
        jax.ShapeDtypeStruct((rows, half), LOW),
        jax.ShapeDtypeStruct((rows, half), LOW),
        jax.ShapeDtypeStruct((rows, half), LOW),
        jax.ShapeDtypeStruct((rows, width), LOW),
        jax.ShapeDtypeStruct((rows, width), LOW),
        jax.ShapeDtypeStruct((rows, width), WIDE),
        jax.ShapeDtypeStruct((rows, width), LOW),
        jax.ShapeDtypeStruct((8, width), WIDE),
        jax.ShapeDtypeStruct((8, 128), WIDE),
    )
    out_specs = tuple(
        tiled(shape.shape[1]) if shape.shape[0] == rows else whole(shape.shape) for shape in shapes
    )
    return pl.pallas_call(
        functools.partial(feed_kernel, half_tiles=half_tiles),
        out_shape=shapes,
        grid_spec=pltpu.PrefetchScalarGridSpec(
            num_scalar_prefetch=1, grid=(steps,), in_specs=in_specs, out_specs=out_specs
        ),
        compiler_params=pltpu.CompilerParams(
            vmem_limit_bytes=VMEM_LIMIT, dimension_semantics=("arbitrary",)
        ),
        cost_estimate=pl.CostEstimate(
            flops=4 * rows * width * hidden,
            transcendentals=2 * rows * hidden,
            bytes_accessed=rows * (4 * hidden + 16 * width) + 4 * width * hidden,
        ),
        name="feed_forward",
    )(place, *args)


def feed_back_kernel(
    place_ref, grad_low_ref, grad_ref, slope_s_ref, slope_k_ref, norm0_ref, norm1_ref, rstd0_ref,
    rstd1_ref, wu_ref, wd_ref, wo_ref, gain_ref, hid_s_ref, hid_k_ref, grad_one_ref, attn_ref,
    ctx_ref, up_sums_ref, sums_ref, *, half_tiles,
):
    step = pl.program_id(0)
    half = hid_s_ref.shape[1]
    core = place_ref[0]

    @pl.when(step == 0)
    def _():
        up_sums_ref[...] = jnp.zeros_like(up_sums_ref)
        sums_ref[...] = jnp.zeros_like(sums_ref)

    grad_low = grad_low_ref[...]
    grad_middle = grad_ref[...]
    for part, (hid_ref, slope_ref) in enumerate(((hid_s_ref, slope_s_ref), (hid_k_ref, slope_k_ref))):
        base = (1 - core if part == 0 else core) * half
        for start in range(0, half, HIDDEN_STEP):
            place = pl.ds(pl.multiple_of(base + start, HIDDEN_STEP), HIDDEN_STEP)
            here = pl.ds(start, HIDDEN_STEP)
            grad_act = nt(grad_low, wd_ref[place, :])
            grad_hidden = (grad_act * slope_ref[:, here].astype(WIDE)).astype(LOW)
            hid_ref[:, here] = grad_hidden
            up_sums_ref[0:1, place] += jnp.sum(grad_hidden.astype(WIDE), axis=0, keepdims=True)
            grad_middle = grad_middle + nt(grad_hidden, wu_ref[:, place])
    first = step < half_tiles
    normal = jnp.where(first, norm0_ref[...].astype(WIDE), norm1_ref[...].astype(WIDE))
    rstd = jnp.where(first, rstd0_ref[...], rstd1_ref[...])
    pulled = grad_middle * gain_ref[...]
    grad_one = rstd * (
        pulled
        - jnp.mean(pulled, axis=1, keepdims=True)
        - normal * jnp.mean(pulled * normal, axis=1, keepdims=True)
    )
    grad_one_ref[...] = grad_one
    attn = grad_one.astype(LOW)
    attn_ref[...] = attn
    ctx_ref[...] = nt(attn, wo_ref[...]).astype(LOW)
    sums_ref[0:1, :] += jnp.sum(grad_middle * normal, axis=0, keepdims=True)
    sums_ref[1:2, :] += jnp.sum(grad_middle, axis=0, keepdims=True)
    sums_ref[2:3, :] += jnp.sum(attn.astype(WIDE), axis=0, keepdims=True)


def feed_back(place, grad_low, grad, slope_s, slope_k, norms, rstds, wu, wd, wo, gain):
    rows, width = grad.shape
    tile = 256
    steps = rows // tile
    half_tiles = steps // 2
    hidden = wu.shape[1]
    half = hidden // 2

    def tiled(columns):
        return pl.BlockSpec((tile, columns), lambda i, *_: (i, 0))

    def first(columns):
        return pl.BlockSpec((tile, columns), lambda i, *_: (jnp.minimum(i, half_tiles - 1), 0))

    def second(columns):
        return pl.BlockSpec((tile, columns), lambda i, *_: (jnp.maximum(i - half_tiles, 0), 0))

    args = (
        grad_low, grad, slope_s, slope_k, norms[0], norms[1], rstds[0], rstds[1], wu, wd, wo, gain,
    )
    in_specs = [
        tiled(width), tiled(width), tiled(half), tiled(half), first(width), second(width),
        first(1), second(1),
    ] + [whole(arg.shape) for arg in args[8:]]
    shapes = (
        jax.ShapeDtypeStruct((rows, half), LOW),
        jax.ShapeDtypeStruct((rows, half), LOW),
        jax.ShapeDtypeStruct((rows, width), WIDE),
        jax.ShapeDtypeStruct((rows, width), LOW),
        jax.ShapeDtypeStruct((rows, width), LOW),
        jax.ShapeDtypeStruct((8, hidden), WIDE),
        jax.ShapeDtypeStruct((8, width), WIDE),
    )
    out_specs = tuple(
        tiled(shape.shape[1]) if shape.shape[0] == rows else whole(shape.shape) for shape in shapes
    )
    return pl.pallas_call(
        functools.partial(feed_back_kernel, half_tiles=half_tiles),
        out_shape=shapes,
        grid_spec=pltpu.PrefetchScalarGridSpec(
            num_scalar_prefetch=1, grid=(steps,), in_specs=in_specs, out_specs=out_specs
        ),
        compiler_params=pltpu.CompilerParams(
            vmem_limit_bytes=VMEM_LIMIT, dimension_semantics=("arbitrary",)
        ),
        cost_estimate=pl.CostEstimate(
            flops=4 * rows * width * hidden + 2 * rows * width * width,
            transcendentals=0,
            bytes_accessed=rows * (4 * hidden + 16 * width) + 4 * width * hidden,
        ),
        name="feed_back",
    )(place, *args)


def attend_back_kernel(
    q_ref, k_ref, v_ref, ctx_ref, grad_ctx_ref, lse_ref, seg_ref, mark_ref, grad_one_ref, wq_ref,
    wk_ref, wv_ref, dq_ref, dk_ref, dv_ref, grad_in_ref, sums_ref, bias_ref,
):
    fill_bias(bias_ref, seg_ref[...], mark_ref[...])
    width = 2 * HEAD_DIM
    pairs = q_ref.shape[1] // width

    def pair_step(pair, carried):
        lanes = pl.ds(pl.multiple_of(pair * width, width), width)
        q, k, v, grad = q_ref[:, lanes], k_ref[:, lanes], v_ref[:, lanes], grad_ctx_ref[:, lanes]
        k_turned = k.T
        shared = (grad.astype(WIDE) * ctx_ref[:, lanes].astype(WIDE)).T
        part_q, part_k, part_v = [], [], []
        for half in range(2):
            inside = slice(half * HEAD_DIM, (half + 1) * HEAD_DIM)
            delta = jnp.sum(shared[inside], axis=0, keepdims=True)
            scores = nt(k * lane_half(half), q) + bias_ref[...]
            chances = jnp.exp(scores - lse_ref[pl.ds(pair * 2 + half, 1), :])
            part_v.append(nn(chances.astype(LOW), grad))
            grad_chances = nt(v * lane_half(half), grad)
            grad_scores = (chances * (grad_chances - delta)).astype(LOW)
            part_k.append(nn(grad_scores, q))
            part_q.append(nn(k_turned[inside], grad_scores))
        first = lax.broadcasted_iota(jnp.int32, part_k[0].shape, 1) < HEAD_DIM
        dq_ref[:, lanes] = jnp.concatenate(part_q, axis=0).T.astype(LOW)
        dk_ref[:, lanes] = jnp.where(first, part_k[0], part_k[1]).astype(LOW)
        dv_ref[:, lanes] = jnp.where(first, part_v[0], part_v[1]).astype(LOW)
        return carried

    lax.fori_loop(0, pairs, pair_step, 0)
    dq, dk, dv = dq_ref[...], dk_ref[...], dv_ref[...]
    grad_in_ref[...] = (
        grad_one_ref[...]
        + nt(dq, wq_ref[...]) * SCORE_SCALE
        + nt(dk, wk_ref[...])
        + nt(dv, wv_ref[...])
    )
    sums_ref[...] = jnp.concatenate(
        [
            jnp.sum(dq.astype(WIDE), axis=0, keepdims=True) * SCORE_SCALE,
            jnp.sum(dv.astype(WIDE), axis=0, keepdims=True),
            jnp.zeros((6, dq.shape[1]), WIDE),
        ],
        axis=0,
    )


def attend_back(slot, q, k, v, ctx, grad_ctx, lse, seg_row, mark_col, grad_one, wq, wk, wv):
    length, width = q.shape
    heads = width // HEAD_DIM
    shapes = (
        jax.ShapeDtypeStruct((length, width), LOW),
        jax.ShapeDtypeStruct((length, width), LOW),
        jax.ShapeDtypeStruct((length, width), LOW),
        jax.ShapeDtypeStruct((length, width), WIDE),
        jax.ShapeDtypeStruct((8, width), WIDE),
    )
    args = (q, k, v, ctx, grad_ctx, lse, seg_row, mark_col, grad_one, wq, wk, wv)
    picked = pl.BlockSpec((length, width), lambda i: (slot, 0), pipeline_mode=pl.Buffered(1))
    in_specs = [
        picked if arg is grad_ctx or arg is grad_one else whole(arg.shape) for arg in args
    ]
    return pl.pallas_call(
        attend_back_kernel,
        grid=(1,),
        out_shape=shapes,
        in_specs=in_specs,
        out_specs=tuple(whole(shape.shape) for shape in shapes),
        scratch_shapes=[pltpu.VMEM((length, length), WIDE)],
        compiler_params=pltpu.CompilerParams(
            vmem_limit_bytes=VMEM_LIMIT, dimension_semantics=("arbitrary",)
        ),
        cost_estimate=pl.CostEstimate(
            flops=2 * length * width * (3 * width + 5 * length),
            transcendentals=heads * length * length,
            bytes_accessed=24 * length * width + 6 * width * width,
        ),
        name="attend_back",
    )(*args)


def swap_pieces(value, axis):
    count = lax.axis_size(axis)
    me = lax.axis_index(axis)
    slots = value.shape[0] // count
    pieces = [lax.dynamic_slice_in_dim(value, me * slots, slots, 0)]
    for shift in range(1, count):
        target = (me + shift) % count
        block = lax.dynamic_slice_in_dim(value, target * slots, slots, 0)
        pairs = [(source, (source + shift) % count) for source in range(count)]
        pieces.append(lax.ppermute(block, axis, pairs))
    return pieces


def return_pieces(pieces, axis):
    count = lax.axis_size(axis)
    me = lax.axis_index(axis)
    slots = pieces[0].shape[0]
    out = jnp.zeros((slots * count,) + pieces[0].shape[1:], pieces[0].dtype)
    out = lax.dynamic_update_slice_in_dim(out, pieces[0], me * slots, 0)
    for shift in range(1, count):
        pairs = [(source, (source - shift) % count) for source in range(count)]
        got = lax.ppermute(pieces[shift], axis, pairs)
        out = lax.dynamic_update_slice_in_dim(out, got, ((me + shift) % count) * slots, 0)
    return out


def sum_everywhere(value):
    part = lax.psum_scatter(value, ("dp", "seq"), scatter_dimension=0, tiled=True)
    return lax.all_gather(part, ("dp", "seq"), axis=0, tiled=True)


def on_device(
    inputs, cotangent, w_query, b_query, w_key, w_value, b_value, w_out, b_out, gain_one,
    shift_one, w_up, b_up, w_down, b_down, gain_two, shift_two, live_counts, valid_mask, segments,
):
    seqs, piece, width = inputs.shape
    count = lax.axis_size("seq")
    slots = seqs // count
    length = piece * count
    rows = slots * length
    place = (lax.axis_index("dp") % 2).astype(jnp.int32).reshape(1)

    def row_of(vector):
        return vector.astype(WIDE).reshape(1, -1)

    live = (jnp.arange(seqs) < live_counts[0]).astype(jnp.int32)
    code = segments * 2 + valid_mask * live[:, None]
    codes = jnp.concatenate(swap_pieces(code, "seq"), axis=1)
    seg = codes // 2
    weight = codes % 2
    mark = jnp.where(weight > 0, seg, -1)
    x_parts = swap_pieces(inputs, "seq")
    x_all = jnp.concatenate(x_parts, axis=1)
    cot_all = jnp.concatenate(swap_pieces(cotangent, "seq"), axis=1).reshape(rows, width)
    weight_col = weight.astype(WIDE).reshape(rows, 1)

    bq, bv, bo = row_of(b_query), row_of(b_value), row_of(b_out)
    gain1, shift1 = row_of(gain_one), row_of(shift_one)
    gain2, shift2 = row_of(gain_two), row_of(shift_two)
    bu, bd = row_of(b_up), row_of(b_down)

    seg_rows = [seg[slot].reshape(1, length) for slot in range(slots)]
    mark_cols = [mark[slot].reshape(length, 1) for slot in range(slots)]
    forward = [
        attend(
            x_all[slot], seg_rows[slot], mark_cols[slot], w_query, bq, w_key, w_value, bv, w_out,
            bo, gain1, shift1,
        )
        for slot in range(slots)
    ]
    (act_s, act_k, slope_s, slope_k, mid_low, result, grad_h2, grad_feed, sums_two, stat_two) = (
        feed_forward(
            place, [each[5] for each in forward], cot_all, weight_col, w_up, bu, w_down, bd,
            gain2, shift2,
        )
    )
    core = place[0]

    def halves(sent, kept, axis):
        low = jnp.where(core == 0, kept, sent)
        high = jnp.where(core == 0, sent, kept)
        return jnp.concatenate([low, high], axis=axis)

    grad_w_down = halves(tn(act_s, grad_feed).astype(LOW), tn(act_k, grad_feed).astype(LOW), 0)
    grad_w_down = sum_everywhere(grad_w_down)
    hid_s, hid_k, grad_h1, grad_attn, grad_ctx, up_sums, sums_one = feed_back(
        place, grad_feed, grad_h2, slope_s, slope_k, [each[6] for each in forward],
        [each[7] for each in forward], w_up, w_down, w_out, gain1,
    )
    grad_w_up = halves(tn(mid_low, hid_s).astype(LOW), tn(mid_low, hid_k).astype(LOW), 1)
    grad_w_up = sum_everywhere(grad_w_up)
    ctx_all = jnp.concatenate([each[3] for each in forward], axis=0)
    grad_w_out = tn(ctx_all, grad_attn).astype(LOW)
    backward = [
        attend_back(
            slot, *forward[slot][:4], grad_ctx, forward[slot][4], seg_rows[slot],
            mark_cols[slot], grad_h1, w_query, w_key, w_value,
        )
        for slot in range(slots)
    ]
    x_rows = x_all.reshape(rows, width)
    dq, dk, dv = (jnp.concatenate([each[i] for each in backward], axis=0) for i in range(3))
    grads = jnp.concatenate(
        [
            (tn(x_rows, dq) * SCORE_SCALE).astype(LOW),
            tn(x_rows, dk).astype(LOW),
            tn(x_rows, dv).astype(LOW),
            grad_w_out,
        ],
        axis=1,
    )
    grads = sum_everywhere(grads)

    stats = [
        sum(each[8][0, 0] for each in forward),
        sum(each[8][1, 0] for each in forward),
        stat_two[0, 0],
        stat_two[1, 0],
        jnp.sum(weight).astype(WIDE),
    ]
    stats = jnp.concatenate([jnp.stack(stats), jnp.zeros((width - 5,), WIDE)]).reshape(1, width)
    small = jnp.concatenate(
        [
            sum(each[4][0:2] for each in backward),
            sums_one[0:3],
            sums_two[0:3],
            stats,
            up_sums[0:1].reshape(-1, width),
        ],
        axis=0,
    )
    small = lax.psum(small, ("dp", "seq"))
    rms_values = jnp.sqrt(small[8, :4] / (width * small[8, 4]))

    result = result.reshape(slots, length, width)
    grad_inputs = jnp.stack([each[3] for each in backward])
    result_out = return_pieces(
        [result[:, i * piece : (i + 1) * piece] for i in range(count)], "seq"
    )
    sent = [
        grad_inputs[:, i * piece : (i + 1) * piece].astype(LOW if i else WIDE)
        for i in range(count)
    ]
    me = lax.axis_index("seq")
    grad_out = jnp.zeros((seqs, piece, width), WIDE)
    grad_out = lax.dynamic_update_slice_in_dim(grad_out, sent[0], me * slots, 0)
    for shift in range(1, count):
        pairs = [(source, (source - shift) % count) for source in range(count)]
        got = lax.ppermute(sent[shift], "seq", pairs).astype(WIDE)
        grad_out = lax.dynamic_update_slice_in_dim(
            grad_out, got, ((me + shift) % count) * slots, 0
        )

    grads = grads.astype(WIDE)
    return (
        result_out,
        grad_out,
        grads[:, 0 * width : 1 * width],
        small[0],
        grads[:, 1 * width : 2 * width],
        grads[:, 2 * width : 3 * width],
        small[1],
        grads[:, 3 * width : 4 * width],
        small[4],
        small[2],
        small[3],
        grad_w_up.astype(WIDE),
        small[9:].reshape(-1),
        grad_w_down.astype(WIDE),
        small[7],
        small[5],
        small[6],
        rms_values,
    )


def solution(mesh):
    split = P("dp", "seq", None)
    pair = P("dp", "seq")
    return jax.shard_map(
        on_device,
        mesh=mesh,
        in_specs=(split, split) + (P(),) * 15 + (P("dp"), pair, pair),
        out_specs=(split, split) + (P(),) * 16,
        check_vma=False,
    )
```

time: 1770 us -> 660 us (0.37); the launches traced: 1750 us -> 656 us
  blocking collectives: 505 us -> 60.6 us
  local copies, waits for them, and re-layouts: 459 us -> 40.4 us
  other arithmetic: 350 us -> 33.8 us
  matrix products: 185 us -> 23.1 us
  waiting for transfers between devices: 225 us -> 354 us
  Pallas kernels: 0 us -> 118 us
    unnamed x1 -> x0, blocking collectives: 455 us -> none
    reshape x1, other arithmetic: 303 us -> 0.6 us  [row_of(): return vector.astype(WIDE).reshape(1, -1)]
    reduce_scatter x0 -> x3, waiting for transfers between devices: none -> 248 us  [sum_everywhere(): lax.psum_scatter(value, ('dp', 'seq'), scatter_dimension=0, tiled=True)]
    concatenate x1 -> x2, local copies, waits for them, and re-layouts: 234 us -> 1.43 us  [the longest x1 1.38 us: on_device(): jnp.concatenate([jnp.stack(stats), jnp.zeros((width - 5,), WIDE)])]
    dot_general x30 -> x8, matrix products: 185 us -> 23.1 us  [tn(): lax.dot_general(left, right, (((0,), (0,)), ((), ())), preferred_element_...]
    reshape x15 -> x11, local copies, waits for them, and re-layouts: 135 us -> 5.3 us  [the longest x8 4.68 us: row_of(): return vector.astype(WIDE).reshape(1, -1)]
    pallas_call x0 -> x6, Pallas kernels: none -> 118 us  [the longest x2 33.4 us: attend_back(): pl.pallas_call(attend_back_kernel, grid=(1,), out_shape=shapes, in_specs=...]
    all_gather x1 -> x3, waiting for transfers between devices: 161 us -> 96.7 us  [sum_everywhere(): return lax.all_gather(part, ('dp', 'seq'), axis=0, tiled=True)]
  transfers between devices with their start and end apart: 4 -> 11, of which waited for: 3 -> 6; matrix products, arithmetic and copies ran while one was open for 6% -> 11% of each run, Pallas kernels for 0% -> 13%
where the time goes in v1:
time: 660 us; the launch traced here: 656 us
  waiting for transfers between devices  354 us (54%)
  Pallas kernels  118 us (18%)
  blocking collectives  60.6 us (9%)
  local copies, waits for them, and re-layouts  40.4 us (6%)
  other arithmetic  33.8 us (5%)
  matrix products  23.1 us (4%)
  between operations  19.3 us (3%)
  starting transfers between devices  7.58 us (1%)
    reduce_scatter x3, waiting for transfers between devices, sum_everywhere(): lax.psum_scatter(value, ('dp', 'seq'), scatter_dimension=0, tiled=True)  248 us
    all_gather x3, waiting for transfers between devices, sum_everywhere(): return lax.all_gather(part, ('dp', 'seq'), axis=0, tiled=True)  96.7 us
    psum x1, blocking collectives, on_device(): small = lax.psum(small, ('dp', 'seq'))  60.6 us
    pallas_call x2, Pallas kernels, attend_back(): pl.pallas_call(attend_back_kernel, grid=(1,), out_shape=shapes, in_specs=...  33.4 us
    pallas_call x1, Pallas kernels, feed_forward(): pl.pallas_call(functools.partial(feed_kernel, half_tiles=half_tiles), out...  30.9 us
    pallas_call x2, Pallas kernels, attend(): pl.pallas_call(attend_kernel, out_shape=shapes, in_specs=[pl.BlockSpec(me...  30.1 us
    pallas_call x1, Pallas kernels, feed_back(): pl.pallas_call(functools.partial(feed_back_kernel, half_tiles=half_tiles)...  23.2 us
    dot_general x8, matrix products, tn(): lax.dot_general(left, right, (((0,), (0,)), ((), ())), preferred_element_...  23.1 us
  transfers between devices with their start and end apart: 11, of which 6 were waited for; matrix products, arithmetic and copies ran while one was open for 11% of the time, Pallas kernels for 13%

profile of v1, /device:TPU:0, one launch (start us, length us, event | category | flops | bytes accessed | tf_op | source)
XLA Modules:
  0.0 656.2 jit_solution(10490577501689988645)
XLA Ops:
  7.3 2.5 constant_dynamic-slice_fusion.4
  9.8 3.0 collective-permute-start
  13.7 1.0 constant_dynamic-slice_fusion.1
  14.7 2.0 collective-permute-start.2
  22.0 9.5 %collective-permute-done.1 = s32[2,256]{1,0:T(2,128)S(1)} collective-permute-done((s32[2,256]{1,0:T(2,128)S(1)}, s32[2,256]{1,0:T(2,128)S(1)}, u32[]{:S(2)}, u32[]{:S(2)}) %collective-permute-start.1) | collective-permute-done | bytes 2080 | tf_op jit(solution)/shard_map/ppermute | solution.py:450
  32.4 1.0 fusion.32.weight_ref
  35.7 1.2 fusion.30
  37.0 15.1 %attend.3 = (bf16[512,768]{1,0:T(8,128)(2,1)}, bf16[512,768]{1,0:T(8,128)(2,1)}, bf16[512,768]{1,0:T(8,128)(2,1)}, bf16[512,768]{1,0:T(8,128)(2,1)}, f32[16,512]...) custom-call(bf16[512,768]{1,0:T(8,128)(2,1)} %get-tuple-element.168.x_ref, ...), custom_call_target="tpu_custom_call" | custom-call | flops 3221225472 | bytes 9437184 | tf_op jit(solution)/shard_map/attend/pallas_call | solution.py:139
  52.1 15.0 %attend.2 = (bf16[512,768]{1,0:T(8,128)(2,1)}, bf16[512,768]{1,0:T(8,128)(2,1)}, bf16[512,768]{1,0:T(8,128)(2,1)}, bf16[512,768]{1,0:T(8,128)(2,1)}, f32[16,512]...) custom-call(bf16[512,768]{1,0:T(8,128)(2,1)} %get-tuple-element.169.x_ref, ...), custom_call_target="tpu_custom_call" | custom-call | flops 3221225472 | bytes 9437184 | tf_op jit(solution)/shard_map/attend/pallas_call | solution.py:139
  67.0 2.4 pad_maximum_fusion.5
  69.4 30.9 %feed_forward.1 = (bf16[1024,1536]{1,0:T(8,128)(2,1)}, bf16[1024,1536]{1,0:T(8,128)(2,1)}, bf16[1024,1536]{1,0:T(8,128)(2,1)}, bf16[1024,1536]{1,0:T(8,128)(2,1)...) custom-call(s32[1]{0:T(128)} %bitcast.place_ref, ...), custom_call_target="tpu_custom_call" | custom-call | flops 9663676416 | bytes 34603008 | tf_op jit(solution)/shard_map/feed_forward/pallas_call | solution.py:243
  100.4 5.2 convolution_convert_fusion
  105.6 2.9 broadcast_select_fusion.1
  108.5 2.5 pad_maximum_fusion.2
  111.1 23.2 %feed_back.1 = (bf16[1024,1536]{1,0:T(8,128)(2,1)}, bf16[1024,1536]{1,0:T(8,128)(2,1)}, f32[1024,768]{1,0:T(8,128)}, bf16[1024,768]{1,0:T(8,128)(2,1)}, bf16[102...) custom-call(s32[1]{0:T(128)} %bitcast.place_ref, bf16[1024,768]{1,0:T(8,128)(2,1)} %get-tuple-element.70.grad_low_ref, ...), custom_call_target="tpu_custom_call" | custom-call | flops 10871635968 | bytes 34603008 | tf_op jit(solution)/shard_map/feed_back/pallas_call | solution.py:341
  134.3 5.0 convolution_convert_fusion.2
  139.3 3.0 broadcast_select_fusion.3
  142.3 2.8 pad_maximum_fusion.1
  145.3 1.0 copy-done.17
  147.0 1.4 fusion.18
  148.5 17.0 %attend_back.3 = (bf16[512,768]{1,0:T(8,128)(2,1)}, bf16[512,768]{1,0:T(8,128)(2,1)}, bf16[512,768]{1,0:T(8,128)(2,1)}, f32[512,768]{1,0:T(8,128)}, f32[8,768]{1,0:T(8,128)}) custom-call(bf16[512,768]{1,0:T(8,128)(2,1)} %get-tuple-element.82.q_ref, bf16[512,768]{1,0:T(8,128)(2,1)} %get-tuple-element.83.k_ref, bf16[512,768]{1,0:T(8,128)(2,1)} %get-tuple-element.84.v_ref, ...), custom_call_target="tpu_custom_call" | custom-call | flops 3825205248 | bytes 12976128 | tf_op jit(solution)/shard_map/attend_back/pallas_call | solution.py:422
  165.4 16.4 %attend_back.2 = (bf16[512,768]{1,0:T(8,128)(2,1)}, bf16[512,768]{1,0:T(8,128)(2,1)}, bf16[512,768]{1,0:T(8,128)(2,1)}, f32[512,768]{1,0:T(8,128)}, f32[8,768]{1,0:T(8,128)}) custom-call(bf16[512,768]{1,0:T(8,128)(2,1)} %get-tuple-element.66.q_ref, bf16[512,768]{1,0:T(8,128)(2,1)} %get-tuple-element.67.k_ref, bf16[512,768]{1,0:T(8,128)(2,1)} %get-tuple-element.68.v_ref, ...), custom_call_target="tpu_custom_call" | custom-call | flops 3825205248 | bytes 12976128 | tf_op jit(solution)/shard_map/attend_back/pallas_call | solution.py:422
  181.9 2.7 fusion.24
  184.6 1.5 fusion.21
  186.1 1.5 multiply_convert_fusion
  187.6 2.4 pad_maximum_fusion
  190.0 6.6 %copy.64 = bf16[768,3072]{1,0:T(8,128)(2,1)} copy(bf16[768,3072]{0,1:T(8,128)(2,1)} %pad_maximum_fusion) | data formatting | bytes 9437184
  196.7 23.2 %reduce-scatter.8.cloned.1.call-done = bf16[96,768]{1,0:T(8,128)(2,1)} async-done(((bf16[3072,768]{1,0:T(8,128)(2,1)}), bf16[96,768]{1,0:T(8,128)(2,1)}) %reduce-scatter.8.cloned.1.call-update) | async-done | bytes 147472 | tf_op jit(solution)/shard_map/reduce_scatter | solution.py:468
  220.0 112.4 %reduce-scatter.6.cloned.1.call-done = bf16[24,3072]{1,0:T(8,128)(2,1)} async-done(((bf16[768,3072]{1,0:T(8,128)(2,1)}), bf16[24,3072]{1,0:T(8,128)(2,1)}) %reduce-scatter.6.cloned.1.call-update) | async-done | bytes 147472 | tf_op jit(solution)/shard_map/reduce_scatter | solution.py:468
  332.7 111.9 %reduce-scatter.10.cloned.1.call-done = bf16[24,3072]{1,0:T(8,128)(2,1)} async-done(((bf16[768,3072]{1,0:T(8,128)(2,1)}), bf16[24,3072]{1,0:T(8,128)(2,1)}) %reduce-scatter.10.cloned.1.call-update) | async-done | bytes 147472 | tf_op jit(solution)/shard_map/reduce_scatter | solution.py:468
  445.2 1.2 broadcast_in_dim.12
  446.4 2.9 fusion.42
  449.3 1.4 collective-permute-start.3
  450.7 1.3 fusion.44
  452.1 0.9 slice_reduce_fusion
  453.0 1.0 fusion.2
  454.0 1.3 fusion.43
  457.8 1.4 concatenate.47
  460.8 60.6 %psum.7 = f32[13,768]{1,0:T(8,128)S(1)} all-reduce(f32[13,768]{1,0:T(8,128)S(1)} %concatenate.48), channel_id=1, replica_groups=mesh['dp'=16,'seq'=2] {'dp','seq'}, use_global_device_ids=true, to_apply=%region_2.3 | all-reduce | flops 9984 | bytes 79872 | tf_op jit(solution)/shard_map/psum | solution.py:572
  523.9 1.9 broadcast_in_dim.13
  525.8 1.2 fusion.1
  527.6 2.1 constant_dynamic-update-slice_fusion
  529.6 2.4 convert_dynamic-update-slice_fusion
  532.0 6.8 %convert_element_type.80 = f32[3072,768]{1,0:T(8,128)} convert(bf16[3072,768]{1,0:T(8,128)(2,1)} %all-gather.8.cloned.1.call-done) | non-fusion elementwise | flops 2359296 | bytes 14155776 | tf_op jit(solution)/shard_map/convert_element_type | solution.py:609
  538.8 38.4 %all-gather.6.cloned.1.call-done = bf16[768,3072]{1,0:T(8,128)(2,1)} async-done(((bf16[24,3072]{1,0:T(8,128)(2,1)}), bf16[768,3072]{1,0:T(8,128)(2,1)}) %all-gather.6.cloned.1.call-update) | async-done | bytes 4718608 | tf_op jit(solution)/shard_map/all_gather | solution.py:469
  577.3 7.4 %convert_element_type.77 = f32[768,3072]{1,0:T(8,128)} convert(bf16[768,3072]{1,0:T(8,128)(2,1)} %all-gather.6.cloned.1.call-done) | non-fusion elementwise | flops 2359296 | bytes 14155776 | tf_op jit(solution)/shard_map/convert_element_type | solution.py:607
  584.6 58.3 %all-gather.4.cloned.1.call-done = bf16[768,3072]{1,0:T(8,128)(2,1)} async-done(((bf16[24,3072]{1,0:T(8,128)(2,1)}), bf16[768,3072]{1,0:T(8,128)(2,1)}) %all-gather.4.cloned.1.call-update) | async-done | bytes 4718608 | tf_op jit(solution)/shard_map/all_gather | solution.py:469
  642.9 6.2 fusion.41
  (107 shorter events, 14.1 us)
Async XLA Ops:
  7.2 6.3 copy-start.6
  7.2 6.3 copy-start.7
  7.2 212.7 %reduce-scatter.8.cloned.1.call-start = ((), (), s32[]{:S(2)}) async-start(), calls=%async_computation.6 | async-start | bytes 4866048 | tf_op jit(solution)/shard_map/reduce_scatter | solution.py:468
  7.3 6.4 copy-start.2
  9.8 6.9 %copy-start.8 = (bf16[768]{0:T(1024)(128)(2,1)S(1)}, bf16[768]{0:T(1024)(128)(2,1)}, u32[]{:S(2)}) copy-start(bf16[768]{0:T(1024)(128)(2,1)} %param.29) | copy-start | bytes 4612
  9.8 7.5 %copy-start.9 = (bf16[768]{0:T(1024)(128)(2,1)S(1)}, bf16[768]{0:T(1024)(128)(2,1)}, u32[]{:S(2)}) copy-start(bf16[768]{0:T(1024)(128)(2,1)} %param.23) | copy-start | bytes 4612
  9.8 8.1 %copy-start.10 = (bf16[768]{0:T(1024)(128)(2,1)S(1)}, bf16[768]{0:T(1024)(128)(2,1)}, u32[]{:S(2)}) copy-start(bf16[768]{0:T(1024)(128)(2,1)} %param.26) | copy-start | bytes 4612
  9.8 8.7 %copy-start.11 = (bf16[768]{0:T(1024)(128)(2,1)S(1)}, bf16[768]{0:T(1024)(128)(2,1)}, u32[]{:S(2)}) copy-start(bf16[768]{0:T(1024)(128)(2,1)} %param.28) | copy-start | bytes 4612
  9.8 9.3 %copy-start.12 = (bf16[768]{0:T(1024)(128)(2,1)S(1)}, bf16[768]{0:T(1024)(128)(2,1)}, u32[]{:S(2)}) copy-start(bf16[768]{0:T(1024)(128)(2,1)} %param.30) | copy-start | bytes 4612
  9.8 9.8 %copy-start.5 = (bf16[3072]{0:T(1024)(128)(2,1)S(1)}, bf16[3072]{0:T(1024)(128)(2,1)}, u32[]{:S(2)}) copy-start(bf16[3072]{0:T(1024)(128)(2,1)} %param.32) | copy-start | bytes 18436
  9.8 10.4 %copy-start.13 = (bf16[768]{0:T(1024)(128)(2,1)S(1)}, bf16[768]{0:T(1024)(128)(2,1)}, u32[]{:S(2)}) copy-start(bf16[768]{0:T(1024)(128)(2,1)} %param.34) | copy-start | bytes 4612
  9.8 11.0 %copy-start.14 = (bf16[768]{0:T(1024)(128)(2,1)S(1)}, bf16[768]{0:T(1024)(128)(2,1)}, u32[]{:S(2)}) copy-start(bf16[768]{0:T(1024)(128)(2,1)} %param.35) | copy-start | bytes 4612
  9.8 11.6 %copy-start.15 = (bf16[768]{0:T(1024)(128)(2,1)S(1)}, bf16[768]{0:T(1024)(128)(2,1)}, u32[]{:S(2)}) copy-start(bf16[768]{0:T(1024)(128)(2,1)} %param.36) | copy-start | bytes 4612
  9.8 25.9 %collective-permute-start = (bf16[2,256,768]{2,1,0:T(8,128)(2,1)}, bf16[2,256,768]{2,1,0:T(8,128)(2,1)S(1)}, u32[]{:S(2)}, u32[]{:S(2)}) collective-permute-start(bf16[2,256,768]{2,1,0:T(8,128)(2,1)} %get-tuple-element.170), channel_id=1, source_target_pairs={{0,1},{1,0},{2,3},{3,2},{4,5},{5,4},{6,7},{7,6},{8,9},{9,8},{10,11... | collective-permute-start | bytes 2359304 | tf_op jit(solution)/shard_map/ppermute | solution.py:450
  13.6 17.9 %collective-permute-start.1 = (s32[2,256]{1,0:T(2,128)S(1)}, s32[2,256]{1,0:T(2,128)S(1)}, u32[]{:S(2)}, u32[]{:S(2)}) collective-permute-start(s32[2,256]{1,0:T(2,128)S(1)} %get-tuple-element.184), channel_id=1, source_target_pairs={{0,1},{1,0},{2,3},{3,2},{4,5},{5,4},{6,7},{7,6},{8,9},{9,8},{10,11... | collective-permute-start | bytes 6152 | tf_op jit(solution)/shard_map/ppermute | solution.py:450
  14.7 52.4 %collective-permute-start.2 = (bf16[2,256,768]{2,1,0:T(8,128)(2,1)}, bf16[2,256,768]{2,1,0:T(8,128)(2,1)}, u32[]{:S(2)}, u32[]{:S(2)}) collective-permute-start(bf16[2,256,768]{2,1,0:T(8,128)(2,1)} %get-tuple-element.167), channel_id=1, source_target_pairs={{0,1},{1,0},{2,3},{3,2},{4,5},{5,4},{6,7},{7,6},{8,9},{9,8},{10,11... | collective-permute-start | bytes 2359304 | tf_op jit(solution)/shard_map/ppermute | solution.py:450
  100.4 5.2 copy-start.26
  100.4 5.2 copy-start.27
  111.0 221.4 %reduce-scatter.6.cloned.1.call-start = ((), (), s32[]{:S(2)}) async-start(), calls=%async_computation.4 | async-start | bytes 4866048 | tf_op jit(solution)/shard_map/reduce_scatter | solution.py:468
  111.1 23.2 %copy-start.16 = (bf16[1024,768]{1,0:T(8,128)(2,1)S(1)}, bf16[1024,768]{1,0:T(8,128)(2,1)}, u32[]{:S(2)}) copy-start(bf16[1024,768]{1,0:T(8,128)(2,1)} %get-tuple-element.103) | copy-start | bytes 4718596
  134.3 5.0 copy-start.24
  145.1 1.1 copy-start.17
  145.1 1.4 copy-start.18
  145.1 299.5 %reduce-scatter.10.cloned.1.call-start = ((), (), s32[]{:S(2)}) async-start(), calls=%async_computation.8 | async-start | bytes 4866048 | tf_op jit(solution)/shard_map/reduce_scatter | solution.py:468
  145.1 1.9 copy-start.25
  165.4 16.4 %copy-start.21 = (bf16[512,768]{1,0:T(8,128)(2,1)S(1)}, bf16[512,768]{1,0:T(8,128)(2,1)}, u32[]{:S(2)}) copy-start(bf16[512,768]{1,0:T(8,128)(2,1)} %get-tuple-element.91) | copy-start | bytes 2359300
  181.9 2.7 copy-start.20
  181.9 2.7 copy-start.23
  184.6 1.5 copy-start.19
  184.6 1.5 copy-start.22
  196.7 335.3 %all-gather.8.cloned.1.call-start = ((), (), s32[]{:S(2)}) async-start(), calls=%async_computation.7 | async-start | bytes 4866048 | tf_op jit(solution)/shard_map/all_gather | solution.py:469
  219.9 357.3 %all-gather.6.cloned.1.call-start = ((), (), s32[]{:S(2)}) async-start(), calls=%async_computation.5 | async-start | bytes 4866048 | tf_op jit(solution)/shard_map/all_gather | solution.py:469
  332.4 310.5 %all-gather.4.cloned.1.call-start = ((), (), s32[]{:S(2)}) async-start(), calls=%async_computation.3 | async-start | bytes 4866048 | tf_op jit(solution)/shard_map/all_gather | solution.py:469
  445.2 7.8 %copy-start = (f32[512,768]{1,0:T(8,128)S(1)}, f32[512,768]{1,0:T(8,128)}, u32[]{:S(2)}) copy-start(f32[512,768]{1,0:T(8,128)} %get-tuple-element.87) | copy-start | bytes 4718596
  445.2 7.8 %copy-start.1 = (f32[512,768]{1,0:T(8,128)S(1)}, f32[512,768]{1,0:T(8,128)}, u32[]{:S(2)}) copy-start(f32[512,768]{1,0:T(8,128)} %get-tuple-element.81) | copy-start | bytes 4718596
  449.3 10.0 %copy-start.4 = (f32[8,768]{1,0:T(8,128)S(1)}, f32[8,768]{1,0:T(8,128)}, u32[]{:S(2)}) copy-start(f32[8,768]{1,0:T(8,128)} %get-tuple-element.97) | copy-start | bytes 73732
  449.3 10.0 %copy-start.3 = (f32[8,768]{1,0:T(8,128)S(1)}, f32[8,768]{1,0:T(8,128)}, u32[]{:S(2)}) copy-start(f32[8,768]{1,0:T(8,128)} %get-tuple-element.98) | copy-start | bytes 73732
  449.3 78.3 %collective-permute-start.3 = (bf16[2,256,768]{2,1,0:T(8,128)(2,1)}, bf16[2,256,768]{2,1,0:T(8,128)(2,1)}, u32[]{:S(2)}, u32[]{:S(2)}) collective-permute-start(bf16[2,256,768]{2,1,0:T(8,128)(2,1)} %get-tuple-element.164), channel_id=1, source_target_pairs={{0,1},{1,0},{2,3},{3,2},{4,5},{5,4},{6,7},{7,6},{8,9},{9,8},{10,11... | collective-permute-start | bytes 2359304 | tf_op jit(solution)/shard_map/ppermute | solution.py:462
  459.3 70.4 %collective-permute-start.4 = (bf16[2,256,768]{2,1,0:T(8,128)(2,1)}, bf16[2,256,768]{2,1,0:T(8,128)(2,1)}, u32[]{:S(2)}, u32[]{:S(2)}) collective-permute-start(bf16[2,256,768]{2,1,0:T(8,128)(2,1)} %fusion.2), channel_id=1, source_target_pairs={{0,1},{1,0},{2,3},{3,2},{4,5},{5,4},{6,7},{7,6},{8,9},{9,8},{10,11... | collective-permute-start | bytes 2359304 | tf_op jit(solution)/shard_map/ppermute | solution.py:589
Sparse Core Ops, SparseCore 0:
  111.2 108.7 reduce-scatter.7
  226.3 106.0 reduce-scatter.5
  338.5 106.0 reduce-scatter.9
  447.8 63.7 all-gather.7
  514.7 62.4 all-gather.5
  580.4 62.4 all-gather.3

commit v2 on v1

--- a/solution.py
+++ b/solution.py
@@ -438,35 +438,173 @@
     )(*args)
 
 
-def swap_pieces(value, axis):
-    count = lax.axis_size(axis)
-    me = lax.axis_index(axis)
-    slots = value.shape[0] // count
-    pieces = [lax.dynamic_slice_in_dim(value, me * slots, slots, 0)]
+def after(value, *earlier):
+    return lax.optimization_barrier((value,) + earlier)[0]
+
+
+def own_pieces(value, slot, slots):
+    count = lax.axis_size("seq")
+    me = lax.axis_index("seq")
+    pieces = [lax.dynamic_index_in_dim(value, me * slots + slot, 0, keepdims=False)]
     for shift in range(1, count):
         target = (me + shift) % count
-        block = lax.dynamic_slice_in_dim(value, target * slots, slots, 0)
+        block = lax.dynamic_index_in_dim(value, target * slots + slot, 0, keepdims=False)
         pairs = [(source, (source + shift) % count) for source in range(count)]
-        pieces.append(lax.ppermute(block, axis, pairs))
+        pieces.append(lax.ppermute(block, "seq", pairs))
     return pieces
 
 
-def return_pieces(pieces, axis):
-    count = lax.axis_size(axis)
-    me = lax.axis_index(axis)
+def return_pieces(pieces, link_type):
+    count = lax.axis_size("seq")
+    me = lax.axis_index("seq")
     slots = pieces[0].shape[0]
     out = jnp.zeros((slots * count,) + pieces[0].shape[1:], pieces[0].dtype)
     out = lax.dynamic_update_slice_in_dim(out, pieces[0], me * slots, 0)
     for shift in range(1, count):
         pairs = [(source, (source - shift) % count) for source in range(count)]
-        got = lax.ppermute(pieces[shift], axis, pairs)
+        got = lax.ppermute(pieces[shift].astype(link_type), "seq", pairs).astype(out.dtype)
         out = lax.dynamic_update_slice_in_dim(out, got, ((me + shift) % count) * slots, 0)
     return out
 
 
-def sum_everywhere(value):
-    part = lax.psum_scatter(value, ("dp", "seq"), scatter_dimension=0, tiled=True)
-    return lax.all_gather(part, ("dp", "seq"), axis=0, tiled=True)
+def swap(value, axis, bit):
+    count = lax.axis_size(axis)
+    return lax.ppermute(value, axis, [(source, source ^ bit) for source in range(count)])
+
+
+def bit_of(axis, bit):
+    return (lax.axis_index(axis) // bit) % 2
+
+
+def chip_orders():
+    dp, seq = lax.axis_size("dp"), lax.axis_size("seq")
+    along_dp = [("dp", 2**i) for i in range(1, dp.bit_length() - 1)]
+    along_seq = [("seq", 2**i) for i in range(seq.bit_length() - 1)]
+    x, z, y = along_dp[0], along_dp[1], along_seq[0]
+    rest = along_dp[2:] + along_seq[1:]
+    return [x, y, z] + rest, [y, z, x] + rest, [z, x, y] + rest
+
+
+HALVINGS = 4
+
+
+def scatter_sum(first, second, order):
+    for axis, bit in order[:HALVINGS]:
+        half = first.shape[0] // 2
+        mine = bit_of(axis, bit)
+
+        def part(which):
+            a = lax.dynamic_slice_in_dim(first, which * half, half, 0).astype(WIDE)
+            b = lax.dynamic_slice_in_dim(second, which * half, half, 0).astype(WIDE)
+            return (a + b).astype(LOW)
+
+        second_next = swap(part(1 - mine), axis, bit)
+        first, second = part(mine), second_next
+    share = (first.astype(WIDE) + second.astype(WIDE)).astype(LOW)
+    for axis, bit in order[HALVINGS:]:
+        share = (share.astype(WIDE) + swap(share, axis, bit).astype(WIDE)).astype(LOW)
+    return share
+
+
+def gather_shares(share, order):
+    for axis, bit in reversed(order[:HALVINGS]):
+        share = jnp.concatenate([share, swap(share, axis, bit)], axis=0)
+    return share
+
+
+def place_in(order):
+    place = 0
+    for axis, bit in order[:HALVINGS]:
+        place = place * 2 + bit_of(axis, bit)
+    return place
+
+
+def finish_down_kernel(place_ref, own_ref, other_ref, out_ref):
+    half, tile = pl.program_id(0), pl.program_id(1)
+    block = own_ref.shape[0] >> HALVINGS
+    for j in range(out_ref.shape[0] // block):
+        inside = tile * (out_ref.shape[0] // block) + j
+        spot = pl.multiple_of((inside ^ place_ref[1]) * block, block)
+        own, other = own_ref[pl.ds(spot, block), :], other_ref[pl.ds(spot, block), :]
+        out_ref[j * block : (j + 1) * block, :] = jnp.where(
+            place_ref[0] == half, own.astype(WIDE), other.astype(WIDE)
+        )
+
+
+def finish_up_kernel(place_ref, own_ref, other_ref, out_ref):
+    half, tile = pl.program_id(0), pl.program_id(1)
+    block = own_ref.shape[0] >> HALVINGS
+    found = []
+    for j in range(out_ref.shape[1] // block):
+        inside = tile * (out_ref.shape[1] // block) + j
+        spot = pl.multiple_of((inside ^ place_ref[1]) * block, block)
+        own, other = own_ref[pl.ds(spot, block), :], other_ref[pl.ds(spot, block), :]
+        found.append(jnp.where(place_ref[0] == half, own.astype(WIDE), other.astype(WIDE)))
+    out_ref[...] = jnp.concatenate(found, axis=0).T
+
+
+def finish(place, own, other, turned):
+    rows, width = own.shape
+    tile = rows // 4
+    if turned:
+        shape = (width, 2 * rows)
+        spec = pl.BlockSpec((width, tile), lambda h, t, *_: (0, h * 4 + t))
+    else:
+        shape = (2 * rows, width)
+        spec = pl.BlockSpec((tile, width), lambda h, t, *_: (h * 4 + t, 0))
+    return pl.pallas_call(
+        finish_up_kernel if turned else finish_down_kernel,
+        out_shape=jax.ShapeDtypeStruct(shape, WIDE),
+        grid_spec=pltpu.PrefetchScalarGridSpec(
+            num_scalar_prefetch=1,
+            grid=(2, 4),
+            in_specs=[whole(own.shape), whole(other.shape)],
+            out_specs=spec,
+        ),
+        compiler_params=pltpu.CompilerParams(vmem_limit_bytes=VMEM_LIMIT),
+        cost_estimate=pl.CostEstimate(
+            flops=0, transcendentals=0, bytes_accessed=12 * rows * width
+        ),
+        name="finish",
+    )(place, own, other)
+
+
+def finish_square_kernel(place_ref, *refs):
+    parts = (len(refs) - 4) // 2
+    own_refs, other_refs, out_refs = refs[:parts], refs[parts : 2 * parts], refs[2 * parts :]
+    rows_each, width = own_refs[0].shape
+    block = rows_each >> HALVINGS
+    core = place_ref[0]
+    for half in range(2):
+        for row in range(0, rows_each * parts, block):
+            part = row // rows_each
+            inside = (row - part * rows_each) // block
+            spot = pl.multiple_of((inside ^ place_ref[1 + part]) * block, block)
+            own = own_refs[part][pl.ds(spot, block), :].astype(WIDE)
+            other = other_refs[part][pl.ds(spot, block), :].astype(WIDE)
+            out = out_refs[half * 2 + row // width]
+            out[row % width : row % width + block, :] = jnp.where(core == half, own, other)
+
+
+def finish_square(place, owns, others):
+    width = owns[0].shape[1]
+    shape = jax.ShapeDtypeStruct((width, width), WIDE)
+    args = (*owns, *others)
+    return pl.pallas_call(
+        finish_square_kernel,
+        out_shape=(shape,) * 4,
+        grid_spec=pltpu.PrefetchScalarGridSpec(
+            num_scalar_prefetch=1,
+            grid=(1,),
+            in_specs=[whole(arg.shape) for arg in args],
+            out_specs=(whole(shape.shape),) * 4,
+        ),
+        compiler_params=pltpu.CompilerParams(vmem_limit_bytes=VMEM_LIMIT),
+        cost_estimate=pl.CostEstimate(
+            flops=0, transcendentals=0, bytes_accessed=24 * width * width
+        ),
+        name="finish_square",
+    )(place, *args)
 
 
 def on_device(
@@ -478,20 +616,24 @@
     slots = seqs // count
     length = piece * count
     rows = slots * length
-    place = (lax.axis_index("dp") % 2).astype(jnp.int32).reshape(1)
+    core = bit_of("dp", 1).astype(jnp.int32)
+    orders = chip_orders()
+    places = [place_in(order).astype(jnp.int32) for order in orders]
+    core_place = core.reshape(1)
 
     def row_of(vector):
         return vector.astype(WIDE).reshape(1, -1)
 
     live = (jnp.arange(seqs) < live_counts[0]).astype(jnp.int32)
     code = segments * 2 + valid_mask * live[:, None]
-    codes = jnp.concatenate(swap_pieces(code, "seq"), axis=1)
+    codes = jnp.stack([jnp.concatenate(own_pieces(code, slot, slots)) for slot in range(slots)])
     seg = codes // 2
     weight = codes % 2
     mark = jnp.where(weight > 0, seg, -1)
-    x_parts = swap_pieces(inputs, "seq")
-    x_all = jnp.concatenate(x_parts, axis=1)
-    cot_all = jnp.concatenate(swap_pieces(cotangent, "seq"), axis=1).reshape(rows, width)
+    x_slots = []
+    for slot in range(slots):
+        value = inputs if slot == 0 else after(inputs, x_slots[-1])
+        x_slots.append(jnp.concatenate(own_pieces(value, slot, slots)))
     weight_col = weight.astype(WIDE).reshape(rows, 1)
 
     bq, bv, bo = row_of(b_query), row_of(b_value), row_of(b_out)
@@ -503,32 +645,44 @@
     mark_cols = [mark[slot].reshape(length, 1) for slot in range(slots)]
     forward = [
         attend(
-            x_all[slot], seg_rows[slot], mark_cols[slot], w_query, bq, w_key, w_value, bv, w_out,
-            bo, gain1, shift1,
+            x_slots[slot], seg_rows[slot], mark_cols[slot], w_query, bq, w_key, w_value, bv,
+            w_out, bo, gain1, shift1,
         )
         for slot in range(slots)
     ]
+    late_cot = after(cotangent, x_slots[-1])
+    cot_all = jnp.concatenate(
+        [piece_of for slot in range(slots) for piece_of in own_pieces(late_cot, slot, slots)]
+    )
     (act_s, act_k, slope_s, slope_k, mid_low, result, grad_h2, grad_feed, sums_two, stat_two) = (
         feed_forward(
-            place, [each[5] for each in forward], cot_all, weight_col, w_up, bu, w_down, bd,
+            core_place, [each[5] for each in forward], cot_all, weight_col, w_up, bu, w_down, bd,
             gain2, shift2,
         )
     )
-    core = place[0]
-
-    def halves(sent, kept, axis):
-        low = jnp.where(core == 0, kept, sent)
-        high = jnp.where(core == 0, sent, kept)
-        return jnp.concatenate([low, high], axis=axis)
-
-    grad_w_down = halves(tn(act_s, grad_feed).astype(LOW), tn(act_k, grad_feed).astype(LOW), 0)
-    grad_w_down = sum_everywhere(grad_w_down)
+    down_got = swap(tn(act_s, grad_feed).astype(LOW), "dp", 1)
+    down_kept = tn(act_k, grad_feed).astype(LOW)
+    down_share = scatter_sum(down_kept, down_got, orders[0])
+    down_own = gather_shares(down_share, orders[0])
+    down_other = swap(down_own, "dp", 1)
+    grad_w_down = finish(jnp.stack([core, places[0]]), down_own, down_other, False)
+
+    result = result.reshape(slots, length, width)
+    result_out = return_pieces(
+        [result[:, i * piece : (i + 1) * piece] for i in range(count)], LOW
+    )
+
     hid_s, hid_k, grad_h1, grad_attn, grad_ctx, up_sums, sums_one = feed_back(
-        place, grad_feed, grad_h2, slope_s, slope_k, [each[6] for each in forward],
+        core_place, grad_feed, grad_h2, slope_s, slope_k, [each[6] for each in forward],
         [each[7] for each in forward], w_up, w_down, w_out, gain1,
     )
-    grad_w_up = halves(tn(mid_low, hid_s).astype(LOW), tn(mid_low, hid_k).astype(LOW), 1)
-    grad_w_up = sum_everywhere(grad_w_up)
+    up_got = swap(tn(hid_s, mid_low).astype(LOW), "dp", 1)
+    up_kept = tn(hid_k, mid_low).astype(LOW)
+    up_share = scatter_sum(up_kept, up_got, orders[1])
+    up_own = gather_shares(up_share, orders[1])
+    up_other = swap(up_own, "dp", 1)
+    grad_w_up = finish(jnp.stack([core, places[1]]), up_own, up_other, True)
+
     ctx_all = jnp.concatenate([each[3] for each in forward], axis=0)
     grad_w_out = tn(ctx_all, grad_attn).astype(LOW)
     backward = [
@@ -538,18 +692,23 @@
         )
         for slot in range(slots)
     ]
-    x_rows = x_all.reshape(rows, width)
+    x_rows = jnp.concatenate(x_slots)
     dq, dk, dv = (jnp.concatenate([each[i] for each in backward], axis=0) for i in range(3))
-    grads = jnp.concatenate(
-        [
-            (tn(x_rows, dq) * SCORE_SCALE).astype(LOW),
-            tn(x_rows, dk).astype(LOW),
-            tn(x_rows, dv).astype(LOW),
-            grad_w_out,
-        ],
-        axis=1,
-    )
-    grads = sum_everywhere(grads)
+    low_half = jnp.concatenate(
+        [(tn(x_rows, dq) * SCORE_SCALE).astype(LOW), tn(x_rows, dk).astype(LOW)]
+    )
+    high_half = jnp.concatenate([tn(x_rows, dv).astype(LOW), grad_w_out])
+    square_got = swap(jnp.where(core == 0, high_half, low_half), "dp", 1)
+    square_kept = jnp.where(core == 0, low_half, high_half)
+    parts = len(orders)
+    each_rows = square_kept.shape[0] // parts
+    square_own, square_other = [], []
+    for part, order in enumerate(orders):
+        inside = slice(part * each_rows, (part + 1) * each_rows)
+        share = scatter_sum(square_kept[inside], square_got[inside], order)
+        square_own.append(gather_shares(share, order))
+        square_other.append(swap(square_own[-1], "dp", 1))
+    squares = finish_square(jnp.stack([core] + places), square_own, square_other)
 
     stats = [
         sum(each[8][0, 0] for each in forward),
@@ -569,44 +728,29 @@
         ],
         axis=0,
     )
-    small = lax.psum(small, ("dp", "seq"))
+    for axis, bit in [("dp", 1)] + orders[0]:
+        small = small + swap(small, axis, bit)
     rms_values = jnp.sqrt(small[8, :4] / (width * small[8, 4]))
 
-    result = result.reshape(slots, length, width)
     grad_inputs = jnp.stack([each[3] for each in backward])
-    result_out = return_pieces(
-        [result[:, i * piece : (i + 1) * piece] for i in range(count)], "seq"
-    )
-    sent = [
-        grad_inputs[:, i * piece : (i + 1) * piece].astype(LOW if i else WIDE)
-        for i in range(count)
-    ]
-    me = lax.axis_index("seq")
-    grad_out = jnp.zeros((seqs, piece, width), WIDE)
-    grad_out = lax.dynamic_update_slice_in_dim(grad_out, sent[0], me * slots, 0)
-    for shift in range(1, count):
-        pairs = [(source, (source - shift) % count) for source in range(count)]
-        got = lax.ppermute(sent[shift], "seq", pairs).astype(WIDE)
-        grad_out = lax.dynamic_update_slice_in_dim(
-            grad_out, got, ((me + shift) % count) * slots, 0
-        )
-
-    grads = grads.astype(WIDE)
+    grad_out = return_pieces(
+        [grad_inputs[:, i * piece : (i + 1) * piece] for i in range(count)], LOW
+    )
     return (
         result_out,
         grad_out,
-        grads[:, 0 * width : 1 * width],
+        squares[0],
         small[0],
-        grads[:, 1 * width : 2 * width],
-        grads[:, 2 * width : 3 * width],
+        squares[1],
+        squares[2],
         small[1],
-        grads[:, 3 * width : 4 * width],
+        squares[3],
         small[4],
         small[2],
         small[3],
-        grad_w_up.astype(WIDE),
+        grad_w_up,
         small[9:].reshape(-1),
-        grad_w_down.astype(WIDE),
+        grad_w_down,
         small[7],
         small[5],
         small[6],

time: 660 us -> 443 us (0.67)
  waiting for transfers between devices: 354 us -> 117 us
  starting transfers between devices: 7.58 us -> 76.1 us
  blocking collectives: 60.6 us -> 0 us
  Pallas kernels: 118 us -> 141 us
  between operations: 19.3 us -> 6.16 us
  other arithmetic: 33.8 us -> 23.1 us
    reduce_scatter x3 -> x0, waiting for transfers between devices: 248 us -> none  [sum_everywhere(): lax.psum_scatter(value, ('dp', 'seq'), scatter_dimension=0, tiled=True)]
    ppermute x5 -> x61, waiting for transfers between devices: 9.5 us -> 117 us  [the longest x53 93.4 us: swap(): lax.ppermute(value, axis, [(source, source ^ bit) for source in range(cou...]
    all_gather x3 -> x0, waiting for transfers between devices: 96.7 us -> none  [sum_everywhere(): return lax.all_gather(part, ('dp', 'seq'), axis=0, tiled=True)]
    ppermute x5 -> x61, starting transfers between devices: 7.17 us -> 76.1 us  [the longest x53 66.8 us: swap(): lax.ppermute(value, axis, [(source, source ^ bit) for source in range(cou...]
    psum x1 -> x0, blocking collectives: 60.6 us -> none  [on_device(): small = lax.psum(small, ('dp', 'seq'))]
    pallas_call x0 -> x3, Pallas kernels: none -> 24.3 us  [the longest x2 16.4 us: finish(): pl.pallas_call(finish_up_kernel if turned else finish_down_kernel, out_sh...]
    convert_element_type x2 -> x20, other arithmetic: 14.2 us -> 6.42 us  [part(): return (a + b).astype(LOW)]
    concatenate x5 -> x20, other arithmetic: 10.2 us -> 3.55 us  [the longest x2 1.86 us: on_device(): x_slots.append(jnp.concatenate(own_pieces(value, slot, slots)))]
  transfers between devices with their start and end apart: 11 -> 61, of which waited for: 6 -> 19; matrix products, arithmetic and copies ran while one was open for 11% -> 19% of each run, Pallas kernels for 13% -> 23%
where the time goes in v2:
time: 443 us; the launch traced here: 435 us
  Pallas kernels  141 us (32%)
  waiting for transfers between devices  117 us (26%)
  starting transfers between devices  76.1 us (17%)
  local copies, waits for them, and re-layouts  43.5 us (10%)
  matrix products  28.3 us (6%)
  other arithmetic  23.1 us (5%)
  between operations  6.16 us (1%)
    ppermute x53, waiting for transfers between devices, swap(): lax.ppermute(value, axis, [(source, source ^ bit) for source in range(cou...  93.4 us
    ppermute x53, starting transfers between devices, swap(): lax.ppermute(value, axis, [(source, source ^ bit) for source in range(cou...  66.8 us
    pallas_call x2, Pallas kernels, attend_back(): pl.pallas_call(attend_back_kernel, grid=(1,), out_shape=shapes, in_specs=...  32.9 us
    pallas_call x1, Pallas kernels, feed_forward(): pl.pallas_call(functools.partial(feed_kernel, half_tiles=half_tiles), out...  31.1 us
    pallas_call x2, Pallas kernels, attend(): pl.pallas_call(attend_kernel, out_shape=shapes, in_specs=[pl.BlockSpec(me...  30 us
    dot_general x8, matrix products, tn(): lax.dot_general(left, right, (((0,), (0,)), ((), ())), preferred_element_...  28.3 us
    pallas_call x1, Pallas kernels, feed_back(): pl.pallas_call(functools.partial(feed_back_kernel, half_tiles=half_tiles)...  23 us
    pallas_call x2, Pallas kernels, finish(): pl.pallas_call(finish_up_kernel if turned else finish_down_kernel, out_sh...  16.4 us
  transfers between devices with their start and end apart: 61, of which 19 were waited for; matrix products, arithmetic and copies ran while one was open for 19% of the time, Pallas kernels for 23%

profile of v2, /device:TPU:0, one launch (start us, length us, event | category | flops | bytes accessed | tf_op | source)
XLA Modules:
  0.0 435.1 jit_solution(6455099448705878513)
XLA Ops:
  2.0 3.0 collective-permute-start
  6.6 2.0 collective-permute-start.2
  27.4 8.3 %collective-permute-done.3 = bf16[256,768]{1,0:T(8,128)(2,1)S(1)} collective-permute-done((bf16[256,768]{1,0:T(8,128)(2,1)S(1)}, bf16[256,768]{1,0:T(8,128)(2,1)S(1)}, u32[]{:S(2)}, u32[]{:S(2)}) %collective-permute-start.3) | collective-permute-done | bytes 393248 | tf_op jit(solution)/shard_map/ppermute | solution.py:453
  38.8 15.1 %attend.2 = (bf16[512,768]{1,0:T(8,128)(2,1)}, bf16[512,768]{1,0:T(8,128)(2,1)}, bf16[512,768]{1,0:T(8,128)(2,1)}, bf16[512,768]{1,0:T(8,128)(2,1)}, f32[16,512]...) custom-call(bf16[512,768]{1,0:T(8,128)(2,1)} %pad_maximum_fusion.7.x_ref, ...), custom_call_target="tpu_custom_call" | custom-call | flops 3221225472 | bytes 9437184 | tf_op jit(solution)/shard_map/attend/pallas_call | solution.py:139
  53.9 14.9 %attend.3 = (bf16[512,768]{1,0:T(8,128)(2,1)}, bf16[512,768]{1,0:T(8,128)(2,1)}, bf16[512,768]{1,0:T(8,128)(2,1)}, bf16[512,768]{1,0:T(8,128)(2,1)}, f32[16,512]...) custom-call(bf16[512,768]{1,0:T(8,128)(2,1)} %pad_maximum_fusion.8.x_ref, ...), custom_call_target="tpu_custom_call" | custom-call | flops 3221225472 | bytes 9437184 | tf_op jit(solution)/shard_map/attend/pallas_call | solution.py:139
  70.1 31.1 %feed_forward.1 = (bf16[1024,1536]{1,0:T(8,128)(2,1)}, bf16[1024,1536]{1,0:T(8,128)(2,1)}, bf16[1024,1536]{1,0:T(8,128)(2,1)}, bf16[1024,1536]{1,0:T(8,128)(2,1)...) custom-call(s32[1]{0:T(128)} %bitcast.place_ref, ...), custom_call_target="tpu_custom_call" | custom-call | flops 9663676416 | bytes 34603008 | tf_op jit(solution)/shard_map/feed_forward/pallas_call | solution.py:243
  101.3 6.4 %convolution_convert_fusion = bf16[1536,768]{1,0:T(8,128)(2,1)} fusion(bf16[1024,1536]{1,0:T(8,128)(2,1)} %get-tuple-element.119, bf16[1024,768]{1,0:T(8,128)(2,1)} %get-tuple-element.78.grad_low_ref), kind=kOutput, calls=%fused_computation | convolution fusion | flops 2417098752 | bytes 7077888 | tf_op jit(solution)/shard_map/dot_general | solution.py:36
  107.7 23.0 %feed_back.1 = (bf16[1024,1536]{1,0:T(8,128)(2,1)}, bf16[1024,1536]{1,0:T(8,128)(2,1)}, f32[1024,768]{1,0:T(8,128)}, bf16[1024,768]{1,0:T(8,128)(2,1)}, bf16[102...) custom-call(s32[1]{0:T(128)} %bitcast.place_ref, bf16[1024,768]{1,0:T(8,128)(2,1)} %get-tuple-element.78.grad_low_ref, ...), custom_call_target="tpu_custom_call" | custom-call | flops 10871635968 | bytes 34603008 | tf_op jit(solution)/shard_map/feed_back/pallas_call | solution.py:341
  130.7 6.6 %convolution_convert_fusion.2 = bf16[1536,768]{1,0:T(8,128)(2,1)} fusion(bf16[1024,1536]{1,0:T(8,128)(2,1)} %get-tuple-element.117, bf16[1024,768]{1,0:T(8,128)(2,1)} %get-tuple-element.116), kind=kOutput, calls=%fused_computation.2 | convolution fusion | flops 2417098752 | bytes 7077888 | tf_op jit(solution)/shard_map/dot_general | solution.py:36
  139.2 16.5 %attend_back.3 = (bf16[512,768]{1,0:T(8,128)(2,1)}, bf16[512,768]{1,0:T(8,128)(2,1)}, bf16[512,768]{1,0:T(8,128)(2,1)}, f32[512,768]{1,0:T(8,128)}, f32[8,768]{1,0:T(8,128)}) custom-call(bf16[512,768]{1,0:T(8,128)(2,1)} %get-tuple-element.90.q_ref, bf16[512,768]{1,0:T(8,128)(2,1)} %get-tuple-element.91.k_ref, bf16[512,768]{1,0:T(8,128)(2,1)} %get-tuple-element.92.v_ref, ...), custom_call_target="tpu_custom_call" | custom-call | flops 3825205248 | bytes 12976128 | tf_op jit(solution)/shard_map/attend_back/pallas_call | solution.py:422
  155.7 16.4 %attend_back.2 = (bf16[512,768]{1,0:T(8,128)(2,1)}, bf16[512,768]{1,0:T(8,128)(2,1)}, bf16[512,768]{1,0:T(8,128)(2,1)}, f32[512,768]{1,0:T(8,128)}, f32[8,768]{1,0:T(8,128)}) custom-call(bf16[512,768]{1,0:T(8,128)(2,1)} %get-tuple-element.74.q_ref, bf16[512,768]{1,0:T(8,128)(2,1)} %get-tuple-element.75.k_ref, bf16[512,768]{1,0:T(8,128)(2,1)} %get-tuple-element.76.v_ref, ...), custom_call_target="tpu_custom_call" | custom-call | flops 3825205248 | bytes 12976128 | tf_op jit(solution)/shard_map/attend_back/pallas_call | solution.py:422
  172.1 2.7 multiply_convert_fusion
  177.8 2.0 broadcast_select_fusion.1
  188.8 5.2 %convolution_convert_fusion.1 = bf16[1536,768]{1,0:T(8,128)(2,1)S(1)} fusion(bf16[1024,1536]{1,0:T(8,128)(2,1)} %get-tuple-element.118, bf16[1024,768]{1,0:T(8,128)(2,1)} %get-tuple-element.78.grad_low_ref), kind=kOutput, calls=%fused_computation.1 | convolution fusion | flops 2417098752 | bytes 7077888 | tf_op jit(solution)/shard_map/dot_general | solution.py:36
  195.5 3.1 convolution_convert_fusion.3
  199.4 3.4 collective-permute-done.38
  204.5 2.2 add_convert_fusion.1
  207.7 2.2 add_convert_fusion.3
  218.7 2.2 collective-permute-done.25
  222.6 21.4 %collective-permute-done.17 = bf16[256,768]{1,0:T(8,128)(2,1)S(1)} collective-permute-done((bf16[256,768]{1,0:T(8,128)(2,1)S(1)}, bf16[256,768]{1,0:T(8,128)(2,1)S(1)}, u32[]{:S(2)}, u32[]{:S(2)}) %collective-permute-start.17) | collective-permute-done | bytes 393248 | tf_op jit(solution)/shard_map/ppermute | solution.py:472
  247.9 2.0 collective-permute-start.43
  249.9 2.1 collective-permute-done.18
  254.3 8.6 %collective-permute-done.27 = bf16[64,768]{1,0:T(8,128)(2,1)S(1)} collective-permute-done((bf16[64,768]{1,0:T(8,128)(2,1)S(1)}, bf16[64,768]{1,0:T(8,128)(2,1)S(1)}, u32[]{:S(2)}, u32[]{:S(2)}) %collective-permute-start.27) | collective-permute-done | bytes 98336 | tf_op jit(solution)/shard_map/ppermute | solution.py:472
  262.9 2.7 collective-permute-start.28
  267.6 2.7 collective-permute-start.12
  270.4 1.9 collective-permute-start.44
  272.4 2.1 collective-permute-done.54
  275.2 2.9 collective-permute-start.29
  278.2 8.4 %collective-permute-done.55 = bf16[96,768]{1,0:T(8,128)(2,1)S(1)} collective-permute-done((bf16[96,768]{1,0:T(8,128)(2,1)S(1)}, bf16[96,768]{1,0:T(8,128)(2,1)S(1)}, u32[]{:S(2)}, u32[]{:S(2)}) %collective-permute-start.55) | collective-permute-done | bytes 147488 | tf_op jit(solution)/shard_map/ppermute | solution.py:472
  287.4 2.8 collective-permute-done.45
  291.7 2.8 collective-permute-start.21
  294.5 2.2 collective-permute-done.56
  296.7 3.9 collective-permute-start.57
  303.1 2.9 collective-permute-start.13
  309.9 2.4 collective-permute-start.48
  315.9 6.2 %collective-permute-done.58 = bf16[384,768]{1,0:T(8,128)(2,1)S(1)} collective-permute-done((bf16[384,768]{1,0:T(8,128)(2,1)S(1)}, bf16[384,768]{1,0:T(8,128)(2,1)S(1)}, u32[]{:S(2)}, u32[]{:S(2)}) %collective-permute-start.58) | collective-permute-done | bytes 589856 | tf_op jit(solution)/shard_map/ppermute | solution.py:472
  322.2 3.6 collective-permute-start.59
  334.2 17.0 %collective-permute-done.59 = bf16[768,768]{1,0:T(8,128)(2,1)S(1)} collective-permute-done((bf16[768,768]{1,0:T(8,128)(2,1)S(1)}, bf16[768,768]{1,0:T(8,128)(2,1)S(1)}, u32[]{:S(2)}, u32[]{:S(2)}) %collective-permute-start.59) | collective-permute-done | bytes 1179680 | tf_op jit(solution)/shard_map/ppermute | solution.py:472
  358.1 3.6 collective-permute-done.15
  361.9 3.2 collective-permute-done.32
  367.5 2.6 collective-permute-done.24
  374.8 4.5 %collective-permute-done.16 = bf16[256,768]{1,0:T(8,128)(2,1)S(1)} collective-permute-done((bf16[256,768]{1,0:T(8,128)(2,1)S(1)}, bf16[256,768]{1,0:T(8,128)(2,1)S(1)}, u32[]{:S(2)}, u32[]{:S(2)}) %collective-permute-start.16) | collective-permute-done | bytes 393248 | tf_op jit(solution)/shard_map/ppermute | solution.py:472
  379.4 6.1 %collective-permute-start.40 = (f32[13,768]{1,0:T(8,128)S(1)}, f32[13,768]{1,0:T(8,128)S(1)}, u32[]{:S(2)}, u32[]{:S(2)}) collective-permute-start(f32[13,768]{1,0:T(8,128)S(1)} %add.542), channel_id=1, source_target_pairs={{0,16},{2,18},{4,20},{6,22},{8,24},{10,26},{12,28},{14,30},{16,0},... | collective-permute-start | bytes 119816 | tf_op jit(solution)/shard_map/ppermute | solution.py:472
  388.0 14.9 %collective-permute-done.6 = bf16[2,256,768]{2,1,0:T(8,128)(2,1)S(1)} collective-permute-done((bf16[2,256,768]{2,1,0:T(8,128)(2,1)S(1)}, bf16[2,256,768]{2,1,0:T(8,128)(2,1)S(1)}, u32[]{:S(2)}, u32[]{:S(2)}) %collective-permute-start.6) | collective-permute-done | bytes 786464 | tf_op jit(solution)/shard_map/ppermute | solution.py:465
  407.2 2.1 constant_dynamic-update-slice_fusion.25
  410.6 7.9 %finish_square.1 = (f32[768,768]{1,0:T(8,128)}, f32[768,768]{1,0:T(8,128)}, f32[768,768]{1,0:T(8,128)}, f32[768,768]{1,0:T(8,128)}) custom-call(s32[4]{0:T(128)} %pad_add_fusion.3.place_ref, bf16[512,768]{1,0:T(8,128)(2,1)} %constant_dynamic-update-slice_fusion.refs_0_, bf16[512,768]{1,0:T(8,128)(2,1)} %constant_dynamic-update-slice_fusion.5.refs_1_, ...), custom_call_target="tpu_custom_call" | custom-call | bytes 14155776 | tf_op jit(solution)/shard_map/finish_square/pallas_call | solution.py:593
  418.4 8.0 %finish.3 = f32[3072,768]{1,0:T(8,128)} custom-call(s32[2]{0:T(128)} %get-tuple-element.206.place_ref, bf16[1536,768]{1,0:T(8,128)(2,1)} %constant_dynamic-update-slice_fusion.20.own_ref, bf16[1536,768]{1,0:T(8,128)(2,1)} %collective-permute-done.60.other_ref), custom_call_target="tpu_custom_call" | custom-call | bytes 14155776 | tf_op jit(solution)/shard_map/finish/pallas_call | solution.py:555
  426.4 8.5 %finish.2 = f32[768,3072]{1,0:T(8,128)} custom-call(s32[2]{0:T(128)} %get-tuple-element.205.place_ref, bf16[1536,768]{1,0:T(8,128)(2,1)} %constant_dynamic-update-slice_fusion.15.own_ref, bf16[1536,768]{1,0:T(8,128)(2,1)} %collective-permute-done.50.other_ref), custom_call_target="tpu_custom_call" | custom-call | bytes 14155776 | tf_op jit(solution)/shard_map/finish/pallas_call | solution.py:555
  (255 shorter events, 102.8 us)
Async XLA Ops:
  2.0 22.6 %collective-permute-start = (bf16[256,768]{1,0:T(8,128)(2,1)S(1)}, bf16[256,768]{1,0:T(8,128)(2,1)S(1)}, u32[]{:S(2)}, u32[]{:S(2)}) collective-permute-start(bf16[256,768]{1,0:T(8,128)(2,1)S(1)} %get-tuple-element.173), channel_id=1, source_target_pairs={{0,1},{1,0},{2,3},{3,2},{4,5},{5,4},{6,7},{7,6},{8,9},{9,8},{10,11... | collective-permute-start | bytes 1179656 | tf_op jit(solution)/shard_map/ppermute | solution.py:453
  6.5 14.8 %collective-permute-start.1 = (s32[256]{0:T(256)S(1)}, s32[256]{0:T(256)S(1)}, u32[]{:S(2)}, u32[]{:S(2)}) collective-permute-start(s32[256]{0:T(256)S(1)} %bitcast.75), channel_id=1, source_target_pairs={{0,1},{1,0},{2,3},{3,2},{4,5},{5,4},{6,7},{7,6},{8,9},{9,8},{10,11... | collective-permute-start | bytes 3080 | tf_op jit(solution)/shard_map/ppermute | solution.py:453
  6.6 14.7 %collective-permute-start.2 = (s32[256]{0:T(256)S(1)}, s32[256]{0:T(256)S(1)}, u32[]{:S(2)}, u32[]{:S(2)}) collective-permute-start(s32[256]{0:T(256)S(1)} %bitcast.74), channel_id=1, source_target_pairs={{0,1},{1,0},{2,3},{3,2},{4,5},{5,4},{6,7},{7,6},{8,9},{9,8},{10,11... | collective-permute-start | bytes 3080 | tf_op jit(solution)/shard_map/ppermute | solution.py:453
  25.6 10.1 %collective-permute-start.3 = (bf16[256,768]{1,0:T(8,128)(2,1)S(1)}, bf16[256,768]{1,0:T(8,128)(2,1)S(1)}, u32[]{:S(2)}, u32[]{:S(2)}) collective-permute-start(bf16[256,768]{1,0:T(8,128)(2,1)S(1)} %get-tuple-element.171), channel_id=1, source_target_pairs={{0,1},{1,0},{2,3},{3,2},{4,5},{5,4},{6,7},{7,6},{8,9},{9,8},{10,11... | collective-permute-start | bytes 1179656 | tf_op jit(solution)/shard_map/ppermute | solution.py:453
  36.7 32.1 %collective-permute-start.4 = (bf16[256,768]{1,0:T(8,128)(2,1)S(1)}, bf16[256,768]{1,0:T(8,128)(2,1)S(1)}, u32[]{:S(2)}, u32[]{:S(2)}) collective-permute-start(bf16[256,768]{1,0:T(8,128)(2,1)S(1)} %get-tuple-element.169), channel_id=1, source_target_pairs={{0,1},{1,0},{2,3},{3,2},{4,5},{5,4},{6,7},{7,6},{8,9},{9,8},{10,11... | collective-permute-start | bytes 1179656 | tf_op jit(solution)/shard_map/ppermute | solution.py:453
  37.2 31.7 %collective-permute-start.5 = (bf16[256,768]{1,0:T(8,128)(2,1)S(1)}, bf16[256,768]{1,0:T(8,128)(2,1)S(1)}, u32[]{:S(2)}, u32[]{:S(2)}) collective-permute-start(bf16[256,768]{1,0:T(8,128)(2,1)S(1)} %get-tuple-element.167), channel_id=1, source_target_pairs={{0,1},{1,0},{2,3},{3,2},{4,5},{5,4},{6,7},{7,6},{8,9},{9,8},{10,11... | collective-permute-start | bytes 1179656 | tf_op jit(solution)/shard_map/ppermute | solution.py:453
  107.7 96.8 %collective-permute-start.51 = (bf16[1536,768]{1,0:T(8,128)(2,1)}, bf16[1536,768]{1,0:T(8,128)(2,1)}, u32[]{:S(2)}, u32[]{:S(2)}) collective-permute-start(bf16[1536,768]{1,0:T(8,128)(2,1)} %convolution_convert_fusion), channel_id=1, source_target_pairs={{0,2},{2,0},{4,6},{6,4},{8,10},{10,8},{12,14},{14,12},{16,18},{18,... | collective-permute-start | bytes 7077896 | tf_op jit(solution)/shard_map/ppermute | solution.py:472
  137.3 70.4 %collective-permute-start.41 = (bf16[1536,768]{1,0:T(8,128)(2,1)}, bf16[1536,768]{1,0:T(8,128)(2,1)}, u32[]{:S(2)}, u32[]{:S(2)}) collective-permute-start(bf16[1536,768]{1,0:T(8,128)(2,1)} %convolution_convert_fusion.2), channel_id=1, source_target_pairs={{0,2},{2,0},{4,6},{6,4},{8,10},{10,8},{12,14},{14,12},{16,18},{18,... | collective-permute-start | bytes 7077896 | tf_op jit(solution)/shard_map/ppermute | solution.py:472
  179.8 30.6 %collective-permute-start.8 = (bf16[1536,768]{1,0:T(8,128)(2,1)}, bf16[1536,768]{1,0:T(8,128)(2,1)}, u32[]{:S(2)}, u32[]{:S(2)}) collective-permute-start(bf16[1536,768]{1,0:T(8,128)(2,1)} %get-tuple-element.147), channel_id=1, source_target_pairs={{0,2},{2,0},{4,6},{6,4},{8,10},{10,8},{12,14},{14,12},{16,18},{18,... | collective-permute-start | bytes 7077896 | tf_op jit(solution)/shard_map/ppermute | solution.py:472
  202.9 12.1 %collective-permute-start.39 = (f32[13,768]{1,0:T(8,128)S(1)}, f32[13,768]{1,0:T(8,128)S(1)}, u32[]{:S(2)}, u32[]{:S(2)}) collective-permute-start(f32[13,768]{1,0:T(8,128)S(1)} %add.541), channel_id=1, source_target_pairs={{0,8},{2,10},{4,12},{6,14},{8,0},{10,2},{12,4},{14,6},{16,24},{18,... | collective-permute-start | bytes 119816 | tf_op jit(solution)/shard_map/ppermute | solution.py:472
  206.7 38.4 %collective-permute-start.52 = (bf16[768,768]{1,0:T(8,128)(2,1)S(1)}, bf16[768,768]{1,0:T(8,128)(2,1)S(1)}, u32[]{:S(2)}, u32[]{:S(2)}) collective-permute-start(bf16[768,768]{1,0:T(8,128)(2,1)S(1)} %get-tuple-element.143), channel_id=1, source_target_pairs={{0,4},{2,6},{4,0},{6,2},{8,12},{10,14},{12,8},{14,10},{16,20},{18,... | collective-permute-start | bytes 3538952 | tf_op jit(solution)/shard_map/ppermute | solution.py:472
  209.9 37.7 %collective-permute-start.42 = (bf16[768,768]{1,0:T(8,128)(2,1)S(1)}, bf16[768,768]{1,0:T(8,128)(2,1)S(1)}, u32[]{:S(2)}, u32[]{:S(2)}) collective-permute-start(bf16[768,768]{1,0:T(8,128)(2,1)S(1)} %get-tuple-element.145), channel_id=1, source_target_pairs={{0,1},{1,0},{2,3},{3,2},{4,5},{5,4},{6,7},{7,6},{8,9},{9,8},{10,11... | collective-permute-start | bytes 3538952 | tf_op jit(solution)/shard_map/ppermute | solution.py:472
  213.2 30.8 %collective-permute-start.17 = (bf16[256,768]{1,0:T(8,128)(2,1)S(1)}, bf16[256,768]{1,0:T(8,128)(2,1)S(1)}, u32[]{:S(2)}, u32[]{:S(2)}) collective-permute-start(bf16[256,768]{1,0:T(8,128)(2,1)S(1)} %get-tuple-element.161), channel_id=1, source_target_pairs={{0,1},{1,0},{2,3},{3,2},{4,5},{5,4},{6,7},{7,6},{8,9},{9,8},{10,11... | collective-permute-start | bytes 1179656 | tf_op jit(solution)/shard_map/ppermute | solution.py:472
  215.0 29.6 %collective-permute-start.9 = (bf16[256,768]{1,0:T(8,128)(2,1)S(1)}, bf16[256,768]{1,0:T(8,128)(2,1)S(1)}, u32[]{:S(2)}, u32[]{:S(2)}) collective-permute-start(bf16[256,768]{1,0:T(8,128)(2,1)S(1)} %get-tuple-element.163), channel_id=1, source_target_pairs={{0,4},{2,6},{4,0},{6,2},{8,12},{10,14},{12,8},{14,10},{16,20},{18,... | collective-permute-start | bytes 1179656 | tf_op jit(solution)/shard_map/ppermute | solution.py:472
  221.0 26.1 %collective-permute-start.26 = (bf16[128,768]{1,0:T(8,128)(2,1)S(1)}, bf16[128,768]{1,0:T(8,128)(2,1)S(1)}, u32[]{:S(2)}, u32[]{:S(2)}) collective-permute-start(bf16[128,768]{1,0:T(8,128)(2,1)S(1)} %get-tuple-element.179), channel_id=1, source_target_pairs={{0,4},{2,6},{4,0},{6,2},{8,12},{10,14},{12,8},{14,10},{16,20},{18,... | collective-permute-start | bytes 589832 | tf_op jit(solution)/shard_map/ppermute | solution.py:472
  245.3 20.2 %collective-permute-start.53 = (bf16[384,768]{1,0:T(8,128)(2,1)S(1)}, bf16[384,768]{1,0:T(8,128)(2,1)S(1)}, u32[]{:S(2)}, u32[]{:S(2)}) collective-permute-start(bf16[384,768]{1,0:T(8,128)(2,1)S(1)} %get-tuple-element.149), channel_id=1, source_target_pairs={{0,1},{1,0},{2,3},{3,2},{4,5},{5,4},{6,7},{7,6},{8,9},{9,8},{10,11... | collective-permute-start | bytes 1769480 | tf_op jit(solution)/shard_map/ppermute | solution.py:472
  247.1 15.7 %collective-permute-start.27 = (bf16[64,768]{1,0:T(8,128)(2,1)S(1)}, bf16[64,768]{1,0:T(8,128)(2,1)S(1)}, u32[]{:S(2)}, u32[]{:S(2)}) collective-permute-start(bf16[64,768]{1,0:T(8,128)(2,1)S(1)} %get-tuple-element.185), channel_id=1, source_target_pairs={{0,1},{1,0},{2,3},{3,2},{4,5},{5,4},{6,7},{7,6},{8,9},{9,8},{10,11... | collective-permute-start | bytes 294920 | tf_op jit(solution)/shard_map/ppermute | solution.py:472
  247.9 22.4 %collective-permute-start.43 = (bf16[384,768]{1,0:T(8,128)(2,1)S(1)}, bf16[384,768]{1,0:T(8,128)(2,1)S(1)}, u32[]{:S(2)}, u32[]{:S(2)}) collective-permute-start(bf16[384,768]{1,0:T(8,128)(2,1)S(1)} %get-tuple-element.151), channel_id=1, source_target_pairs={{0,8},{2,10},{4,12},{6,14},{8,0},{10,2},{12,4},{14,6},{16,24},{18,... | collective-permute-start | bytes 1769480 | tf_op jit(solution)/shard_map/ppermute | solution.py:472
  252.0 15.2 %collective-permute-start.19 = (bf16[64,768]{1,0:T(8,128)(2,1)S(1)}, bf16[64,768]{1,0:T(8,128)(2,1)S(1)}, u32[]{:S(2)}, u32[]{:S(2)}) collective-permute-start(bf16[64,768]{1,0:T(8,128)(2,1)S(1)} %get-tuple-element.187), channel_id=1, source_target_pairs={{0,4},{2,6},{4,0},{6,2},{8,12},{10,14},{12,8},{14,10},{16,20},{18,... | collective-permute-start | bytes 294920 | tf_op jit(solution)/shard_map/ppermute | solution.py:472
  253.5 14.1 %collective-permute-start.11 = (bf16[64,768]{1,0:T(8,128)(2,1)S(1)}, bf16[64,768]{1,0:T(8,128)(2,1)S(1)}, u32[]{:S(2)}, u32[]{:S(2)}) collective-permute-start(bf16[64,768]{1,0:T(8,128)(2,1)S(1)} %get-tuple-element.189), channel_id=1, source_target_pairs={{0,8},{2,10},{4,12},{6,14},{8,0},{10,2},{12,4},{14,6},{16,24},{18,... | collective-permute-start | bytes 294920 | tf_op jit(solution)/shard_map/ppermute | solution.py:472
  262.9 11.7 %collective-permute-start.28 = (bf16[32,768]{1,0:T(8,128)(2,1)S(1)}, bf16[32,768]{1,0:T(8,128)(2,1)S(1)}, u32[]{:S(2)}, u32[]{:S(2)}) collective-permute-start(bf16[32,768]{1,0:T(8,128)(2,1)S(1)} %add_convert_fusion.37), channel_id=1, source_target_pairs={{0,16},{2,18},{4,20},{6,22},{8,24},{10,26},{12,28},{14,30},{16,0},... | collective-permute-start | bytes 147464 | tf_op jit(solution)/shard_map/ppermute | solution.py:472
  267.2 23.8 %collective-permute-start.20 = (bf16[32,768]{1,0:T(8,128)(2,1)S(1)}, bf16[32,768]{1,0:T(8,128)(2,1)S(1)}, u32[]{:S(2)}, u32[]{:S(2)}) collective-permute-start(bf16[32,768]{1,0:T(8,128)(2,1)S(1)} %add_convert_fusion.40), channel_id=1, source_target_pairs={{0,16},{2,18},{4,20},{6,22},{8,24},{10,26},{12,28},{14,30},{16,0},... | collective-permute-start | bytes 147464 | tf_op jit(solution)/shard_map/ppermute | solution.py:472
  267.6 34.8 %collective-permute-start.12 = (bf16[32,768]{1,0:T(8,128)(2,1)S(1)}, bf16[32,768]{1,0:T(8,128)(2,1)S(1)}, u32[]{:S(2)}, u32[]{:S(2)}) collective-permute-start(bf16[32,768]{1,0:T(8,128)(2,1)S(1)} %add_convert_fusion.43), channel_id=1, source_target_pairs={{0,16},{2,18},{4,20},{6,22},{8,24},{10,26},{12,28},{14,30},{16,0},... | collective-permute-start | bytes 147464 | tf_op jit(solution)/shard_map/ppermute | solution.py:472
  274.5 12.2 %collective-permute-start.55 = (bf16[96,768]{1,0:T(8,128)(2,1)S(1)}, bf16[96,768]{1,0:T(8,128)(2,1)S(1)}, u32[]{:S(2)}, u32[]{:S(2)}) collective-permute-start(bf16[96,768]{1,0:T(8,128)(2,1)S(1)} %add_convert_fusion.25), channel_id=1, source_target_pairs={{0,16},{2,18},{4,20},{6,22},{8,24},{10,26},{12,28},{14,30},{16,0},... | collective-permute-start | bytes 442376 | tf_op jit(solution)/shard_map/ppermute | solution.py:472
  275.2 33.9 %collective-permute-start.29 = (bf16[32,768]{1,0:T(8,128)(2,1)S(1)}, bf16[32,768]{1,0:T(8,128)(2,1)S(1)}, u32[]{:S(2)}, u32[]{:S(2)}) collective-permute-start(bf16[32,768]{1,0:T(8,128)(2,1)S(1)} %get-tuple-element.135), channel_id=1, source_target_pairs={{0,16},{2,18},{4,20},{6,22},{8,24},{10,26},{12,28},{14,30},{16,0},... | collective-permute-start | bytes 147464 | tf_op jit(solution)/shard_map/ppermute | solution.py:472
  278.1 12.1 %collective-permute-start.45 = (bf16[96,768]{1,0:T(8,128)(2,1)S(1)}, bf16[96,768]{1,0:T(8,128)(2,1)S(1)}, u32[]{:S(2)}, u32[]{:S(2)}) collective-permute-start(bf16[96,768]{1,0:T(8,128)(2,1)S(1)} %add_convert_fusion.28), channel_id=1, source_target_pairs={{0,16},{2,18},{4,20},{6,22},{8,24},{10,26},{12,28},{14,30},{16,0},... | collective-permute-start | bytes 442376 | tf_op jit(solution)/shard_map/ppermute | solution.py:472
  287.4 9.3 %collective-permute-start.56 = (bf16[96,768]{1,0:T(8,128)(2,1)S(1)}, bf16[96,768]{1,0:T(8,128)(2,1)S(1)}, u32[]{:S(2)}, u32[]{:S(2)}) collective-permute-start(bf16[96,768]{1,0:T(8,128)(2,1)S(1)} %get-tuple-element.129), channel_id=1, source_target_pairs={{0,16},{2,18},{4,20},{6,22},{8,24},{10,26},{12,28},{14,30},{16,0},... | collective-permute-start | bytes 442376 | tf_op jit(solution)/shard_map/ppermute | solution.py:472
  290.9 9.7 %collective-permute-start.46 = (bf16[96,768]{1,0:T(8,128)(2,1)S(1)}, bf16[96,768]{1,0:T(8,128)(2,1)S(1)}, u32[]{:S(2)}, u32[]{:S(2)}) collective-permute-start(bf16[96,768]{1,0:T(8,128)(2,1)S(1)} %get-tuple-element.131), channel_id=1, source_target_pairs={{0,16},{2,18},{4,20},{6,22},{8,24},{10,26},{12,28},{14,30},{16,0},... | collective-permute-start | bytes 442376 | tf_op jit(solution)/shard_map/ppermute | solution.py:472
  291.7 20.6 %collective-permute-start.21 = (bf16[32,768]{1,0:T(8,128)(2,1)S(1)}, bf16[32,768]{1,0:T(8,128)(2,1)S(1)}, u32[]{:S(2)}, u32[]{:S(2)}) collective-permute-start(bf16[32,768]{1,0:T(8,128)(2,1)S(1)} %get-tuple-element.137), channel_id=1, source_target_pairs={{0,16},{2,18},{4,20},{6,22},{8,24},{10,26},{12,28},{14,30},{16,0},... | collective-permute-start | bytes 147464 | tf_op jit(solution)/shard_map/ppermute | solution.py:472
  296.7 10.9 %collective-permute-start.57 = (bf16[192,768]{1,0:T(8,128)(2,1)S(1)}, bf16[192,768]{1,0:T(8,128)(2,1)S(1)}, u32[]{:S(2)}, u32[]{:S(2)}) collective-permute-start(bf16[192,768]{1,0:T(8,128)(2,1)S(1)} %pad_maximum_fusion.15), channel_id=1, source_target_pairs={{0,8},{2,10},{4,12},{6,14},{8,0},{10,2},{12,4},{14,6},{16,24},{18,... | collective-permute-start | bytes 884744 | tf_op jit(solution)/shard_map/ppermute | solution.py:472
  303.1 11.0 %collective-permute-start.13 = (bf16[32,768]{1,0:T(8,128)(2,1)S(1)}, bf16[32,768]{1,0:T(8,128)(2,1)S(1)}, u32[]{:S(2)}, u32[]{:S(2)}) collective-permute-start(bf16[32,768]{1,0:T(8,128)(2,1)S(1)} %get-tuple-element.139), channel_id=1, source_target_pairs={{0,16},{2,18},{4,20},{6,22},{8,24},{10,26},{12,28},{14,30},{16,0},... | collective-permute-start | bytes 147464 | tf_op jit(solution)/shard_map/ppermute | solution.py:472
  307.7 14.5 %collective-permute-start.58 = (bf16[384,768]{1,0:T(8,128)(2,1)S(1)}, bf16[384,768]{1,0:T(8,128)(2,1)S(1)}, u32[]{:S(2)}, u32[]{:S(2)}) collective-permute-start(bf16[384,768]{1,0:T(8,128)(2,1)S(1)} %pad_maximum_fusion.10), channel_id=1, source_target_pairs={{0,1},{1,0},{2,3},{3,2},{4,5},{5,4},{6,7},{7,6},{8,9},{9,8},{10,11... | collective-permute-start | bytes 1769480 | tf_op jit(solution)/shard_map/ppermute | solution.py:472
  309.1 17.8 %collective-permute-start.30 = (bf16[64,768]{1,0:T(8,128)(2,1)S(1)}, bf16[64,768]{1,0:T(8,128)(2,1)S(1)}, u32[]{:S(2)}, u32[]{:S(2)}) collective-permute-start(bf16[64,768]{1,0:T(8,128)(2,1)S(1)} %pad_maximum_fusion.21), channel_id=1, source_target_pairs={{0,1},{1,0},{2,3},{3,2},{4,5},{5,4},{6,7},{7,6},{8,9},{9,8},{10,11... | collective-permute-start | bytes 294920 | tf_op jit(solution)/shard_map/ppermute | solution.py:472
  309.9 15.9 %collective-permute-start.48 = (bf16[384,768]{1,0:T(8,128)(2,1)S(1)}, bf16[384,768]{1,0:T(8,128)(2,1)S(1)}, u32[]{:S(2)}, u32[]{:S(2)}) collective-permute-start(bf16[384,768]{1,0:T(8,128)(2,1)S(1)} %pad_maximum_fusion.9), channel_id=1, source_target_pairs={{0,8},{2,10},{4,12},{6,14},{8,0},{10,2},{12,4},{14,6},{16,24},{18,... | collective-permute-start | bytes 1769480 | tf_op jit(solution)/shard_map/ppermute | solution.py:472
  312.3 16.2 %collective-permute-start.22 = (bf16[64,768]{1,0:T(8,128)(2,1)S(1)}, bf16[64,768]{1,0:T(8,128)(2,1)S(1)}, u32[]{:S(2)}, u32[]{:S(2)}) collective-permute-start(bf16[64,768]{1,0:T(8,128)(2,1)S(1)} %pad_maximum_fusion.20), channel_id=1, source_target_pairs={{0,4},{2,6},{4,0},{6,2},{8,12},{10,14},{12,8},{14,10},{16,20},{18,... | collective-permute-start | bytes 294920 | tf_op jit(solution)/shard_map/ppermute | solution.py:472
  314.1 39.8 %collective-permute-start.14 = (bf16[64,768]{1,0:T(8,128)(2,1)S(1)}, bf16[64,768]{1,0:T(8,128)(2,1)S(1)}, u32[]{:S(2)}, u32[]{:S(2)}) collective-permute-start(bf16[64,768]{1,0:T(8,128)(2,1)S(1)} %pad_maximum_fusion.19), channel_id=1, source_target_pairs={{0,8},{2,10},{4,12},{6,14},{8,0},{10,2},{12,4},{14,6},{16,24},{18,... | collective-permute-start | bytes 294920 | tf_op jit(solution)/shard_map/ppermute | solution.py:472
  322.2 28.9 %collective-permute-start.59 = (bf16[768,768]{1,0:T(8,128)(2,1)S(1)}, bf16[768,768]{1,0:T(8,128)(2,1)S(1)}, u32[]{:S(2)}, u32[]{:S(2)}) collective-permute-start(bf16[768,768]{1,0:T(8,128)(2,1)S(1)} %pad_maximum_fusion.6), channel_id=1, source_target_pairs={{0,4},{2,6},{4,0},{6,2},{8,12},{10,14},{12,8},{14,10},{16,20},{18,... | collective-permute-start | bytes 3538952 | tf_op jit(solution)/shard_map/ppermute | solution.py:472
  325.9 26.3 %collective-permute-start.49 = (bf16[768,768]{1,0:T(8,128)(2,1)S(1)}, bf16[768,768]{1,0:T(8,128)(2,1)S(1)}, u32[]{:S(2)}, u32[]{:S(2)}) collective-permute-start(bf16[768,768]{1,0:T(8,128)(2,1)S(1)} %pad_maximum_fusion.5), channel_id=1, source_target_pairs={{0,1},{1,0},{2,3},{3,2},{4,5},{5,4},{6,7},{7,6},{8,9},{9,8},{10,11... | collective-permute-start | bytes 3538952 | tf_op jit(solution)/shard_map/ppermute | solution.py:472
  326.9 27.2 %collective-permute-start.31 = (bf16[128,768]{1,0:T(8,128)(2,1)S(1)}, bf16[128,768]{1,0:T(8,128)(2,1)S(1)}, u32[]{:S(2)}, u32[]{:S(2)}) collective-permute-start(bf16[128,768]{1,0:T(8,128)(2,1)S(1)} %pad_maximum_fusion.18), channel_id=1, source_target_pairs={{0,4},{2,6},{4,0},{6,2},{8,12},{10,14},{12,8},{14,10},{16,20},{18,... | collective-permute-start | bytes 589832 | tf_op jit(solution)/shard_map/ppermute | solution.py:472
  328.5 26.5 %collective-permute-start.23 = (bf16[128,768]{1,0:T(8,128)(2,1)S(1)}, bf16[128,768]{1,0:T(8,128)(2,1)S(1)}, u32[]{:S(2)}, u32[]{:S(2)}) collective-permute-start(bf16[128,768]{1,0:T(8,128)(2,1)S(1)} %pad_maximum_fusion.17), channel_id=1, source_target_pairs={{0,8},{2,10},{4,12},{6,14},{8,0},{10,2},{12,4},{14,6},{16,24},{18,... | collective-permute-start | bytes 589832 | tf_op jit(solution)/shard_map/ppermute | solution.py:472
  352.2 66.2 %collective-permute-start.60 = (bf16[1536,768]{1,0:T(8,128)(2,1)}, bf16[1536,768]{1,0:T(8,128)(2,1)}, u32[]{:S(2)}, u32[]{:S(2)}) collective-permute-start(bf16[1536,768]{1,0:T(8,128)(2,1)} %constant_dynamic-update-slice_fusion.20.own_ref), channel_id=1, source_target_pairs={{0,2},{2,0},{4,6},{6,4},{8,10},{10,8},{12,14},{14,12},{16,18},{18,... | collective-permute-start | bytes 7077896 | tf_op jit(solution)/shard_map/ppermute | solution.py:472
  353.4 73.1 %collective-permute-start.50 = (bf16[1536,768]{1,0:T(8,128)(2,1)}, bf16[1536,768]{1,0:T(8,128)(2,1)}, u32[]{:S(2)}, u32[]{:S(2)}) collective-permute-start(bf16[1536,768]{1,0:T(8,128)(2,1)} %constant_dynamic-update-slice_fusion.15.own_ref), channel_id=1, source_target_pairs={{0,2},{2,0},{4,6},{6,4},{8,10},{10,8},{12,14},{14,12},{16,18},{18,... | collective-permute-start | bytes 7077896 | tf_op jit(solution)/shard_map/ppermute | solution.py:472
  354.1 10.9 %collective-permute-start.32 = (bf16[256,768]{1,0:T(8,128)(2,1)S(1)}, bf16[256,768]{1,0:T(8,128)(2,1)S(1)}, u32[]{:S(2)}, u32[]{:S(2)}) collective-permute-start(bf16[256,768]{1,0:T(8,128)(2,1)S(1)} %pad_maximum_fusion.13), channel_id=1, source_target_pairs={{0,8},{2,10},{4,12},{6,14},{8,0},{10,2},{12,4},{14,6},{16,24},{18,... | collective-permute-start | bytes 1179656 | tf_op jit(solution)/shard_map/ppermute | solution.py:472
  355.1 15.1 %collective-permute-start.24 = (bf16[256,768]{1,0:T(8,128)(2,1)S(1)}, bf16[256,768]{1,0:T(8,128)(2,1)S(1)}, u32[]{:S(2)}, u32[]{:S(2)}) collective-permute-start(bf16[256,768]{1,0:T(8,128)(2,1)S(1)} %pad_maximum_fusion.12), channel_id=1, source_target_pairs={{0,1},{1,0},{2,3},{3,2},{4,5},{5,4},{6,7},{7,6},{8,9},{9,8},{10,11... | collective-permute-start | bytes 1179656 | tf_op jit(solution)/shard_map/ppermute | solution.py:472
  361.7 25.8 %collective-permute-start.7 = (bf16[2,256,768]{2,1,0:T(8,128)(2,1)S(1)}, bf16[2,256,768]{2,1,0:T(8,128)(2,1)S(1)}, u32[]{:S(2)}, u32[]{:S(2)}) collective-permute-start(bf16[2,256,768]{2,1,0:T(8,128)(2,1)S(1)} %fusion.2), channel_id=1, source_target_pairs={{0,1},{1,0},{2,3},{3,2},{4,5},{5,4},{6,7},{7,6},{8,9},{9,8},{10,11... | collective-permute-start | bytes 2359304 | tf_op jit(solution)/shard_map/ppermute | solution.py:465
  365.1 37.8 %collective-permute-start.6 = (bf16[2,256,768]{2,1,0:T(8,128)(2,1)S(1)}, bf16[2,256,768]{2,1,0:T(8,128)(2,1)S(1)}, u32[]{:S(2)}, u32[]{:S(2)}) collective-permute-start(bf16[2,256,768]{2,1,0:T(8,128)(2,1)S(1)} %get-tuple-element.164), channel_id=1, source_target_pairs={{0,1},{1,0},{2,3},{3,2},{4,5},{5,4},{6,7},{7,6},{8,9},{9,8},{10,11... | collective-permute-start | bytes 2359304 | tf_op jit(solution)/shard_map/ppermute | solution.py:465
  387.5 23.0 %collective-permute-start.35 = (bf16[512,768]{1,0:T(8,128)(2,1)}, bf16[512,768]{1,0:T(8,128)(2,1)}, u32[]{:S(2)}, u32[]{:S(2)}) collective-permute-start(bf16[512,768]{1,0:T(8,128)(2,1)} %constant_dynamic-update-slice_fusion.10.refs_2_), channel_id=1, source_target_pairs={{0,2},{2,0},{4,6},{6,4},{8,10},{10,8},{12,14},{14,12},{16,18},{18,... | collective-permute-start | bytes 2359304 | tf_op jit(solution)/shard_map/ppermute | solution.py:472
  387.5 23.0 %collective-permute-start.34 = (bf16[512,768]{1,0:T(8,128)(2,1)}, bf16[512,768]{1,0:T(8,128)(2,1)}, u32[]{:S(2)}, u32[]{:S(2)}) collective-permute-start(bf16[512,768]{1,0:T(8,128)(2,1)} %constant_dynamic-update-slice_fusion.5.refs_1_), channel_id=1, source_target_pairs={{0,2},{2,0},{4,6},{6,4},{8,10},{10,8},{12,14},{14,12},{16,18},{18,... | collective-permute-start | bytes 2359304 | tf_op jit(solution)/shard_map/ppermute | solution.py:472
  (34 other events, 248.3 us)

commit v3 on v2

v3 whole, which is shorter than its diff:
```python
import functools

import jax
import jax.numpy as jnp
from jax import lax
from jax.experimental import pallas as pl
from jax.experimental.pallas import tpu as pltpu
from jax.sharding import PartitionSpec as P

HEAD_DIM = 64
EPSILON = 1e-05
NEGATIVE = -1e30
SCORE_SCALE = 0.125
LOW = jnp.bfloat16
WIDE = jnp.float32
VMEM_LIMIT = 56 * 1024 * 1024
HIDDEN_STEP = 512
TILE = 256
ROWS = 32
ROWS_NORM = 16
ANY = pl.BlockSpec(memory_space=pl.ANY)
IN_VMEM = pl.BlockSpec(memory_space=pltpu.VMEM)
IN_SMEM = pl.BlockSpec(memory_space=pltpu.SMEM)

ERF_P = 0.3275911
ERF_C = (0.254829592, -0.284496736, 1.421413741, -1.453152027, 1.061405429)
ROOT_HALF = 0.7071067811865476
DENSITY = 0.3989422804014327


def nn(left, right):
    return jnp.dot(left, right, preferred_element_type=WIDE)


def nt(left, right):
    return lax.dot_general(
        left, right, (((1,), (1,)), ((), ())), preferred_element_type=WIDE
    )


def tn(left, right):
    return lax.dot_general(
        left, right, (((0,), (0,)), ((), ())), preferred_element_type=WIDE
    )


def gelu_pair(hidden):
    tail_exp = jnp.exp(hidden * hidden * -0.5)
    slow = 1.0 + (ERF_P * ROOT_HALF) * jnp.abs(hidden)
    t = pl.reciprocal(slow, approx=True)
    t = t * (2.0 - slow * t)
    c1, c2, c3, c4, c5 = (0.5 * c for c in ERF_C)
    tail = ((((c5 * t + c4) * t + c3) * t + c2) * t + c1) * t * tail_exp
    below = jnp.where(hidden >= 0.0, 1.0 - tail, tail)
    return hidden * below, below + hidden * (DENSITY * tail_exp)


def lane_half(half):
    lane = lax.broadcasted_iota(jnp.int32, (1, 2 * HEAD_DIM), 1)
    inside = (lane < HEAD_DIM) if half == 0 else (lane >= HEAD_DIM)
    return inside.astype(WIDE).astype(LOW)


def fill_bias(bias_ref, seg_row, mark_col):
    length = bias_ref.shape[0]
    key_place = lax.broadcasted_iota(jnp.int32, (length, length), 0)
    query_place = lax.broadcasted_iota(jnp.int32, (length, length), 1)
    visible = (mark_col == seg_row) | (key_place == query_place)
    bias_ref[...] = jnp.where(visible, 0.0, NEGATIVE)


def total(rows_weight, values):
    per_row = jnp.sum(values * values, axis=1, keepdims=True) * rows_weight
    return jnp.sum(per_row, axis=0, keepdims=True)


def column(row):
    return jnp.broadcast_to(row.astype(WIDE), (8, row.shape[1])).T[:, 0:1]


VECTORS = ("b_query", "b_value", "b_out", "gain_one", "shift_one", "b_down", "gain_two", "shift_two")


def vector(ref, name):
    place = VECTORS.index(name)
    return ref[place : place + 1, :]


def attend_kernel(
    x_ref, seg_ref, mark_ref, vectors_ref, wq_ref, wk_ref, wv_ref, wo_ref,
    q_ref, k_ref, v_ref, ctx_ref, lse_ref, mid_ref, norm_ref, rstd_ref, stat_ref,
    wq_s, wk_s, wv_s, wo_s, q_s, k_s, v_s, bias_s, score_s, chance_s, weight_s, in_sems, out_sems,
    *, slot,
):
    loads = [
        pltpu.make_async_copy(a, b, in_sems.at[n])
        for n, (a, b) in enumerate(
            ((wk_ref, wk_s), (wq_ref, wq_s), (wv_ref, wv_s), (wo_ref, wo_s))
        )
    ]
    for load in loads:
        load.start()
    stores = [
        pltpu.make_async_copy(a, b, out_sems.at[n])
        for n, (a, b) in enumerate(((k_s, k_ref), (q_s, q_ref), (v_s, v_ref)))
    ]
    mark_col = column(mark_ref[slot : slot + 1, :])
    weight_s[...] = (mark_col >= 0).astype(WIDE)
    fill_bias(bias_s, seg_ref[slot : slot + 1, :].astype(WIDE), mark_col)
    length, model = x_ref.shape
    heads = model // HEAD_DIM
    width = 2 * HEAD_DIM
    loads[0].wait()
    k_s[...] = nn(x_ref[...], wk_s[...]).astype(LOW)
    stores[0].start()
    loads[1].wait()
    q_s[...] = ((nn(x_ref[...], wq_s[...]) + vector(vectors_ref, "b_query")) * SCORE_SCALE).astype(LOW)
    stores[1].start()
    loads[2].wait()
    v_s[...] = (nn(x_ref[...], wv_s[...]) + vector(vectors_ref, "b_value")).astype(LOW)
    stores[2].start()

    def lanes(head):
        return pl.ds(head // 2 * width, width)

    def scores(head):
        keys = k_s[:, lanes(head)] * lane_half(head % 2)
        score_s[head % 2] = nt(keys, q_s[:, lanes(head)])

    def soften(head):
        here, chance = score_s.at[head % 2], chance_s.at[head % 2]
        top = jnp.full((8, length), NEGATIVE, WIDE)
        for row in range(0, length, ROWS):
            block = here[row : row + ROWS, :] + bias_s[row : row + ROWS, :]
            here[row : row + ROWS, :] = block
            top = jnp.maximum(top, jnp.max(block.reshape(-1, 8, length), axis=0))
        top = jnp.max(top, axis=0, keepdims=True)
        amount = jnp.zeros((8, length), WIDE)
        for row in range(0, length, ROWS):
            block = jnp.exp(here[row : row + ROWS, :] - top)
            chance[row : row + ROWS, :] = block.astype(LOW)
            amount = amount + jnp.sum(block.reshape(-1, 8, length), axis=0)
        amount = jnp.sum(amount, axis=0, keepdims=True)
        lse_ref[head : head + 1, :] = top + jnp.log(amount)
        return 1.0 / amount

    def combine(head, share, turned):
        part = turned[head % 2 * HEAD_DIM : (head % 2 + 1) * HEAD_DIM]
        summed = nn(part, chance_s[head % 2]) * share
        ctx_ref[head * HEAD_DIM : (head + 1) * HEAD_DIM, :] = summed.astype(LOW)

    scores(0)
    waiting = None
    for head in range(heads):
        share = soften(head)
        if head % 2 == 0:
            turned = v_s[:, lanes(head)].T
        if head + 1 < heads:
            scores(head + 1)
        if waiting is not None:
            combine(*waiting)
        waiting = (head, share, turned)
    combine(*waiting)
    loads[3].wait()
    attention_all = tn(ctx_ref[...], wo_s[...])
    bias, gain, shift = (vector(vectors_ref, n) for n in ("b_out", "gain_one", "shift_one"))
    stats = [jnp.zeros((1, 1), WIDE) for _ in range(2)]
    for row in range(0, length, ROWS_NORM):
        at = pl.ds(row, ROWS_NORM)
        attention = attention_all[row : row + ROWS_NORM] + bias
        rows = x_ref[at, :].astype(WIDE)
        total_in = rows + attention
        center = total_in - jnp.mean(total_in, axis=1, keepdims=True)
        rstd = lax.rsqrt(jnp.mean(center * center, axis=1, keepdims=True) + EPSILON)
        normal = center * rstd
        mid_ref[at, :] = normal * gain + shift
        norm_ref[at, :] = normal.astype(LOW)
        rstd_ref[at, :] = rstd
        row_weight = weight_s[at, :]
        stats[0] = stats[0] + total(row_weight, rows)
        stats[1] = stats[1] + total(row_weight, attention)
    stat_ref[...] = jnp.concatenate(
        [jnp.broadcast_to(stat, (1, 128)) for stat in stats] + [jnp.zeros((6, 128), WIDE)], axis=0
    )
    for store in stores:
        store.wait()


def cost(flops):
    return pl.CostEstimate(flops=flops, transcendentals=0, bytes_accessed=0)


def ignoring(kernel, inputs, extra):
    def wrapped(*refs):
        return kernel(*refs[:inputs], *refs[inputs + extra :])

    return wrapped


def whole(shape):
    return pl.BlockSpec(shape, lambda *_: (0,) * len(shape), pipeline_mode=pl.Buffered(1))


def attend(slot, x, segs, marks, vectors, wq, wk, wv, wo):
    length, width = x.shape
    heads = width // HEAD_DIM
    lse_rows = heads + (-heads) % 8
    shapes = (
        jax.ShapeDtypeStruct((length, width), LOW),
        jax.ShapeDtypeStruct((length, width), LOW),
        jax.ShapeDtypeStruct((length, width), LOW),
        jax.ShapeDtypeStruct((width, length), LOW),
        jax.ShapeDtypeStruct((lse_rows, length), WIDE),
        jax.ShapeDtypeStruct((length, width), WIDE),
        jax.ShapeDtypeStruct((length, width), LOW),
        jax.ShapeDtypeStruct((length, 1), WIDE),
        jax.ShapeDtypeStruct((8, 128), WIDE),
    )
    args = (x, segs, marks, vectors, wq, wk, wv, wo)
    weight = pltpu.VMEM((width, width), LOW)
    tokens = pltpu.VMEM((length, width), LOW)
    return pl.pallas_call(
        functools.partial(attend_kernel, slot=slot),
        out_shape=shapes,
        in_specs=[IN_VMEM] * 4 + [ANY] * 4,
        out_specs=(ANY,) * 3 + (IN_VMEM,) * 6,
        scratch_shapes=[weight] * 4 + [tokens] * 3 + [
            pltpu.VMEM((length, length), WIDE),
            pltpu.VMEM((2, length, length), WIDE),
            pltpu.VMEM((2, length, length), LOW),
            pltpu.VMEM((length, 1), WIDE),
            pltpu.SemaphoreType.DMA((4,)),
            pltpu.SemaphoreType.DMA((3,)),
        ],
        compiler_params=pltpu.CompilerParams(vmem_limit_bytes=VMEM_LIMIT),
        cost_estimate=cost(0),
        name="attend",
    )(*args)


def lane_split(core, half, length):
    return [
        pl.multiple_of(start * half, length) for start in (1 - core, core)
    ]


def norm_back(grad, normal, rstd, gain):
    pulled = grad * gain
    return rstd * (
        pulled
        - jnp.mean(pulled, axis=1, keepdims=True)
        - normal * jnp.mean(pulled * normal, axis=1, keepdims=True)
    )


def row_total(values):
    return jnp.sum(values, axis=0, keepdims=True)


def feed_kernel(
    place_ref, mid0_ref, mid1_ref, cot_ref, mark_ref, bu_ref, vectors_ref, wu_ref, wd_ref,
    slope_ref, low_ref, result_ref, grad_ref, grad_low_ref, send_ref, keep_ref, sums_ref, stat_ref,
    mid_s, cot_s, wu_s, wd_s, act_s, slope_s, low_s, result_s, grad_s, grad_low_s, out_s,
    feed_s, weight_s, in_sems, up_sems, down_sems, tile_sems, out_sems,
):
    length, width = mid0_ref.shape
    rows = cot_ref.shape[0]
    hidden = wu_ref.shape[1]
    half = hidden // 2
    chunks = hidden // HIDDEN_STEP
    tile = TILE
    core = place_ref[0]
    bases = lane_split(core, half, HIDDEN_STEP)

    def place_of(chunk):
        part, inside = divmod(chunk * HIDDEN_STEP, half)
        return pl.ds(pl.multiple_of(bases[part] + inside, HIDDEN_STEP), HIDDEN_STEP)

    def own(chunk):
        return pl.ds(chunk * HIDDEN_STEP, HIDDEN_STEP)

    first_in = pltpu.make_async_copy(mid0_ref, mid_s.at[pl.ds(0, length)], in_sems.at[0])
    second_in = pltpu.make_async_copy(mid1_ref, mid_s.at[pl.ds(length, length)], in_sems.at[1])
    cot_in = pltpu.make_async_copy(cot_ref, cot_s, in_sems.at[2])
    ups = [
        pltpu.make_async_copy(wu_ref.at[:, place_of(c)], wu_s.at[:, own(c)], up_sems.at[c])
        for c in range(chunks)
    ]
    downs = [
        pltpu.make_async_copy(wd_ref.at[place_of(c), :], wd_s.at[own(c), :], down_sems.at[c])
        for c in range(chunks)
    ]
    first_in.start()
    for chunk in range(chunks):
        ups[chunk].start()
        downs[chunk].start()
    cot_in.start()
    second_in.start()
    sums_ref[...] = jnp.zeros_like(sums_ref)
    stat_ref[...] = jnp.zeros_like(stat_ref)
    for slot in range(mark_ref.shape[0]):
        mark_col = column(mark_ref[slot : slot + 1, :])
        weight_s[pl.ds(slot * length, length), :] = (mark_col >= 0).astype(WIDE)

    def tile_copies(index):
        spot = pl.ds(pl.multiple_of(index * tile, tile), tile)
        pairs = (
            (slope_s, slope_ref), (low_s, low_ref), (result_s, result_ref), (grad_s, grad_ref),
            (grad_low_s, grad_low_ref),
        )
        return [
            pltpu.make_async_copy(a.at[spot, :], b.at[spot, :], tile_sems.at[n, index])
            for n, (a, b) in enumerate(pairs)
        ]

    def inside(index, row, count=ROWS):
        return pl.ds(pl.multiple_of(index * tile + row, count), count)

    def work(index, opening):
        spot = pl.ds(pl.multiple_of(index * tile, tile), tile)
        for row in range(0, tile, ROWS):
            low_s[inside(index, row), :] = mid_s[inside(index, row), :].astype(LOW)
        middle_low = low_s[spot, :]

        def up(chunk):
            if opening:
                ups[chunk].wait()
            return nn(middle_low, wu_s[:, own(chunk)])

        def down(chunk, feed):
            if opening:
                downs[chunk].wait()
            more = nn(act_s[spot, own(chunk)], wd_s[own(chunk), :])
            return more if feed is None else feed + more

        feed = None
        ahead = up(0)
        for chunk in range(chunks):
            bias = bu_ref[:, place_of(chunk)]
            for row in range(0, tile, ROWS):
                active, slope = gelu_pair(ahead[row : row + ROWS] + bias)
                act_s[inside(index, row), own(chunk)] = active.astype(LOW)
                slope_s[inside(index, row), own(chunk)] = slope.astype(LOW)
            if chunk + 1 < chunks:
                ahead = up(chunk + 1)
            if chunk > 0:
                feed = down(chunk - 1, feed)
        feed_s[...] = down(chunks - 1, feed)

    def norm(index):
        gain, shift, bias = (vector(vectors_ref, n) for n in ("gain_two", "shift_two", "b_down"))
        sums = [jnp.zeros((1, width), WIDE) for _ in range(3)]
        stats = [jnp.zeros((1, 1), WIDE) for _ in range(2)]
        for row in range(0, tile, ROWS_NORM):
            here = inside(index, row, ROWS_NORM)
            feed_here = feed_s[row : row + ROWS_NORM, :] + bias
            total_in = mid_s[here, :] + feed_here
            center = total_in - jnp.mean(total_in, axis=1, keepdims=True)
            rstd = lax.rsqrt(jnp.mean(center * center, axis=1, keepdims=True) + EPSILON)
            normal = center * rstd
            result = normal * gain + shift
            result_s[here, :] = result.astype(LOW)
            weight = weight_s[here, :]
            grad_result = cot_s[here, :].astype(WIDE) * weight
            grad = norm_back(grad_result, normal, rstd, gain)
            grad_s[here, :] = grad
            grad_low = grad.astype(LOW)
            grad_low_s[here, :] = grad_low
            sums[0] = sums[0] + row_total(grad_result * normal)
            sums[1] = sums[1] + row_total(grad_result)
            sums[2] = sums[2] + row_total(grad_low.astype(WIDE))
            stats[0] = stats[0] + total(weight, feed_here)
            stats[1] = stats[1] + total(weight, result)
        for copy in tile_copies(index):
            copy.start()
        for n in range(3):
            sums_ref[n : n + 1, :] += sums[n]
        for n in range(2):
            stat_ref[n : n + 1, :] += jnp.broadcast_to(stats[n], (1, 128))

    first_in.wait()
    work(0, True)
    second_in.wait()
    cot_in.wait()

    def turn(index, carried):
        norm(index - 1)
        work(index, False)
        return carried

    lax.fori_loop(1, rows // tile, turn, 0)
    norm(rows // tile - 1)
    outer(act_s, grad_low_s, out_s, send_ref, keep_ref, out_sems)
    for index in range(rows // tile):
        for copy in tile_copies(index):
            copy.wait()


def outer(left_s, right_s, out_s, send_ref, keep_ref, sems):
    half = left_s.shape[1] // 2
    steps = left_s.shape[1] // HIDDEN_STEP
    copies = []
    for step in range(steps):
        part, inside = divmod(step * HIDDEN_STEP, half)
        spot = pl.ds(step * HIDDEN_STEP, HIDDEN_STEP)
        out_s[spot, :] = tn(left_s[:, spot], right_s[...]).astype(LOW)
        target = (send_ref, keep_ref)[part].at[pl.ds(inside, HIDDEN_STEP), :]
        copies.append(pltpu.make_async_copy(out_s.at[spot, :], target, sems.at[step]))
        copies[-1].start()
    for copy in copies:
        copy.wait()


def feed_forward(place, mids, cot, marks, wu, bu, wd, vectors):
    length, width = mids[0].shape
    rows = cot.shape[0]
    hidden = wu.shape[1]
    half = hidden // 2
    chunks = hidden // HIDDEN_STEP
    shapes = (
        jax.ShapeDtypeStruct((rows, hidden), LOW),
        jax.ShapeDtypeStruct((rows, width), LOW),
        jax.ShapeDtypeStruct((rows, width), LOW),
        jax.ShapeDtypeStruct((rows, width), WIDE),
        jax.ShapeDtypeStruct((rows, width), LOW),
        jax.ShapeDtypeStruct((half, width), LOW),
        jax.ShapeDtypeStruct((half, width), LOW),
        jax.ShapeDtypeStruct((8, width), WIDE),
        jax.ShapeDtypeStruct((8, 128), WIDE),
    )
    return pl.pallas_call(
        feed_kernel,
        out_shape=shapes,
        in_specs=[IN_SMEM] + [ANY] * 3 + [IN_VMEM] * 3 + [ANY] * 2,
        out_specs=(ANY,) * 7 + (IN_VMEM,) * 2,
        scratch_shapes=[
            pltpu.VMEM((rows, width), WIDE),
            pltpu.VMEM((rows, width), LOW),
            pltpu.VMEM((width, hidden), LOW),
            pltpu.VMEM((hidden, width), LOW),
            pltpu.VMEM((rows, hidden), LOW),
            pltpu.VMEM((rows, hidden), LOW),
            pltpu.VMEM((rows, width), LOW),
            pltpu.VMEM((rows, width), LOW),
            pltpu.VMEM((rows, width), WIDE),
            pltpu.VMEM((rows, width), LOW),
            pltpu.VMEM((hidden, width), LOW),
            pltpu.VMEM((TILE, width), WIDE),
            pltpu.VMEM((rows, 1), WIDE),
            pltpu.SemaphoreType.DMA((3,)),
            pltpu.SemaphoreType.DMA((chunks,)),
            pltpu.SemaphoreType.DMA((chunks,)),
            pltpu.SemaphoreType.DMA((5, rows // TILE)),
            pltpu.SemaphoreType.DMA((chunks,)),
        ],
        compiler_params=pltpu.CompilerParams(vmem_limit_bytes=VMEM_LIMIT),
        cost_estimate=cost(0),
        name="feed_forward",
    )(place, mids[0], mids[1], cot, marks, bu, vectors, wu, wd)


def feed_back_kernel(
    place_ref, grad_low_ref, grad_ref, slope_ref, norm0_ref, norm1_ref, low_ref, wu_ref, wd_ref,
    wo_ref, rstd0_ref, rstd1_ref, vectors_ref,
    grad_one_ref, attn_ref, ctx_ref, send_ref, keep_ref, up_sums_ref, sums_ref,
    grad_low_s, grad_s, slope_s, norm_s, low_s, wu_s, wd_s, wo_s, rstd_s, grad_one_s, attn_s,
    ctx_s, out_s, middle_s,
    in_sems, slope_sems, up_sems, down_sems, tile_sems, out_sems, ctx_sems,
):
    length = norm0_ref.shape[0]
    rows, width = grad_low_ref.shape
    hidden = wu_ref.shape[1]
    half = hidden // 2
    chunks = hidden // HIDDEN_STEP
    tile = TILE
    core = place_ref[0]
    bases = lane_split(core, half, HIDDEN_STEP)

    def place_of(chunk):
        part, inside = divmod(chunk * HIDDEN_STEP, half)
        return pl.ds(pl.multiple_of(bases[part] + inside, HIDDEN_STEP), HIDDEN_STEP)

    def own(chunk):
        return pl.ds(chunk * HIDDEN_STEP, HIDDEN_STEP)

    def spot_of(index):
        return pl.ds(pl.multiple_of(index * tile, tile), tile)

    slopes = [
        pltpu.make_async_copy(
            slope_ref.at[spot_of(i), :], slope_s.at[spot_of(i), :], slope_sems.at[i]
        )
        for i in range(rows // tile)
    ]
    ups = [
        pltpu.make_async_copy(wu_ref.at[:, place_of(c)], wu_s.at[:, own(c)], up_sems.at[c])
        for c in range(chunks)
    ]
    downs = [
        pltpu.make_async_copy(wd_ref.at[place_of(c), :], wd_s.at[own(c), :], down_sems.at[c])
        for c in range(chunks)
    ]
    others = [
        pltpu.make_async_copy(a, b, in_sems.at[n])
        for n, (a, b) in enumerate(
            (
                (grad_low_ref, grad_low_s),
                (grad_ref, grad_s),
                (norm0_ref, norm_s.at[pl.ds(0, length)]),
                (norm1_ref, norm_s.at[pl.ds(length, length)]),
                (wo_ref, wo_s),
                (low_ref, low_s),
            )
        )
    ]
    others[0].start()
    downs[0].start()
    slopes[0].start()
    ups[0].start()
    for chunk in range(1, chunks):
        downs[chunk].start()
        ups[chunk].start()
    for copy in others[1:5] + slopes[1:] + others[5:]:
        copy.start()
    rstd_s[pl.ds(0, length), :] = rstd0_ref[...]
    rstd_s[pl.ds(length, length), :] = rstd1_ref[...]
    sums_ref[...] = jnp.zeros_like(sums_ref)
    up_sums_ref[...] = jnp.zeros_like(up_sums_ref)

    def tile_copies(index):
        spot = spot_of(index)
        pairs = ((grad_one_s, grad_one_ref), (attn_s, attn_ref))
        return [
            pltpu.make_async_copy(a.at[spot, :], b.at[spot, :], tile_sems.at[n, index])
            for n, (a, b) in enumerate(pairs)
        ]

    def inside(index, row, count=ROWS):
        return pl.ds(pl.multiple_of(index * tile + row, count), count)

    def work(index, opening):
        spot = spot_of(index)
        grad_low = grad_low_s[spot, :]

        def back(chunk):
            if opening:
                downs[chunk].wait()
            return nt(grad_low, wd_s[own(chunk), :])

        def forth(chunk, grad):
            if opening:
                ups[chunk].wait()
            more = nt(slope_s[spot, own(chunk)], wu_s[:, own(chunk)])
            return more if grad is None else grad + more

        ahead = back(0)
        if opening:
            slopes[0].wait()
        grad_middle = None
        for chunk in range(chunks):
            sums = jnp.zeros((8, HIDDEN_STEP), WIDE)
            for row in range(0, tile, ROWS):
                at = inside(index, row)
                slope = slope_s[at, own(chunk)].astype(WIDE)
                grad_hidden = (ahead[row : row + ROWS] * slope).astype(LOW)
                slope_s[at, own(chunk)] = grad_hidden
                sums = sums + jnp.sum(
                    grad_hidden.astype(WIDE).reshape(-1, 8, HIDDEN_STEP), axis=0
                )
            up_sums_ref[:, place_of(chunk)] += sums
            if chunk + 1 < chunks:
                ahead = back(chunk + 1)
            if chunk > 0:
                grad_middle = forth(chunk - 1, grad_middle)
        middle_s[...] = forth(chunks - 1, grad_middle)

    def norm(index):
        gain = vector(vectors_ref, "gain_one")
        sums = [jnp.zeros((1, width), WIDE) for _ in range(3)]
        for row in range(0, tile, ROWS_NORM):
            at = inside(index, row, ROWS_NORM)
            grad = middle_s[row : row + ROWS_NORM, :] + grad_s[at, :]
            normal = norm_s[at, :].astype(WIDE)
            grad_one = norm_back(grad, normal, rstd_s[at, :], gain)
            grad_one_s[at, :] = grad_one
            attn = grad_one.astype(LOW)
            attn_s[at, :] = attn
            sums[0] = sums[0] + row_total(grad * normal)
            sums[1] = sums[1] + row_total(grad)
            sums[2] = sums[2] + row_total(attn.astype(WIDE))
        for copy in tile_copies(index):
            copy.start()
        for n in range(3):
            sums_ref[n : n + 1, :] += sums[n]

    def project(index):
        spot = spot_of(index)
        turned = nt(wo_s[...], attn_s[spot, :]).astype(LOW)
        slot, inner = divmod(index * tile, length)
        ctx_s[slot, :, inner : inner + tile] = turned
        copy = pltpu.make_async_copy(
            ctx_s.at[slot, :, pl.ds(inner, tile)], ctx_ref.at[slot, :, pl.ds(inner, tile)],
            ctx_sems.at[index],
        )
        copy.start()
        return copy

    others[0].wait()
    work(0, True)
    for copy in slopes[1:] + others[1:5]:
        copy.wait()

    def turn(index, carried):
        norm(index - 1)
        work(index, False)
        return carried

    lax.fori_loop(1, rows // tile, turn, 0)
    norm(rows // tile - 1)
    copies = [project(index) for index in range(rows // tile)]
    others[5].wait()
    outer(slope_s, low_s, out_s, send_ref, keep_ref, out_sems)
    for copy in copies:
        copy.wait()
    for index in range(rows // tile):
        for copy in tile_copies(index):
            copy.wait()


def feed_back(place, grad_low, grad, slope, norms, rstds, mid_low, wu, wd, wo, vectors, *earlier):
    rows, width = grad.shape
    length = norms[0].shape[0]
    hidden = wu.shape[1]
    half = hidden // 2
    chunks = hidden // HIDDEN_STEP
    shapes = (
        jax.ShapeDtypeStruct((rows, width), WIDE),
        jax.ShapeDtypeStruct((rows, width), LOW),
        jax.ShapeDtypeStruct((rows // length, width, length), LOW),
        jax.ShapeDtypeStruct((half, width), LOW),
        jax.ShapeDtypeStruct((half, width), LOW),
        jax.ShapeDtypeStruct((8, hidden), WIDE),
        jax.ShapeDtypeStruct((8, width), WIDE),
    )
    return pl.pallas_call(
        ignoring(feed_back_kernel, 13, len(earlier)),
        out_shape=shapes,
        in_specs=[IN_SMEM] + [ANY] * 9 + [IN_VMEM] * 3 + [ANY] * len(earlier),
        out_specs=(ANY,) * 5 + (IN_VMEM,) * 2,
        scratch_shapes=[
            pltpu.VMEM((rows, width), LOW),
            pltpu.VMEM((rows, width), WIDE),
            pltpu.VMEM((rows, hidden), LOW),
            pltpu.VMEM((rows, width), LOW),
            pltpu.VMEM((rows, width), LOW),
            pltpu.VMEM((width, hidden), LOW),
            pltpu.VMEM((hidden, width), LOW),
            pltpu.VMEM((width, width), LOW),
            pltpu.VMEM((rows, 1), WIDE),
            pltpu.VMEM((rows, width), WIDE),
            pltpu.VMEM((rows, width), LOW),
            pltpu.VMEM((rows // length, width, length), LOW),
            pltpu.VMEM((hidden, width), LOW),
            pltpu.VMEM((TILE, width), WIDE),
            pltpu.SemaphoreType.DMA((6,)),
            pltpu.SemaphoreType.DMA((rows // TILE,)),
            pltpu.SemaphoreType.DMA((chunks,)),
            pltpu.SemaphoreType.DMA((chunks,)),
            pltpu.SemaphoreType.DMA((2, rows // TILE)),
            pltpu.SemaphoreType.DMA((chunks,)),
            pltpu.SemaphoreType.DMA((rows // TILE,)),
        ],
        compiler_params=pltpu.CompilerParams(vmem_limit_bytes=VMEM_LIMIT),
        cost_estimate=cost(0),
        name="feed_back",
    )(
        place, grad_low, grad, slope, norms[0], norms[1], mid_low, wu, wd, wo, rstds[0], rstds[1],
        vectors, *earlier,
    )


def attend_back_kernel(
    seg_ref, mark_ref, lse_ref, q_ref, k_ref, v_ref, ctx_ref, grad_ctx_ref, grad_one_ref, wq_ref,
    wk_ref, wv_ref,
    dq_ref, dk_ref, dv_ref, grad_in_ref, sums_ref,
    q_s, k_s, v_s, ctx_s, grad_ctx_s, grad_one_s, wq_s, wk_s, wv_s, bias_s, score_s, pull_s,
    chance_s, grad_s, in_sems, *, slot,
):
    length, model = q_ref.shape
    heads = model // HEAD_DIM
    width = 2 * HEAD_DIM
    loads = [
        pltpu.make_async_copy(a, b, in_sems.at[n])
        for n, (a, b) in enumerate(
            (
                (k_ref, k_s), (q_ref, q_s), (v_ref, v_s), (grad_ctx_ref.at[slot], grad_ctx_s),
                (ctx_ref, ctx_s), (wq_ref, wq_s), (wk_ref, wk_s), (wv_ref, wv_s),
                (grad_one_ref.at[pl.ds(slot * length, length), :], grad_one_s),
            )
        )
    ]
    for load in loads:
        load.start()
    mark_col = column(mark_ref[slot : slot + 1, :])
    fill_bias(bias_s, seg_ref[slot : slot + 1, :].astype(WIDE), mark_col)

    def lanes(head):
        return pl.ds(head // 2 * width, width)

    def rows_of(head):
        return pl.ds(head * HEAD_DIM, HEAD_DIM)

    def products(head):
        score_s[head % 2] = nt(k_s[:, lanes(head)] * lane_half(head % 2), q_s[:, lanes(head)])
        values = v_s[:, lanes(head)] * lane_half(head % 2)
        pull_s[head % 2] = nn(values, grad_ctx_s[lanes(head), :])

    def soften(head):
        score, pull = score_s.at[head % 2], pull_s.at[head % 2]
        chance, grad = chance_s.at[head % 2], grad_s.at[head % 2]
        shared = grad_ctx_s[rows_of(head), :].astype(WIDE) * ctx_s[rows_of(head), :].astype(WIDE)
        delta = jnp.sum(shared, axis=0, keepdims=True)
        lse = lse_ref[head : head + 1, :]
        for row in range(0, length, ROWS):
            at = slice(row, row + ROWS)
            block = jnp.exp(score[at, :] + bias_s[at, :] - lse)
            chance[at, :] = block.astype(LOW)
            grad[at, :] = (block * (pull[at, :] - delta)).astype(LOW)

    def combine(head, turned):
        part_v = nt(chance_s[head % 2], grad_ctx_s[lanes(head), :])
        part_k = nn(grad_s[head % 2], q_s[:, lanes(head)])
        part = turned[head % 2 * HEAD_DIM : (head % 2 + 1) * HEAD_DIM]
        return part_v, part_k, nn(part, grad_s[head % 2])

    def keep(head, one, two):
        first = lax.broadcasted_iota(jnp.int32, one[0].shape, 1) < HEAD_DIM
        dv_ref[:, lanes(head)] = jnp.where(first, one[0], two[0]).astype(LOW)
        dk_ref[:, lanes(head)] = jnp.where(first, one[1], two[1]).astype(LOW)
        dq_ref[:, lanes(head)] = jnp.concatenate([one[2], two[2]], axis=0).T.astype(LOW)

    for load in loads[:4]:
        load.wait()
    products(0)
    loads[4].wait()
    waiting = None
    found = []
    for head in range(heads):
        soften(head)
        if head % 2 == 0:
            turned = k_s[:, lanes(head)].T
        if len(found) == 2:
            keep(head - 2, *found)
            found = []
        if head + 1 < heads:
            products(head + 1)
        if waiting is not None:
            found.append(combine(*waiting))
        waiting = (head, turned)
    found.append(combine(*waiting))
    keep(heads - 1, *found)
    for load in loads[5:]:
        load.wait()
    grad_in_ref[...] = (
        grad_one_s[...]
        + nt(dq_ref[...], wq_s[...]) * SCORE_SCALE
        + nt(dk_ref[...], wk_s[...])
        + nt(dv_ref[...], wv_s[...])
    )
    sums_ref[...] = jnp.concatenate(
        [
            row_total(dq_ref[...].astype(WIDE)) * SCORE_SCALE,
            row_total(dv_ref[...].astype(WIDE)),
            jnp.zeros((6, model), WIDE),
        ],
        axis=0,
    )


def attend_back(slot, q, k, v, ctx, grad_ctx, lse, segs, marks, grad_one, wq, wk, wv, *earlier):
    length, width = q.shape
    heads = width // HEAD_DIM
    shapes = (
        jax.ShapeDtypeStruct((length, width), LOW),
        jax.ShapeDtypeStruct((length, width), LOW),
        jax.ShapeDtypeStruct((length, width), LOW),
        jax.ShapeDtypeStruct((length, width), WIDE),
        jax.ShapeDtypeStruct((8, width), WIDE),
    )
    tokens = pltpu.VMEM((length, width), LOW)
    turned = pltpu.VMEM((width, length), LOW)
    weight = pltpu.VMEM((width, width), LOW)
    return pl.pallas_call(
        ignoring(functools.partial(attend_back_kernel, slot=slot), 12, len(earlier)),
        out_shape=shapes,
        in_specs=[IN_VMEM] * 3 + [ANY] * (9 + len(earlier)),
        out_specs=(IN_VMEM,) * 5,
        scratch_shapes=[
            tokens, tokens, tokens, turned, turned, pltpu.VMEM((length, width), WIDE),
            weight, weight, weight,
            pltpu.VMEM((length, length), WIDE),
            pltpu.VMEM((2, length, length), WIDE),
            pltpu.VMEM((2, length, length), WIDE),
            pltpu.VMEM((2, length, length), LOW),
            pltpu.VMEM((2, length, length), LOW),
            pltpu.SemaphoreType.DMA((9,)),
        ],
        compiler_params=pltpu.CompilerParams(vmem_limit_bytes=VMEM_LIMIT),
        cost_estimate=cost(0),
        name="attend_back",
    )(segs, marks, lse, q, k, v, ctx, grad_ctx, grad_one, wq, wk, wv, *earlier)


def square_kernel(
    place_ref, x0_ref, x1_ref, dq0_ref, dq1_ref, dk0_ref, dk1_ref, dv0_ref, dv1_ref, ctx0_ref,
    ctx1_ref, attn_ref, send_ref, keep_ref, x_s, dq_s, dk_s, dv_s, ctx_s, attn_s, out_s, in_sems,
    out_sems,
):
    length, width = x0_ref.shape
    first, second = pl.ds(0, length), pl.ds(length, length)
    loads = []
    for a, b in (
        (x0_ref, x_s.at[first]), (x1_ref, x_s.at[second]), (dv0_ref, dv_s.at[first]),
        (dv1_ref, dv_s.at[second]), (dq0_ref, dq_s.at[first]), (dq1_ref, dq_s.at[second]),
        (ctx0_ref, ctx_s.at[:, first]), (ctx1_ref, ctx_s.at[:, second]), (attn_ref, attn_s),
        (dk0_ref, dk_s.at[first]), (dk1_ref, dk_s.at[second]),
    ):
        loads.append(pltpu.make_async_copy(a, b, in_sems.at[len(loads)]))
        loads[-1].start()
    mine = place_ref[0] == 0
    x = x_s[...]
    step = 256
    copies = []

    def place(part, columns, low, high):
        for n, (ref, kept) in enumerate(((send_ref, False), (keep_ref, True))):
            spot = pl.ds((n * 2 + part) * width, width)
            out_s[spot, columns] = jnp.where(mine == kept, low, high).astype(LOW)

    def flush(part):
        for n, ref in enumerate((send_ref, keep_ref)):
            spot = pl.ds((n * 2 + part) * width, width)
            copies.append(
                pltpu.make_async_copy(
                    out_s.at[spot, :], ref.at[pl.ds(part * width, width), :],
                    out_sems.at[len(copies)],
                )
            )
            copies[-1].start()

    for load in loads[:6]:
        load.wait()
    x = x_s[...]
    for start in range(0, width, step):
        columns = pl.ds(start, step)
        place(0, columns, tn(x, dq_s[:, columns]) * SCORE_SCALE, tn(x, dv_s[:, columns]))
    flush(0)
    for load in loads[6:]:
        load.wait()
    for start in range(0, width, step):
        columns = pl.ds(start, step)
        place(1, columns, tn(x, dk_s[:, columns]), nn(ctx_s[...], attn_s[:, columns]))
    flush(1)
    for copy in copies:
        copy.wait()


def square_grads(place, xs, dqs, dks, dvs, ctxs, attn, *earlier):
    length, width = xs[0].shape
    rows = length * len(xs)
    tokens = pltpu.VMEM((rows, width), LOW)
    out = jax.ShapeDtypeStruct((2 * width, width), LOW)
    return pl.pallas_call(
        ignoring(square_kernel, 12, len(earlier)),
        out_shape=(out, out),
        in_specs=[IN_SMEM] + [ANY] * (11 + len(earlier)),
        out_specs=(ANY, ANY),
        scratch_shapes=[
            tokens, tokens, tokens, tokens, pltpu.VMEM((width, rows), LOW), tokens,
            pltpu.VMEM((4 * width, width), LOW),
            pltpu.SemaphoreType.DMA((11,)),
            pltpu.SemaphoreType.DMA((4,)),
        ],
        compiler_params=pltpu.CompilerParams(vmem_limit_bytes=VMEM_LIMIT),
        cost_estimate=cost(8 * rows * width * width),
        name="square_grads",
    )(place, *xs, *dqs, *dks, *dvs, *ctxs, attn, *earlier)


def merge_kernel(own_ref, got_ref, out_ref, sems):
    rows = own_ref.shape[0]
    copies = [
        pltpu.make_async_copy(ref, out_ref.at[pl.ds(n * rows, rows), :], sems.at[n])
        for n, ref in enumerate((own_ref, got_ref))
    ]
    for copy in copies:
        copy.start()
    for copy in copies:
        copy.wait()


def merge(own, got):
    rows, width = own.shape
    return pl.pallas_call(
        merge_kernel,
        out_shape=jax.ShapeDtypeStruct((2 * rows, width), own.dtype),
        in_specs=[ANY, ANY],
        out_specs=ANY,
        scratch_shapes=[pltpu.SemaphoreType.DMA((2,))],
        cost_estimate=cost(0),
        name="merge",
    )(own, got)


def pick_kernel(place_ref, value_ref, out_ref, sem):
    copy = pltpu.make_async_copy(value_ref.at[place_ref[0]], out_ref, sem)
    copy.start()
    copy.wait()


def pick(value, place, *earlier):
    return pl.pallas_call(
        ignoring(pick_kernel, 2, len(earlier)),
        out_shape=jax.ShapeDtypeStruct(value.shape[1:], value.dtype),
        in_specs=[IN_SMEM, ANY] + [ANY] * len(earlier),
        out_specs=ANY,
        scratch_shapes=[pltpu.SemaphoreType.DMA],
        cost_estimate=cost(0),
        name="pick",
    )(place.astype(jnp.int32).reshape(1), value, *earlier)


def own_pieces(value, slot, slots, *earlier):
    count = lax.axis_size("seq")
    me = lax.axis_index("seq")
    pieces = [lax.dynamic_index_in_dim(value, me * slots + slot, 0, keepdims=False)]
    for shift in range(1, count):
        block = pick(value, (me + shift) % count * slots + slot, *earlier)
        pairs = [(source, (source + shift) % count) for source in range(count)]
        pieces.append(lax.ppermute(block, "seq", pairs))
    return pieces


def return_pieces(pieces, link_type):
    count = lax.axis_size("seq")
    me = lax.axis_index("seq")
    slots = pieces[0].shape[0]
    out = jnp.zeros((slots * count,) + pieces[0].shape[1:], pieces[0].dtype)
    out = lax.dynamic_update_slice_in_dim(out, pieces[0], me * slots, 0)
    for shift in range(1, count):
        pairs = [(source, (source - shift) % count) for source in range(count)]
        got = lax.ppermute(pieces[shift].astype(link_type), "seq", pairs).astype(out.dtype)
        out = lax.dynamic_update_slice_in_dim(out, got, ((me + shift) % count) * slots, 0)
    return out


def swap(value, axis, bit):
    count = lax.axis_size(axis)
    return lax.ppermute(value, axis, [(source, source ^ bit) for source in range(count)])


def bit_of(axis, bit):
    return (lax.axis_index(axis) // bit) % 2


def chip_orders():
    dp, seq = lax.axis_size("dp"), lax.axis_size("seq")
    along_dp = [("dp", 2**i) for i in range(1, dp.bit_length() - 1)]
    along_seq = [("seq", 2**i) for i in range(seq.bit_length() - 1)]
    x, z, y = along_dp[0], along_dp[1], along_seq[0]
    rest = along_dp[2:] + along_seq[1:]
    return [x, z, y] + rest, [y, x, z] + rest, [z, y, x] + rest


HALVINGS = 4


def half_sum(first, second, which):
    half = first.shape[0] // 2
    a = lax.dynamic_slice_in_dim(first, which * half, half, 0).astype(WIDE)
    b = lax.dynamic_slice_in_dim(second, which * half, half, 0).astype(WIDE)
    return (a + b).astype(LOW)


class Reduction:
    def __init__(self, first, second, order):
        self.first, self.second, self.order = first, second, order
        self.step = 0

    def send(self):
        axis, bit = self.order[self.step]
        mine = bit_of(axis, bit)
        sent = half_sum(self.first, self.second, 1 - mine)
        self.first, self.second = half_sum(self.first, self.second, mine), swap(sent, axis, bit)
        self.step += 1
        return sent

    def finish(self):
        while self.step < HALVINGS:
            self.send()
        share = (self.first.astype(WIDE) + self.second.astype(WIDE)).astype(LOW)
        for axis, bit in self.order[HALVINGS:]:
            share = (share.astype(WIDE) + swap(share, axis, bit).astype(WIDE)).astype(LOW)
        for step in reversed(range(1, HALVINGS)):
            share = merge(share, swap(share, *self.order[step]))
        near, far = share, swap(share, *self.order[0])
        return [near, far, swap(near, "dp", 1), swap(far, "dp", 1)]


def place_in(order):
    place = 0
    for axis, bit in order[:HALVINGS]:
        place = place * 2 + bit_of(axis, bit)
    return place


def found_block(place, half, refs, index):
    core, me = place
    near_own, far_own, near_other, far_other = refs
    block = near_own.shape[0] >> (HALVINGS - 1)
    spot = index ^ me
    blocks = 1 << (HALVINGS - 1)
    rows = pl.ds(pl.multiple_of(lax.rem(spot, blocks) * block, block), block)
    near = jnp.where(core == half, near_own[rows, :], near_other[rows, :])
    far = jnp.where(core == half, far_own[rows, :], far_other[rows, :])
    return jnp.where(spot < blocks, near, far).astype(WIDE)


def finish_kernel(place_ref, near_own, far_own, near_other, far_other, out_ref, *, turned):
    half, tile = pl.program_id(0), pl.program_id(1)
    refs = (near_own, far_own, near_other, far_other)
    place = (place_ref[0], place_ref[1])
    block = near_own.shape[0] >> (HALVINGS - 1)
    count = out_ref.shape[1 if turned else 0] // block
    found = [found_block(place, half, refs, tile * count + j) for j in range(count)]
    if turned:
        out_ref[...] = jnp.concatenate(found, axis=0).T
    else:
        for j in range(count):
            out_ref[j * block : (j + 1) * block, :] = found[j]


def finish(place, arrays, turned):
    rows, width = arrays[0].shape
    tile = rows // 2
    if turned:
        shape = (width, 4 * rows)
        spec = pl.BlockSpec((width, tile), lambda h, t, *_: (0, h * 4 + t))
    else:
        shape = (4 * rows, width)
        spec = pl.BlockSpec((tile, width), lambda h, t, *_: (h * 4 + t, 0))
    return pl.pallas_call(
        functools.partial(finish_kernel, turned=turned),
        out_shape=jax.ShapeDtypeStruct(shape, WIDE),
        grid_spec=pltpu.PrefetchScalarGridSpec(
            num_scalar_prefetch=1,
            grid=(2, 4),
            in_specs=[whole(array.shape) for array in arrays],
            out_specs=spec,
        ),
        compiler_params=pltpu.CompilerParams(vmem_limit_bytes=VMEM_LIMIT),
        cost_estimate=cost(0),
        name="finish",
    )(place, *arrays)


def finish_square_kernel(place_ref, *refs):
    parts = (len(refs) - 4) // 4
    out_refs = refs[4 * parts :]
    width = refs[0].shape[1]
    block = refs[0].shape[0] >> (HALVINGS - 1)
    each = block << HALVINGS
    for half in range(2):
        for row in range(0, each * parts, block):
            part = row // each
            place = (place_ref[0], place_ref[1 + part])
            index = (row - part * each) // block
            out = out_refs[half * 2 + row // width]
            out[row % width : row % width + block, :] = found_block(
                place, half, refs[4 * part : 4 * part + 4], index
            )


def finish_square(place, parts):
    width = parts[0][0].shape[1]
    shape = jax.ShapeDtypeStruct((width, width), WIDE)
    args = [array for part in parts for array in part]
    return pl.pallas_call(
        finish_square_kernel,
        out_shape=(shape,) * 4,
        grid_spec=pltpu.PrefetchScalarGridSpec(
            num_scalar_prefetch=1,
            grid=(1,),
            in_specs=[whole(arg.shape) for arg in args],
            out_specs=(whole(shape.shape),) * 4,
        ),
        compiler_params=pltpu.CompilerParams(vmem_limit_bytes=VMEM_LIMIT),
        cost_estimate=cost(0),
        name="finish_square",
    )(place, *args)


def on_device(
    inputs, cotangent, w_query, b_query, w_key, w_value, b_value, w_out, b_out, gain_one,
    shift_one, w_up, b_up, w_down, b_down, gain_two, shift_two, live_counts, valid_mask, segments,
):
    seqs, piece, width = inputs.shape
    count = lax.axis_size("seq")
    slots = seqs // count
    length = piece * count
    core = bit_of("dp", 1).astype(jnp.int32)
    orders = chip_orders()
    core_place = core.reshape(1)

    vectors = jnp.stack(
        [b_query, b_value, b_out, gain_one, shift_one, b_down, gain_two, shift_two]
    ).astype(WIDE)
    bias_up = b_up.astype(WIDE).reshape(1, -1)
    live = (jnp.arange(seqs) < live_counts[0]).astype(jnp.int32)
    code = segments * 2 + valid_mask * live[:, None]
    codes = jnp.stack([jnp.concatenate(own_pieces(code, slot, slots)) for slot in range(slots)])
    segs = codes // 2
    weight = codes % 2
    marks = jnp.where(weight > 0, segs, -1)
    xs, got = [], []
    for slot in range(slots):
        pieces = own_pieces(inputs, slot, slots, *got)
        got = pieces[-1:]
        xs.append(jnp.concatenate(pieces))
    forward = []
    cots = []
    for slot in range(slots):
        forward.append(attend(slot, xs[slot], segs, marks, vectors, w_query, w_key, w_value, w_out))
    for slot in range(slots):
        cots += own_pieces(cotangent, slot, slots, forward[0][0])
    (slope, mid_low, result, grad_h2, grad_feed, down_sent, down_kept, sums_two, stat_two) = (
        feed_forward(
            core_place, [each[5] for each in forward], jnp.concatenate(cots), marks, w_up, bias_up,
            w_down, vectors,
        )
    )
    along_x, along_y, along_z = orders
    down = Reduction(down_kept, swap(down_sent, "dp", 1), along_x)
    waited = down.send()
    grad_h1, grad_attn, grad_ctx, up_sent, up_kept, up_sums, sums_one = feed_back(
        core_place, grad_feed, grad_h2, slope, [each[6] for each in forward],
        [each[7] for each in forward], mid_low, w_up, w_down, w_out, vectors, waited,
    )
    up = Reduction(up_kept, swap(up_sent, "dp", 1), along_y)
    backward = []
    waiting = [[down.send(), up.send()], [down.send()]]
    for slot in range(slots):
        backward.append(
            attend_back(
                slot, *forward[slot][:4], grad_ctx, forward[slot][4], segs, marks, grad_h1,
                w_query, w_key, w_value, *waiting[min(slot, 1)],
            )
        )
    square_sent, square_kept = square_grads(
        core_place, xs, *([each[i] for each in backward] for i in range(3)),
        [each[3] for each in forward], grad_attn, down.send(), up.send(),
    )
    square_got = swap(square_sent, "dp", 1)
    each_rows = square_kept.shape[0] // len(orders)
    thirds = []
    for part, order in enumerate(orders):
        inside = slice(part * each_rows, (part + 1) * each_rows)
        thirds.append(Reduction(square_kept[inside], square_got[inside], order))
    places = [place_in(order).astype(jnp.int32) for order in orders]
    grad_w_down = finish(jnp.stack([core, places[0]]), down.finish(), False)
    grad_w_up = finish(jnp.stack([core, places[1]]), up.finish(), True)
    squares = finish_square(jnp.stack([core] + places), [third.finish() for third in thirds])

    result = result.reshape(slots, length, width)
    result_out = return_pieces(
        [result[:, i * piece : (i + 1) * piece] for i in range(count)], LOW
    )
    stats = [
        sum(each[8][0, 0] for each in forward),
        sum(each[8][1, 0] for each in forward),
        stat_two[0, 0],
        stat_two[1, 0],
        jnp.sum(weight).astype(WIDE),
    ]
    stats = jnp.concatenate([jnp.stack(stats), jnp.zeros((width - 5,), WIDE)]).reshape(1, width)
    small = jnp.concatenate(
        [
            sum(each[4][0:2] for each in backward),
            sums_one[0:3],
            sums_two[0:3],
            stats,
            jnp.sum(up_sums, axis=0).reshape(-1, width),
        ],
        axis=0,
    )
    for axis, bit in [("dp", 1)] + orders[0]:
        small = small + swap(small, axis, bit)
    rms_values = jnp.sqrt(small[8, :4] / (width * small[8, 4]))

    grad_inputs = jnp.stack([each[3] for each in backward])
    grad_out = return_pieces(
        [grad_inputs[:, i * piece : (i + 1) * piece] for i in range(count)], LOW
    )
    return (
        result_out,
        grad_out,
        squares[0],
        small[0],
        squares[1],
        squares[2],
        small[1],
        squares[3],
        small[4],
        small[2],
        small[3],
        grad_w_up,
        small[9:].reshape(-1),
        grad_w_down,
        small[7],
        small[5],
        small[6],
        rms_values,
    )


def solution(mesh):
    split = P("dp", "seq", None)
    pair = P("dp", "seq")
    return jax.shard_map(
        on_device,
        mesh=mesh,
        in_specs=(split, split) + (P(),) * 15 + (P("dp"), pair, pair),
        out_specs=(split, split) + (P(),) * 16,
        check_vma=False,
    )
```

time: 443 us -> 677 us (1.53)
  Pallas kernels: 141 us -> 416 us
  matrix products: 28.3 us -> 0 us
  local copies, waits for them, and re-layouts: 43.5 us -> 25.2 us
  other arithmetic: 23.1 us -> 32.7 us
  starting transfers between devices: 76.1 us -> 66.9 us
    pallas_call x8 -> x30, Pallas kernels: 133 us -> 408 us  [the longest x15 204 us: merge(): pl.pallas_call(merge_kernel, out_shape=jax.ShapeDtypeStruct((2 * rows, wi...]
    dot_general x8 -> x0, matrix products: 28.3 us -> none  [tn(): lax.dot_general(left, right, (((0,), (0,)), ((), ())), preferred_element_...]
    ppermute x53 -> x58, waiting for transfers between devices: 93.4 us -> 113 us  [swap(): lax.ppermute(value, axis, [(source, source ^ bit) for source in range(cou...]
    ppermute x2, waiting for transfers between devices: 14.9 us -> 0.01 us  [return_pieces(): lax.ppermute(pieces[shift].astype(link_type), 'seq', pairs)]
    convert_element_type x21 -> x26, other arithmetic: 7.42 us -> 18.9 us  [the longest x20 18.1 us: half_sum(): return (a + b).astype(LOW)]
    ppermute x53 -> x58, starting transfers between devices: 66.8 us -> 56.3 us  [swap(): lax.ppermute(value, axis, [(source, source ^ bit) for source in range(cou...]
    reshape x9 -> x1, local copies, waits for them, and re-layouts: 10.1 us -> 0.01 us  [on_device(): jnp.sum(up_sums, axis=0).reshape(-1, width)]
    unnamed x59 -> x112, local copies, waits for them, and re-layouts: 13.8 us -> 9.52 us
  transfers between devices with their start and end apart: 61 -> 66, of which waited for: 19 -> 26; matrix products, arithmetic and copies ran while one was open for 19% -> 6% of each run, Pallas kernels for 23% -> 49%
where the time goes in v3:
time: 677 us; the launch traced here: 668 us
  Pallas kernels  416 us (61%)
  waiting for transfers between devices  120 us (18%)
  starting transfers between devices  66.9 us (10%)
  other arithmetic  32.7 us (5%)
  local copies, waits for them, and re-layouts  25.2 us (4%)
  between operations  7.19 us (1%)
    pallas_call x15, Pallas kernels, merge(): pl.pallas_call(merge_kernel, out_shape=jax.ShapeDtypeStruct((2 * rows, wi...  204 us
    ppermute x58, waiting for transfers between devices, swap(): lax.ppermute(value, axis, [(source, source ^ bit) for source in range(cou...  113 us
    ppermute x58, starting transfers between devices, swap(): lax.ppermute(value, axis, [(source, source ^ bit) for source in range(cou...  56.3 us
    pallas_call x6, Pallas kernels, pick(): pl.pallas_call(ignoring(pick_kernel, 2, len(earlier)), out_shape=jax.Shap...  54.4 us
    pallas_call x1, Pallas kernels, feed_forward(): pl.pallas_call(feed_kernel, out_shape=shapes, in_specs=[IN_SMEM] + [ANY]...  37.7 us
    pallas_call x2, Pallas kernels, attend_back(): pl.pallas_call(ignoring(functools.partial(attend_back_kernel, slot=slot),...  30.4 us
    pallas_call x1, Pallas kernels, feed_back(): pl.pallas_call(ignoring(feed_back_kernel, 13, len(earlier)), out_shape=sh...  29.3 us
    pallas_call x2, Pallas kernels, attend(): pl.pallas_call(functools.partial(attend_kernel, slot=slot), out_shape=sha...  26.5 us
  transfers between devices with their start and end apart: 66, of which 26 were waited for; matrix products, arithmetic and copies ran while one was open for 6% of the time, Pallas kernels for 49%

profile of v3, /device:TPU:0, one launch (start us, length us, event | category | flops | bytes accessed | tf_op | source)
XLA Modules:
  0.0 667.7 jit_solution(13641273916576796080)
XLA Ops:
  8.3 13.0 %pick.6 = bf16[256,768]{1,0:T(8,128)(2,1)} custom-call(s32[1]{0:T(128)} %bitcast.2.refs_0_, bf16[4,256,768]{2,1,0:T(8,128)(2,1)} %refs_1_.5), custom_call_target="tpu_custom_call" | custom-call | tf_op jit(solution)/shard_map/pick/pallas_call | solution.py:922
  25.7 6.5 collective-permute-done.refs_2_
  33.0 13.0 %pick.9 = bf16[256,768]{1,0:T(8,128)(2,1)} custom-call(s32[1]{0:T(128)} %bitcast.7.refs_0_, bf16[4,256,768]{2,1,0:T(8,128)(2,1)} %refs_1_.5, bf16[256,768]{1,0:T(8,128)(2,1)} %copy-done.10), custom_call_target="tpu_custom_call" | custom-call | tf_op jit(solution)/shard_map/pick/pallas_call | solution.py:922
  49.8 13.1 %attend.2 = (bf16[512,768]{1,0:T(8,128)(2,1)}, bf16[512,768]{1,0:T(8,128)(2,1)}, bf16[512,768]{1,0:T(8,128)(2,1)}, bf16[768,512]{1,0:T(8,128)(2,1)}, f32[16,512]...) custom-call(bf16[512,768]{1,0:T(8,128)(2,1)} %pad_maximum_fusion.2.x_ref.ref, ...), custom_call_target="tpu_custom_call" | custom-call | tf_op jit(solution)/shard_map/attend/pallas_call | solution.py:222
  62.9 13.0 %pick.11 = bf16[256,768]{1,0:T(8,128)(2,1)} custom-call(s32[1]{0:T(128)} %bitcast.7.refs_0_, bf16[4,256,768]{2,1,0:T(8,128)(2,1)} %refs_1_.7, bf16[512,768]{1,0:T(8,128)(2,1)} %get-tuple-element.70.refs_2_.refs_3_), custom_call_target="tpu_custom_call" | custom-call | tf_op jit(solution)/shard_map/pick/pallas_call | solution.py:922
  76.0 13.0 %pick.10 = bf16[256,768]{1,0:T(8,128)(2,1)} custom-call(s32[1]{0:T(128)} %bitcast.2.refs_0_, bf16[4,256,768]{2,1,0:T(8,128)(2,1)} %refs_1_.7, bf16[512,768]{1,0:T(8,128)(2,1)} %get-tuple-element.70.refs_2_.refs_3_), custom_call_target="tpu_custom_call" | custom-call | tf_op jit(solution)/shard_map/pick/pallas_call | solution.py:922
  92.7 13.4 %attend.3 = (bf16[512,768]{1,0:T(8,128)(2,1)}, bf16[512,768]{1,0:T(8,128)(2,1)}, bf16[512,768]{1,0:T(8,128)(2,1)}, bf16[768,512]{1,0:T(8,128)(2,1)}, f32[16,512]...) custom-call(bf16[512,768]{1,0:T(8,128)(2,1)} %pad_maximum_fusion.3.x_ref.ref, ...), custom_call_target="tpu_custom_call" | custom-call | tf_op jit(solution)/shard_map/attend/pallas_call | solution.py:222
  107.8 37.7 %feed_forward.1 = (bf16[1024,3072]{1,0:T(8,128)(2,1)}, bf16[1024,768]{1,0:T(8,128)(2,1)}, bf16[1024,768]{1,0:T(8,128)(2,1)}, f32[1024,768]{1,0:T(8,128)}, bf16[1...) custom-call(s32[1]{0:T(128)} %bitcast.place_ref.refs_0_, ...), custom_call_target="tpu_custom_call" | custom-call | tf_op jit(solution)/shard_map/feed_forward/pallas_call | solution.py:431
  145.7 4.7 collective-permute-done.7
  150.4 3.7 add_convert_fusion.2
  154.0 29.3 %feed_back.1 = (f32[1024,768]{1,0:T(8,128)}, bf16[1024,768]{1,0:T(8,128)(2,1)}, bf16[2,768,512]{2,1,0:T(8,128)(2,1)}, bf16[1536,768]{1,0:T(8,128)(2,1)}, bf16[15...) custom-call(s32[1]{0:T(128)} %bitcast.place_ref.refs_0_, bf16[1024,768]{1,0:T(8,128)(2,1)} %get-tuple-element.76.refs_1_, ...), custom_call_target="tpu_custom_call" | custom-call | tf_op jit(solution)/shard_map/feed_back/pallas_call | solution.py:645
  193.2 18.7 %collective-permute-done.8 = bf16[768,768]{1,0:T(8,128)(2,1)} collective-permute-done((bf16[768,768]{1,0:T(8,128)(2,1)S(1)}, bf16[768,768]{1,0:T(8,128)(2,1)}, u32[]{:S(2)}, u32[]{:S(2)}) %collective-permute-start.8) | collective-permute-done | bytes 1179680 | tf_op jit(solution)/shard_map/ppermute | solution.py:959
  215.1 13.3 %collective-permute-done.10 = bf16[384,768]{1,0:T(8,128)(2,1)} collective-permute-done((bf16[384,768]{1,0:T(8,128)(2,1)S(1)}, bf16[384,768]{1,0:T(8,128)(2,1)}, u32[]{:S(2)}, u32[]{:S(2)}) %collective-permute-start.10) | collective-permute-done | bytes 589856 | tf_op jit(solution)/shard_map/ppermute | solution.py:959
  231.0 15.2 %attend_back.3 = (bf16[512,768]{1,0:T(8,128)(2,1)}, bf16[512,768]{1,0:T(8,128)(2,1)}, bf16[512,768]{1,0:T(8,128)(2,1)}, f32[512,768]{1,0:T(8,128)}, f32[8,768]{1,0:T(8,128)}) custom-call(s32[2,512]{1,0:T(2,128)} %get-tuple-element.129.seg_ref.refs_0_, s32[2,512]{1,0:T(2,128)} %get-tuple-element.128.mark_ref.refs_1_, f32[16,512]{1,0:T(8,128)} %get-tuple-element.91.refs_2_, ...), custom_call_target="tpu_custom_call" | custom-call | tf_op jit(solution)/shard_map/attend_back/pallas_call | solution.py:793
  246.9 15.2 %attend_back.2 = (bf16[512,768]{1,0:T(8,128)(2,1)}, bf16[512,768]{1,0:T(8,128)(2,1)}, bf16[512,768]{1,0:T(8,128)(2,1)}, f32[512,768]{1,0:T(8,128)}, f32[8,768]{1,0:T(8,128)}) custom-call(s32[2,512]{1,0:T(2,128)} %get-tuple-element.129.seg_ref.refs_0_, s32[2,512]{1,0:T(2,128)} %get-tuple-element.128.mark_ref.refs_1_, f32[16,512]{1,0:T(8,128)} %get-tuple-element.72.refs_2_, ...), custom_call_target="tpu_custom_call" | custom-call | tf_op jit(solution)/shard_map/attend_back/pallas_call | solution.py:793
  265.1 9.1 %square_grads.1 = (bf16[1536,768]{1,0:T(8,128)(2,1)}, bf16[1536,768]{1,0:T(8,128)(2,1)}) custom-call(s32[1]{0:T(128)} %bitcast.place_ref.refs_0_, bf16[512,768]{1,0:T(8,128)(2,1)} %pad_maximum_fusion.2.x_ref.refs_1_, bf16[512,768]{1,0:T(8,128)(2,1)} %pad_maximum_fusion.3.x_ref.refs_2_, bf16[512,768]{1,0:T(8,128)(2,1)} %get-tuple-element.97.refs_3_, ...), custom_call_target="tpu_custom_call" | custom-call | flops 4831838208 | tf_op jit(solution)/shard_map/square_grads/pallas_call | solution.py:873
  279.1 5.7 collective-permute-done.59
  285.6 8.8 %collective-permute-done.60.got_ref = bf16[96,768]{1,0:T(8,128)(2,1)S(1)} collective-permute-done((bf16[96,768]{1,0:T(8,128)(2,1)S(1)}, bf16[96,768]{1,0:T(8,128)(2,1)S(1)}, u32[]{:S(2)}, u32[]{:S(2)}) %collective-permute-start.60) | collective-permute-done | bytes 147488 | tf_op jit(solution)/shard_map/ppermute | solution.py:959
  295.0 10.1 %merge.27.own_ref = bf16[192,768]{1,0:T(8,128)(2,1)} custom-call(bf16[96,768]{1,0:T(8,128)(2,1)} %copy-done.17, bf16[96,768]{1,0:T(8,128)(2,1)} %copy-done.35), custom_call_target="tpu_custom_call" | custom-call | tf_op jit(solution)/shard_map/merge/pallas_call | solution.py:904
  309.4 3.7 collective-permute-done.61.got_ref
  313.7 19.0 %merge.28.own_ref = bf16[384,768]{1,0:T(8,128)(2,1)} custom-call(bf16[192,768]{1,0:T(8,128)(2,1)} %merge.27.own_ref, bf16[192,768]{1,0:T(8,128)(2,1)} %copy-done.24), custom_call_target="tpu_custom_call" | custom-call | tf_op jit(solution)/shard_map/merge/pallas_call | solution.py:904
  340.0 3.4 collective-permute-start.53
  346.4 3.4 collective-permute-done.46
  350.0 3.9 collective-permute-done.47
  356.3 36.9 %merge.29.near_own = bf16[768,768]{1,0:T(8,128)(2,1)} custom-call(bf16[384,768]{1,0:T(8,128)(2,1)} %merge.28.own_ref, bf16[384,768]{1,0:T(8,128)(2,1)} %copy-done.13), custom_call_target="tpu_custom_call" | custom-call | tf_op jit(solution)/shard_map/merge/pallas_call | solution.py:904
  394.6 10.1 %merge.24.own_ref = bf16[192,768]{1,0:T(8,128)(2,1)} custom-call(bf16[96,768]{1,0:T(8,128)(2,1)} %copy-done.16, bf16[96,768]{1,0:T(8,128)(2,1)} %copy-done.33), custom_call_target="tpu_custom_call" | custom-call | tf_op jit(solution)/shard_map/merge/pallas_call | solution.py:904
  406.5 5.2 collective-permute-done.54.got_ref
  412.4 19.0 %merge.25.own_ref = bf16[384,768]{1,0:T(8,128)(2,1)} custom-call(bf16[192,768]{1,0:T(8,128)(2,1)} %merge.24.own_ref, bf16[192,768]{1,0:T(8,128)(2,1)} %copy-done.25), custom_call_target="tpu_custom_call" | custom-call | tf_op jit(solution)/shard_map/merge/pallas_call | solution.py:904
  441.9 6.1 collective-permute-done.55.got_ref
  448.7 36.9 %merge.26.near_own = bf16[768,768]{1,0:T(8,128)(2,1)} custom-call(bf16[384,768]{1,0:T(8,128)(2,1)} %merge.25.own_ref, bf16[384,768]{1,0:T(8,128)(2,1)} %copy-done.14), custom_call_target="tpu_custom_call" | custom-call | tf_op jit(solution)/shard_map/merge/pallas_call | solution.py:904
  496.1 3.4 collective-permute-done.16
  510.0 3.4 collective-permute-done.17
  515.0 3.6 collective-permute-done.38
  520.4 4.4 collective-permute-done.28
  526.9 3.5 collective-permute-done.18
  538.0 4.1 merge.21.own_ref
  543.5 4.1 merge.18.own_ref
  549.9 4.1 merge.15.own_ref
  555.6 7.1 %merge.22.own_ref = bf16[128,768]{1,0:T(8,128)(2,1)} custom-call(bf16[64,768]{1,0:T(8,128)(2,1)} %merge.21.own_ref, bf16[64,768]{1,0:T(8,128)(2,1)} %copy-done.37), custom_call_target="tpu_custom_call" | custom-call | tf_op jit(solution)/shard_map/merge/pallas_call | solution.py:904
  566.1 7.1 %merge.19.own_ref = bf16[128,768]{1,0:T(8,128)(2,1)} custom-call(bf16[64,768]{1,0:T(8,128)(2,1)} %merge.18.own_ref, bf16[64,768]{1,0:T(8,128)(2,1)} %copy-done.38), custom_call_target="tpu_custom_call" | custom-call | tf_op jit(solution)/shard_map/merge/pallas_call | solution.py:904
  574.6 7.1 %merge.16.own_ref = bf16[128,768]{1,0:T(8,128)(2,1)} custom-call(bf16[64,768]{1,0:T(8,128)(2,1)} %merge.15.own_ref, bf16[64,768]{1,0:T(8,128)(2,1)} %collective-permute-done.20.got_ref), custom_call_target="tpu_custom_call" | custom-call | tf_op jit(solution)/shard_map/merge/pallas_call | solution.py:904
  583.5 13.0 %merge.23.refs_8_ = bf16[256,768]{1,0:T(8,128)(2,1)} custom-call(bf16[128,768]{1,0:T(8,128)(2,1)} %merge.22.own_ref, bf16[128,768]{1,0:T(8,128)(2,1)} %copy-done.26), custom_call_target="tpu_custom_call" | custom-call | tf_op jit(solution)/shard_map/merge/pallas_call | solution.py:904
  596.5 13.0 %merge.20.refs_4_ = bf16[256,768]{1,0:T(8,128)(2,1)} custom-call(bf16[128,768]{1,0:T(8,128)(2,1)} %merge.19.own_ref, bf16[128,768]{1,0:T(8,128)(2,1)} %copy-done.27), custom_call_target="tpu_custom_call" | custom-call | tf_op jit(solution)/shard_map/merge/pallas_call | solution.py:904
  613.0 13.0 %merge.17.refs_0_ = bf16[256,768]{1,0:T(8,128)(2,1)} custom-call(bf16[128,768]{1,0:T(8,128)(2,1)} %merge.16.own_ref, bf16[128,768]{1,0:T(8,128)(2,1)} %collective-permute-done.21.got_ref), custom_call_target="tpu_custom_call" | custom-call | tf_op jit(solution)/shard_map/merge/pallas_call | solution.py:904
  634.0 3.9 collective-permute-done.22.refs_1_
  641.5 8.0 %finish.3 = f32[3072,768]{1,0:T(8,128)} custom-call(s32[2]{0:T(128)} %get-tuple-element.181.place_ref, bf16[768,768]{1,0:T(8,128)(2,1)} %merge.29.near_own, bf16[768,768]{1,0:T(8,128)(2,1)} %collective-permute-done.63.far_own, bf16[768,768]{1,0:T(8,128)(2,1)} %collective-permute-done.64.near_other, bf16[768,768]{1,0:T(8,128)(2,1)} %collective-permute-done.65.far_other), custom_call_target="tpu_custom_call" | custom-call | tf_op jit(solution)/shard_map/finish/pallas_call | solution.py:1052
  651.1 7.6 %finish_square.1 = (f32[768,768]{1,0:T(8,128)}, f32[768,768]{1,0:T(8,128)}, f32[768,768]{1,0:T(8,128)}, f32[768,768]{1,0:T(8,128)}) custom-call(s32[4]{0:T(128)} %pad_add_fusion.3.place_ref, bf16[256,768]{1,0:T(8,128)(2,1)} %merge.17.refs_0_, bf16[256,768]{1,0:T(8,128)(2,1)} %collective-permute-done.22.refs_1_, ...), custom_call_target="tpu_custom_call" | custom-call | tf_op jit(solution)/shard_map/finish_square/pallas_call | solution.py:1088
  658.8 8.4 %finish.2 = f32[768,3072]{1,0:T(8,128)} custom-call(s32[2]{0:T(128)} %get-tuple-element.180.place_ref, bf16[768,768]{1,0:T(8,128)(2,1)} %merge.26.near_own, bf16[768,768]{1,0:T(8,128)(2,1)} %collective-permute-done.56.far_own, bf16[768,768]{1,0:T(8,128)(2,1)} %collective-permute-done.57.near_other, bf16[768,768]{1,0:T(8,128)(2,1)} %collective-permute-done.58.far_other), custom_call_target="tpu_custom_call" | custom-call | tf_op jit(solution)/shard_map/finish/pallas_call | solution.py:1052
  (308 shorter events, 137.8 us)
Async XLA Ops:
  4.0 20.4 %collective-permute-start.2 = (s32[256]{0:T(256)}, s32[256]{0:T(256)S(1)}, u32[]{:S(2)}, u32[]{:S(2)}) collective-permute-start(s32[256]{0:T(256)} %pick.8), channel_id=1, source_target_pairs={{0,1},{1,0},{2,3},{3,2},{4,5},{5,4},{6,7},{7,6},{8,9},{9,8},{10,11... | collective-permute-start | bytes 3080 | tf_op jit(solution)/shard_map/ppermute | solution.py:940
  8.3 16.1 %collective-permute-start.1 = (s32[256]{0:T(256)}, s32[256]{0:T(256)S(1)}, u32[]{:S(2)}, u32[]{:S(2)}) collective-permute-start(s32[256]{0:T(256)} %pick.7), channel_id=1, source_target_pairs={{0,1},{1,0},{2,3},{3,2},{4,5},{5,4},{6,7},{7,6},{8,9},{9,8},{10,11... | collective-permute-start | bytes 3080 | tf_op jit(solution)/shard_map/ppermute | solution.py:940
  21.4 10.9 %collective-permute-start = (bf16[256,768]{1,0:T(8,128)(2,1)}, bf16[256,768]{1,0:T(8,128)(2,1)S(1)}, u32[]{:S(2)}, u32[]{:S(2)}) collective-permute-start(bf16[256,768]{1,0:T(8,128)(2,1)} %pick.6), channel_id=1, source_target_pairs={{0,1},{1,0},{2,3},{3,2},{4,5},{5,4},{6,7},{7,6},{8,9},{9,8},{10,11... | collective-permute-start | bytes 1179656 | tf_op jit(solution)/shard_map/ppermute | solution.py:940
  46.0 45.8 %collective-permute-start.3 = (bf16[256,768]{1,0:T(8,128)(2,1)}, bf16[256,768]{1,0:T(8,128)(2,1)S(1)}, u32[]{:S(2)}, u32[]{:S(2)}) collective-permute-start(bf16[256,768]{1,0:T(8,128)(2,1)} %pick.9), channel_id=1, source_target_pairs={{0,1},{1,0},{2,3},{3,2},{4,5},{5,4},{6,7},{7,6},{8,9},{9,8},{10,11... | collective-permute-start | bytes 1179656 | tf_op jit(solution)/shard_map/ppermute | solution.py:940
  89.0 17.1 %collective-permute-start.5 = (bf16[256,768]{1,0:T(8,128)(2,1)S(1)}, bf16[256,768]{1,0:T(8,128)(2,1)S(1)}, u32[]{:S(2)}, u32[]{:S(2)}) collective-permute-start(bf16[256,768]{1,0:T(8,128)(2,1)S(1)} %copy-done.23), channel_id=1, source_target_pairs={{0,1},{1,0},{2,3},{3,2},{4,5},{5,4},{6,7},{7,6},{8,9},{9,8},{10,11... | collective-permute-start | bytes 1179656 | tf_op jit(solution)/shard_map/ppermute | solution.py:940
  89.4 17.2 %collective-permute-start.4 = (bf16[256,768]{1,0:T(8,128)(2,1)}, bf16[256,768]{1,0:T(8,128)(2,1)S(1)}, u32[]{:S(2)}, u32[]{:S(2)}) collective-permute-start(bf16[256,768]{1,0:T(8,128)(2,1)} %pick.10), channel_id=1, source_target_pairs={{0,1},{1,0},{2,3},{3,2},{4,5},{5,4},{6,7},{7,6},{8,9},{9,8},{10,11... | collective-permute-start | bytes 1179656 | tf_op jit(solution)/shard_map/ppermute | solution.py:940
  183.5 28.4 %collective-permute-start.8 = (bf16[768,768]{1,0:T(8,128)(2,1)S(1)}, bf16[768,768]{1,0:T(8,128)(2,1)}, u32[]{:S(2)}, u32[]{:S(2)}) collective-permute-start(bf16[768,768]{1,0:T(8,128)(2,1)S(1)} %copy-done.4), channel_id=1, source_target_pairs={{0,4},{2,6},{4,0},{6,2},{8,12},{10,14},{12,8},{14,10},{16,20},{18,... | collective-permute-start | bytes 3538952 | tf_op jit(solution)/shard_map/ppermute | solution.py:959
  192.5 69.6 %collective-permute-start.13 = (bf16[768,768]{1,0:T(8,128)(2,1)S(1)}, bf16[768,768]{1,0:T(8,128)(2,1)}, u32[]{:S(2)}, u32[]{:S(2)}) collective-permute-start(bf16[768,768]{1,0:T(8,128)(2,1)S(1)} %get-tuple-element.131.refs_13_), channel_id=1, source_target_pairs={{0,1},{1,0},{2,3},{3,2},{4,5},{5,4},{6,7},{7,6},{8,9},{9,8},{10,11... | collective-permute-start | bytes 3538952 | tf_op jit(solution)/shard_map/ppermute | solution.py:959
  213.4 15.0 %collective-permute-start.10 = (bf16[384,768]{1,0:T(8,128)(2,1)S(1)}, bf16[384,768]{1,0:T(8,128)(2,1)}, u32[]{:S(2)}, u32[]{:S(2)}) collective-permute-start(bf16[384,768]{1,0:T(8,128)(2,1)S(1)} %get-tuple-element.143.refs_12_), channel_id=1, source_target_pairs={{0,8},{2,10},{4,12},{6,14},{8,0},{10,2},{12,4},{14,6},{16,24},{18,... | collective-permute-start | bytes 1769480 | tf_op jit(solution)/shard_map/ppermute | solution.py:959
  230.4 15.8 %collective-permute-start.12 = (bf16[192,768]{1,0:T(8,128)(2,1)}, bf16[192,768]{1,0:T(8,128)(2,1)S(1)}, u32[]{:S(2)}, u32[]{:S(2)}) collective-permute-start(bf16[192,768]{1,0:T(8,128)(2,1)} %get-tuple-element.159.refs_12_), channel_id=1, source_target_pairs={{0,1},{1,0},{2,3},{3,2},{4,5},{5,4},{6,7},{7,6},{8,9},{9,8},{10,11... | collective-permute-start | bytes 884744 | tf_op jit(solution)/shard_map/ppermute | solution.py:959
  263.7 13.7 %collective-permute-start.50 = (bf16[384,768]{1,0:T(8,128)(2,1)S(1)}, bf16[384,768]{1,0:T(8,128)(2,1)S(1)}, u32[]{:S(2)}, u32[]{:S(2)}) collective-permute-start(bf16[384,768]{1,0:T(8,128)(2,1)S(1)} %get-tuple-element.135.refs_13_), channel_id=1, source_target_pairs={{0,4},{2,6},{4,0},{6,2},{8,12},{10,14},{12,8},{14,10},{16,20},{18,... | collective-permute-start | bytes 1769480 | tf_op jit(solution)/shard_map/ppermute | solution.py:959
  274.3 158.5 %collective-permute-start.14 = (bf16[1536,768]{1,0:T(8,128)(2,1)}, bf16[1536,768]{1,0:T(8,128)(2,1)}, u32[]{:S(2)}, u32[]{:S(2)}) collective-permute-start(bf16[1536,768]{1,0:T(8,128)(2,1)} %get-tuple-element.105), channel_id=1, source_target_pairs={{0,2},{2,0},{4,6},{6,4},{8,10},{10,8},{12,14},{14,12},{16,18},{18,... | collective-permute-start | bytes 7077896 | tf_op jit(solution)/shard_map/ppermute | solution.py:959
  274.4 10.4 %collective-permute-start.59 = (bf16[96,768]{1,0:T(8,128)(2,1)S(1)}, bf16[96,768]{1,0:T(8,128)(2,1)S(1)}, u32[]{:S(2)}, u32[]{:S(2)}) collective-permute-start(bf16[96,768]{1,0:T(8,128)(2,1)S(1)} %copy-done.34), channel_id=1, source_target_pairs={{0,16},{2,18},{4,20},{6,22},{8,24},{10,26},{12,28},{14,30},{16,0},... | collective-permute-start | bytes 442376 | tf_op jit(solution)/shard_map/ppermute | solution.py:959
  277.5 30.5 %collective-permute-start.51 = (bf16[192,768]{1,0:T(8,128)(2,1)S(1)}, bf16[192,768]{1,0:T(8,128)(2,1)S(1)}, u32[]{:S(2)}, u32[]{:S(2)}) collective-permute-start(bf16[192,768]{1,0:T(8,128)(2,1)S(1)} %get-tuple-element.157), channel_id=1, source_target_pairs={{0,8},{2,10},{4,12},{6,14},{8,0},{10,2},{12,4},{14,6},{16,24},{18,... | collective-permute-start | bytes 884744 | tf_op jit(solution)/shard_map/ppermute | solution.py:959
  284.9 9.5 %collective-permute-start.60 = (bf16[96,768]{1,0:T(8,128)(2,1)S(1)}, bf16[96,768]{1,0:T(8,128)(2,1)S(1)}, u32[]{:S(2)}, u32[]{:S(2)}) collective-permute-start(bf16[96,768]{1,0:T(8,128)(2,1)S(1)} %add_convert_fusion.24.own_ref), channel_id=1, source_target_pairs={{0,16},{2,18},{4,20},{6,22},{8,24},{10,26},{12,28},{14,30},{16,0},... | collective-permute-start | bytes 442376 | tf_op jit(solution)/shard_map/ppermute | solution.py:959
  305.1 7.9 %collective-permute-start.61 = (bf16[192,768]{1,0:T(8,128)(2,1)}, bf16[192,768]{1,0:T(8,128)(2,1)S(1)}, u32[]{:S(2)}, u32[]{:S(2)}) collective-permute-start(bf16[192,768]{1,0:T(8,128)(2,1)} %merge.27.own_ref), channel_id=1, source_target_pairs={{0,1},{1,0},{2,3},{3,2},{4,5},{5,4},{6,7},{7,6},{8,9},{9,8},{10,11... | collective-permute-start | bytes 884744 | tf_op jit(solution)/shard_map/ppermute | solution.py:959
  308.0 31.9 %collective-permute-start.52 = (bf16[96,768]{1,0:T(8,128)(2,1)S(1)}, bf16[96,768]{1,0:T(8,128)(2,1)S(1)}, u32[]{:S(2)}, u32[]{:S(2)}) collective-permute-start(bf16[96,768]{1,0:T(8,128)(2,1)S(1)} %add_convert_fusion.27), channel_id=1, source_target_pairs={{0,16},{2,18},{4,20},{6,22},{8,24},{10,26},{12,28},{14,30},{16,0},... | collective-permute-start | bytes 442376 | tf_op jit(solution)/shard_map/ppermute | solution.py:959
  332.7 22.8 %collective-permute-start.62 = (bf16[384,768]{1,0:T(8,128)(2,1)}, bf16[384,768]{1,0:T(8,128)(2,1)S(1)}, u32[]{:S(2)}, u32[]{:S(2)}) collective-permute-start(bf16[384,768]{1,0:T(8,128)(2,1)} %merge.28.own_ref), channel_id=1, source_target_pairs={{0,8},{2,10},{4,12},{6,14},{8,0},{10,2},{12,4},{14,6},{16,24},{18,... | collective-permute-start | bytes 1769480 | tf_op jit(solution)/shard_map/ppermute | solution.py:959
  340.0 53.9 %collective-permute-start.53 = (bf16[96,768]{1,0:T(8,128)(2,1)S(1)}, bf16[96,768]{1,0:T(8,128)(2,1)S(1)}, u32[]{:S(2)}, u32[]{:S(2)}) collective-permute-start(bf16[96,768]{1,0:T(8,128)(2,1)S(1)} %add_convert_fusion.26.own_ref), channel_id=1, source_target_pairs={{0,16},{2,18},{4,20},{6,22},{8,24},{10,26},{12,28},{14,30},{16,0},... | collective-permute-start | bytes 442376 | tf_op jit(solution)/shard_map/ppermute | solution.py:959
  353.9 84.7 %collective-permute-start.48 = (f32[13,768]{1,0:T(8,128)S(1)}, f32[13,768]{1,0:T(8,128)S(1)}, u32[]{:S(2)}, u32[]{:S(2)}) collective-permute-start(f32[13,768]{1,0:T(8,128)S(1)} %add.540), channel_id=1, source_target_pairs={{0,1},{1,0},{2,3},{3,2},{4,5},{5,4},{6,7},{7,6},{8,9},{9,8},{10,11... | collective-permute-start | bytes 119816 | tf_op jit(solution)/shard_map/ppermute | solution.py:959
  393.2 102.3 %collective-permute-start.63 = (bf16[768,768]{1,0:T(8,128)(2,1)}, bf16[768,768]{1,0:T(8,128)(2,1)}, u32[]{:S(2)}, u32[]{:S(2)}) collective-permute-start(bf16[768,768]{1,0:T(8,128)(2,1)} %merge.29.near_own), channel_id=1, source_target_pairs={{0,4},{2,6},{4,0},{6,2},{8,12},{10,14},{12,8},{14,10},{16,20},{18,... | collective-permute-start | bytes 3538952 | tf_op jit(solution)/shard_map/ppermute | solution.py:959
  404.7 7.0 %collective-permute-start.54 = (bf16[192,768]{1,0:T(8,128)(2,1)}, bf16[192,768]{1,0:T(8,128)(2,1)S(1)}, u32[]{:S(2)}, u32[]{:S(2)}) collective-permute-start(bf16[192,768]{1,0:T(8,128)(2,1)} %merge.24.own_ref), channel_id=1, source_target_pairs={{0,8},{2,10},{4,12},{6,14},{8,0},{10,2},{12,4},{14,6},{16,24},{18,... | collective-permute-start | bytes 884744 | tf_op jit(solution)/shard_map/ppermute | solution.py:959
  431.4 16.5 %collective-permute-start.55 = (bf16[384,768]{1,0:T(8,128)(2,1)}, bf16[384,768]{1,0:T(8,128)(2,1)S(1)}, u32[]{:S(2)}, u32[]{:S(2)}) collective-permute-start(bf16[384,768]{1,0:T(8,128)(2,1)} %merge.25.own_ref), channel_id=1, source_target_pairs={{0,4},{2,6},{4,0},{6,2},{8,12},{10,14},{12,8},{14,10},{16,20},{18,... | collective-permute-start | bytes 1769480 | tf_op jit(solution)/shard_map/ppermute | solution.py:959
  435.5 50.1 %collective-permute-start.35 = (bf16[256,768]{1,0:T(8,128)(2,1)}, bf16[256,768]{1,0:T(8,128)(2,1)}, u32[]{:S(2)}, u32[]{:S(2)}) collective-permute-start(bf16[256,768]{1,0:T(8,128)(2,1)} %get-tuple-element.145), channel_id=1, source_target_pairs={{0,8},{2,10},{4,12},{6,14},{8,0},{10,2},{12,4},{14,6},{16,24},{18,... | collective-permute-start | bytes 1179656 | tf_op jit(solution)/shard_map/ppermute | solution.py:959
  437.2 51.0 %collective-permute-start.25 = (bf16[256,768]{1,0:T(8,128)(2,1)}, bf16[256,768]{1,0:T(8,128)(2,1)S(1)}, u32[]{:S(2)}, u32[]{:S(2)}) collective-permute-start(bf16[256,768]{1,0:T(8,128)(2,1)} %get-tuple-element.147), channel_id=1, source_target_pairs={{0,1},{1,0},{2,3},{3,2},{4,5},{5,4},{6,7},{7,6},{8,9},{9,8},{10,11... | collective-permute-start | bytes 1179656 | tf_op jit(solution)/shard_map/ppermute | solution.py:959
  438.6 50.9 %collective-permute-start.15 = (bf16[256,768]{1,0:T(8,128)(2,1)}, bf16[256,768]{1,0:T(8,128)(2,1)S(1)}, u32[]{:S(2)}, u32[]{:S(2)}) collective-permute-start(bf16[256,768]{1,0:T(8,128)(2,1)} %get-tuple-element.149), channel_id=1, source_target_pairs={{0,4},{2,6},{4,0},{6,2},{8,12},{10,14},{12,8},{14,10},{16,20},{18,... | collective-permute-start | bytes 1179656 | tf_op jit(solution)/shard_map/ppermute | solution.py:959
  447.9 77.9 %collective-permute-start.6 = (bf16[2,256,768]{2,1,0:T(8,128)(2,1)}, bf16[2,256,768]{2,1,0:T(8,128)(2,1)}, u32[]{:S(2)}, u32[]{:S(2)}) collective-permute-start(bf16[2,256,768]{2,1,0:T(8,128)(2,1)} %get-tuple-element.150), channel_id=1, source_target_pairs={{0,1},{1,0},{2,3},{3,2},{4,5},{5,4},{6,7},{7,6},{8,9},{9,8},{10,11... | collective-permute-start | bytes 2359304 | tf_op jit(solution)/shard_map/ppermute | solution.py:952
  485.6 45.3 %collective-permute-start.49 = (f32[13,768]{1,0:T(8,128)S(1)}, f32[13,768]{1,0:T(8,128)S(1)}, u32[]{:S(2)}, u32[]{:S(2)}) collective-permute-start(f32[13,768]{1,0:T(8,128)S(1)} %add.541), channel_id=1, source_target_pairs={{0,16},{2,18},{4,20},{6,22},{8,24},{10,26},{12,28},{14,30},{16,0},... | collective-permute-start | bytes 119816 | tf_op jit(solution)/shard_map/ppermute | solution.py:959
  495.5 114.4 %collective-permute-start.64 = (bf16[768,768]{1,0:T(8,128)(2,1)}, bf16[768,768]{1,0:T(8,128)(2,1)}, u32[]{:S(2)}, u32[]{:S(2)}) collective-permute-start(bf16[768,768]{1,0:T(8,128)(2,1)} %merge.29.near_own), channel_id=1, source_target_pairs={{0,2},{2,0},{4,6},{6,4},{8,10},{10,8},{12,14},{14,12},{16,18},{18,... | collective-permute-start | bytes 3538952 | tf_op jit(solution)/shard_map/ppermute | solution.py:959
  495.6 114.3 %collective-permute-start.65 = (bf16[768,768]{1,0:T(8,128)(2,1)}, bf16[768,768]{1,0:T(8,128)(2,1)}, u32[]{:S(2)}, u32[]{:S(2)}) collective-permute-start(bf16[768,768]{1,0:T(8,128)(2,1)} %collective-permute-done.63.far_own), channel_id=1, source_target_pairs={{0,2},{2,0},{4,6},{6,4},{8,10},{10,8},{12,14},{14,12},{16,18},{18,... | collective-permute-start | bytes 3538952 | tf_op jit(solution)/shard_map/ppermute | solution.py:959
  525.8 85.4 %collective-permute-start.56 = (bf16[768,768]{1,0:T(8,128)(2,1)}, bf16[768,768]{1,0:T(8,128)(2,1)}, u32[]{:S(2)}, u32[]{:S(2)}) collective-permute-start(bf16[768,768]{1,0:T(8,128)(2,1)} %merge.26.near_own), channel_id=1, source_target_pairs={{0,1},{1,0},{2,3},{3,2},{4,5},{5,4},{6,7},{7,6},{8,9},{9,8},{10,11... | collective-permute-start | bytes 3538952 | tf_op jit(solution)/shard_map/ppermute | solution.py:959
  535.5 6.6 collective-permute-start.19
  537.1 72.5 %collective-permute-start.11 = (bf16[2,256,768]{2,1,0:T(8,128)(2,1)}, bf16[2,256,768]{2,1,0:T(8,128)(2,1)}, u32[]{:S(2)}, u32[]{:S(2)}) collective-permute-start(bf16[2,256,768]{2,1,0:T(8,128)(2,1)} %fusion.2), channel_id=1, source_target_pairs={{0,1},{1,0},{2,3},{3,2},{4,5},{5,4},{6,7},{7,6},{8,9},{9,8},{10,11... | collective-permute-start | bytes 2359304 | tf_op jit(solution)/shard_map/ppermute | solution.py:952
  554.0 11.2 %collective-permute-start.20 = (bf16[64,768]{1,0:T(8,128)(2,1)}, bf16[64,768]{1,0:T(8,128)(2,1)}, u32[]{:S(2)}, u32[]{:S(2)}) collective-permute-start(bf16[64,768]{1,0:T(8,128)(2,1)} %merge.15.own_ref), channel_id=1, source_target_pairs={{0,1},{1,0},{2,3},{3,2},{4,5},{5,4},{6,7},{7,6},{8,9},{9,8},{10,11... | collective-permute-start | bytes 294920 | tf_op jit(solution)/shard_map/ppermute | solution.py:959
  565.2 8.0 %collective-permute-start.41 = (bf16[128,768]{1,0:T(8,128)(2,1)}, bf16[128,768]{1,0:T(8,128)(2,1)S(1)}, u32[]{:S(2)}, u32[]{:S(2)}) collective-permute-start(bf16[128,768]{1,0:T(8,128)(2,1)} %merge.22.own_ref), channel_id=1, source_target_pairs={{0,1},{1,0},{2,3},{3,2},{4,5},{5,4},{6,7},{7,6},{8,9},{9,8},{10,11... | collective-permute-start | bytes 589832 | tf_op jit(solution)/shard_map/ppermute | solution.py:959
  573.2 8.4 %collective-permute-start.31 = (bf16[128,768]{1,0:T(8,128)(2,1)}, bf16[128,768]{1,0:T(8,128)(2,1)S(1)}, u32[]{:S(2)}, u32[]{:S(2)}) collective-permute-start(bf16[128,768]{1,0:T(8,128)(2,1)} %merge.19.own_ref), channel_id=1, source_target_pairs={{0,4},{2,6},{4,0},{6,2},{8,12},{10,14},{12,8},{14,10},{16,20},{18,... | collective-permute-start | bytes 589832 | tf_op jit(solution)/shard_map/ppermute | solution.py:959
  581.7 29.7 %collective-permute-start.21 = (bf16[128,768]{1,0:T(8,128)(2,1)}, bf16[128,768]{1,0:T(8,128)(2,1)}, u32[]{:S(2)}, u32[]{:S(2)}) collective-permute-start(bf16[128,768]{1,0:T(8,128)(2,1)} %merge.16.own_ref), channel_id=1, source_target_pairs={{0,8},{2,10},{4,12},{6,14},{8,0},{10,2},{12,4},{14,6},{16,24},{18,... | collective-permute-start | bytes 589832 | tf_op jit(solution)/shard_map/ppermute | solution.py:959
  609.6 16.4 %collective-permute-start.42 = (bf16[256,768]{1,0:T(8,128)(2,1)}, bf16[256,768]{1,0:T(8,128)(2,1)S(1)}, u32[]{:S(2)}, u32[]{:S(2)}) collective-permute-start(bf16[256,768]{1,0:T(8,128)(2,1)} %merge.23.refs_8_), channel_id=1, source_target_pairs={{0,8},{2,10},{4,12},{6,14},{8,0},{10,2},{12,4},{14,6},{16,24},{18,... | collective-permute-start | bytes 1179656 | tf_op jit(solution)/shard_map/ppermute | solution.py:959
  609.9 16.3 %collective-permute-start.43 = (bf16[256,768]{1,0:T(8,128)(2,1)}, bf16[256,768]{1,0:T(8,128)(2,1)}, u32[]{:S(2)}, u32[]{:S(2)}) collective-permute-start(bf16[256,768]{1,0:T(8,128)(2,1)} %merge.23.refs_8_), channel_id=1, source_target_pairs={{0,2},{2,0},{4,6},{6,4},{8,10},{10,8},{12,14},{14,12},{16,18},{18,... | collective-permute-start | bytes 1179656 | tf_op jit(solution)/shard_map/ppermute | solution.py:959
  609.9 17.0 %collective-permute-start.32 = (bf16[256,768]{1,0:T(8,128)(2,1)}, bf16[256,768]{1,0:T(8,128)(2,1)}, u32[]{:S(2)}, u32[]{:S(2)}) collective-permute-start(bf16[256,768]{1,0:T(8,128)(2,1)} %merge.20.refs_4_), channel_id=1, source_target_pairs={{0,1},{1,0},{2,3},{3,2},{4,5},{5,4},{6,7},{7,6},{8,9},{9,8},{10,11... | collective-permute-start | bytes 1179656 | tf_op jit(solution)/shard_map/ppermute | solution.py:959
  611.2 47.6 %collective-permute-start.57 = (bf16[768,768]{1,0:T(8,128)(2,1)}, bf16[768,768]{1,0:T(8,128)(2,1)}, u32[]{:S(2)}, u32[]{:S(2)}) collective-permute-start(bf16[768,768]{1,0:T(8,128)(2,1)} %merge.26.near_own), channel_id=1, source_target_pairs={{0,2},{2,0},{4,6},{6,4},{8,10},{10,8},{12,14},{14,12},{16,18},{18,... | collective-permute-start | bytes 3538952 | tf_op jit(solution)/shard_map/ppermute | solution.py:959
  611.3 47.4 %collective-permute-start.58 = (bf16[768,768]{1,0:T(8,128)(2,1)}, bf16[768,768]{1,0:T(8,128)(2,1)}, u32[]{:S(2)}, u32[]{:S(2)}) collective-permute-start(bf16[768,768]{1,0:T(8,128)(2,1)} %collective-permute-done.56.far_own), channel_id=1, source_target_pairs={{0,2},{2,0},{4,6},{6,4},{8,10},{10,8},{12,14},{14,12},{16,18},{18,... | collective-permute-start | bytes 3538952 | tf_op jit(solution)/shard_map/ppermute | solution.py:959
  626.0 7.6 %collective-permute-start.33 = (bf16[256,768]{1,0:T(8,128)(2,1)}, bf16[256,768]{1,0:T(8,128)(2,1)}, u32[]{:S(2)}, u32[]{:S(2)}) collective-permute-start(bf16[256,768]{1,0:T(8,128)(2,1)} %merge.20.refs_4_), channel_id=1, source_target_pairs={{0,2},{2,0},{4,6},{6,4},{8,10},{10,8},{12,14},{14,12},{16,18},{18,... | collective-permute-start | bytes 1179656 | tf_op jit(solution)/shard_map/ppermute | solution.py:959
  626.2 11.7 %collective-permute-start.22 = (bf16[256,768]{1,0:T(8,128)(2,1)}, bf16[256,768]{1,0:T(8,128)(2,1)}, u32[]{:S(2)}, u32[]{:S(2)}) collective-permute-start(bf16[256,768]{1,0:T(8,128)(2,1)} %merge.17.refs_0_), channel_id=1, source_target_pairs={{0,4},{2,6},{4,0},{6,2},{8,12},{10,14},{12,8},{14,10},{16,20},{18,... | collective-permute-start | bytes 1179656 | tf_op jit(solution)/shard_map/ppermute | solution.py:959
  627.0 11.0 %collective-permute-start.23 = (bf16[256,768]{1,0:T(8,128)(2,1)}, bf16[256,768]{1,0:T(8,128)(2,1)}, u32[]{:S(2)}, u32[]{:S(2)}) collective-permute-start(bf16[256,768]{1,0:T(8,128)(2,1)} %merge.17.refs_0_), channel_id=1, source_target_pairs={{0,2},{2,0},{4,6},{6,4},{8,10},{10,8},{12,14},{14,12},{16,18},{18,... | collective-permute-start | bytes 1179656 | tf_op jit(solution)/shard_map/ppermute | solution.py:959
  633.6 15.9 %collective-permute-start.44 = (bf16[256,768]{1,0:T(8,128)(2,1)S(1)}, bf16[256,768]{1,0:T(8,128)(2,1)S(1)}, u32[]{:S(2)}, u32[]{:S(2)}) collective-permute-start(bf16[256,768]{1,0:T(8,128)(2,1)S(1)} %collective-permute-done.42.refs_9_), channel_id=1, source_target_pairs={{0,2},{2,0},{4,6},{6,4},{8,10},{10,8},{12,14},{14,12},{16,18},{18,... | collective-permute-start | bytes 1179656 | tf_op jit(solution)/shard_map/ppermute | solution.py:959
  637.9 11.6 %collective-permute-start.34 = (bf16[256,768]{1,0:T(8,128)(2,1)}, bf16[256,768]{1,0:T(8,128)(2,1)S(1)}, u32[]{:S(2)}, u32[]{:S(2)}) collective-permute-start(bf16[256,768]{1,0:T(8,128)(2,1)} %collective-permute-done.32.refs_5_), channel_id=1, source_target_pairs={{0,2},{2,0},{4,6},{6,4},{8,10},{10,8},{12,14},{14,12},{16,18},{18,... | collective-permute-start | bytes 1179656 | tf_op jit(solution)/shard_map/ppermute | solution.py:959
  637.9 11.6 %collective-permute-start.24 = (bf16[256,768]{1,0:T(8,128)(2,1)}, bf16[256,768]{1,0:T(8,128)(2,1)S(1)}, u32[]{:S(2)}, u32[]{:S(2)}) collective-permute-start(bf16[256,768]{1,0:T(8,128)(2,1)} %collective-permute-done.22.refs_1_), channel_id=1, source_target_pairs={{0,2},{2,0},{4,6},{6,4},{8,10},{10,8},{12,14},{14,12},{16,18},{18,... | collective-permute-start | bytes 1179656 | tf_op jit(solution)/shard_map/ppermute | solution.py:959
  (74 other events, 987.6 us)
